TPU v7x, 32 devices: a whole 2x2x4 slice. The times are simulated.
32 devices in a mesh: days: 2 (over y), sta: 8 (over z, x), win: 2 (over core).
Axes of the slice: x: 2, y: 2, z: 4, core: 2. Of those that a mesh axis runs over, the one named last changes fastest.
Arguments:
- phases: bfloat16 [48, 2048, 16], P(('days', 'win'), 'sta'), parts along dimension 0, may hold values from -3.140625 to 3.140625
- window_valid: int32 [48], P('days'), parts along dimension 0, may hold values 0 or 1
- freq_taper: float32 [2048], replicated, may hold values from 0.1 to 1.9
- pair_mask: int32 [8, 8], replicated, may hold values from 0 to 1, as said below
Outputs:
- correlations: float32 [32, 16, 512], P(('days', 'sta'), None, 'win'), parts along dimension 0
There are 2 independent parts, one for each index of `days`. A program takes and returns all parts, laid end to end along the dimension named above; an argument that names none is the same for every part. Nothing has to cross between parts.
Inputs may be any that keep to these rules, and one draw needn't show every extreme that they name: `pair_mask`: symmetric over the two block indices; every diagonal block is kept.
All inputs are finite; a program needn't handle non-finite values.
Results may differ from a plain program's by a relative error of at most 0.005.
Values may be sent and summed in bfloat16 or wider, within the bound.
No kernel may reach another device: no remote copies, remote signals or barrier semaphores. Data moves between devices by JAX's collectives and lax.ppermute only.
A program may use at most 64 MiB of HBM per device.

v0:
```python
import math

import jax
import jax.numpy as jnp
from jax import lax
from jax.sharding import PartitionSpec as P

LAGS = 512


def lag_table(freq_bins, lag_count):
    freq_index = jnp.arange(freq_bins, dtype=jnp.int32)[:, None]
    lag_index = jnp.arange(lag_count, dtype=jnp.int32)[None, :] - lag_count // 2
    wrapped = jnp.mod(freq_index * lag_index, 2 * freq_bins)
    angle = wrapped.astype(jnp.float32) * (math.pi / freq_bins)
    return jnp.stack((jnp.cos(angle), -jnp.sin(angle))).astype(jnp.bfloat16)


def per_device(phases, window_valid, freq_taper, pair_mask):
    sta_count = lax.axis_size("sta")
    win_rows, band_bins, stations = phases.shape
    freq_bins = band_bins * sta_count
    recv_rows = stations // sta_count
    sta_index = lax.axis_index("sta")
    win_group = lax.axis_index("win")
    valid_count = jnp.sum(window_valid.astype(jnp.float32))
    norm_scale = 1.0 / jnp.sqrt(freq_bins * jnp.maximum(valid_count, 1.0))
    bin_weight = freq_taper * norm_scale
    group_valid = lax.dynamic_slice_in_dim(window_valid, win_group * win_rows, win_rows)
    group_weight = group_valid.astype(jnp.bfloat16)[:, None, None]
    own_f = phases.astype(jnp.float32)
    own_cos = jnp.cos(own_f).astype(jnp.bfloat16)
    own_sin = jnp.sin(own_f).astype(jnp.bfloat16)
    left_cos = own_cos * group_weight
    left_sin = own_sin * group_weight
    band_weight = lax.dynamic_slice_in_dim(bin_weight, sta_index * band_bins, band_bins)
    pair_re = jnp.einsum("wki,wkj->ijk", left_cos, own_cos, preferred_element_type=jnp.float32)
    pair_re = pair_re + jnp.einsum(
        "wki,wkj->ijk", left_sin, own_sin, preferred_element_type=jnp.float32
    )
    band_re = (pair_re * band_weight).astype(jnp.bfloat16)
    pair_im = jnp.einsum("wki,wkj->ijk", left_sin, own_cos, preferred_element_type=jnp.float32)
    pair_im = pair_im - jnp.einsum(
        "wki,wkj->ijk", left_cos, own_sin, preferred_element_type=jnp.float32
    )
    band_im = (pair_im * band_weight).astype(jnp.bfloat16)
    spectra = lax.all_to_all(
        jnp.stack((band_re, band_im)), "sta", split_axis=1, concat_axis=3, tiled=True
    )
    lag_count = LAGS
    transform = lag_table(freq_bins, lag_count)
    flat_spectra = spectra.reshape(2, recv_rows * stations, freq_bins)
    correlation = jnp.einsum(
        "cnk,ckt->nt", flat_spectra, transform, preferred_element_type=jnp.float32
    )
    block_row = lax.dynamic_index_in_dim(pair_mask, sta_index, 0, keepdims=False)
    station_row = jnp.repeat(block_row, recv_rows).astype(jnp.float32)
    receiver = sta_index * recv_rows + jnp.arange(recv_rows, dtype=jnp.int32)
    distinct = (receiver[:, None] != jnp.arange(stations, dtype=jnp.int32)[None, :]).astype(
        jnp.float32
    )
    pair_keep = station_row[None, :] * distinct
    correlation = correlation.reshape(recv_rows, stations, lag_count) * pair_keep[:, :, None]
    return lax.psum_scatter(correlation, "win", scatter_dimension=2, tiled=True)


def solution(mesh):
    return jax.shard_map(
        per_device,
        mesh=mesh,
        in_specs=(P(("days", "win"), "sta", None), P("days"), P(), P()),
        out_specs=P(("days", "sta"), None, "win"),
        check_vma=False,
    )
```

profile of v0, /device:TPU:0, one launch (start us, length us, event | category | flops | bytes accessed | tf_op | source)
XLA Modules:
  0.0 74.8 jit_solution(9505695054169387936)
XLA Ops:
  6.5 1.3 %convert_reduce_fusion = f32[]{:T(128)} fusion(s32[24]{0:T(128)} %param.5), kind=kLoop, calls=%fused_computation.32 | loop fusion | flops 47 | bytes 100 | tf_op jit(solution)/shard_map/reduce_sum | solution.py:26
  8.5 0.7 dynamic-slice_convert_fusion
  9.2 1.6 %fusion.12 = (bf16[12,256,16]{1,2,0:T(8,128)(2,1)S(1)}, bf16[12,256,16]{1,2,0:T(8,128)(2,1)S(1)}) fusion(bf16[12,256,16]{1,2,0:T(8,128)(2,1)} %param.4), kind=kLoop, calls=%fused_computation.24 | loop fusion | flops 147456 | bytes 294912 | tf_op jit(solution)/shard_map/convert_element_type | solution.py:33
  10.8 1.6 %broadcast_multiply_fusion.1 = (bf16[12,256,16]{1,2,0:T(8,128)(2,1)S(1)}, bf16[12,256,16]{1,2,0:T(8,128)(2,1)S(1)}) fusion(bf16[12]{0:T(256)(128)(2,1)S(1)} %dynamic-slice_convert_fusion, bf16[12,256,16]{1,2,0:T(8,128)(2,1)} %param.4), kind=kLoop, calls=%fused_computation.26 | loop fusion | flops 491520 | bytes 294936 | tf_op jit(solution)/shard_map/mul | solution.py:34
  12.4 1.0 %copy.35 = bf16[12,256,16]{0,2,1:T(8,128)(2,1)S(1)} copy(bf16[12,256,16]{1,2,0:T(8,128)(2,1)S(1)} %get-tuple-element.5) | data formatting | bytes 196608 | tf_op jit(solution)/shard_map/mul | solution.py:34
  13.5 1.9 %copy.36 = bf16[12,256,16]{2,0,1:T(8,128)(2,1)} copy(bf16[12,256,16]{1,2,0:T(8,128)(2,1)S(1)} %get-tuple-element.8) | data formatting | bytes 196608 | tf_op jit(solution)/shard_map/convert_element_type | solution.py:32
  15.4 1.0 %copy.37 = bf16[12,256,16]{0,2,1:T(8,128)(2,1)S(1)} copy(bf16[12,256,16]{1,2,0:T(8,128)(2,1)S(1)} %get-tuple-element.6) | data formatting | bytes 196608 | tf_op jit(solution)/shard_map/mul | solution.py:35
  16.4 0.9 %copy.38 = bf16[12,256,16]{2,0,1:T(8,128)(2,1)S(1)} copy(bf16[12,256,16]{1,2,0:T(8,128)(2,1)S(1)} %get-tuple-element.7) | data formatting | bytes 196608 | tf_op jit(solution)/shard_map/convert_element_type | solution.py:33
  17.4 3.3 %fusion.14 = f32[256,16,16]{2,1,0:T(8,128)} fusion(bf16[12,256,16]{0,2,1:T(8,128)(2,1)S(1)} %copy.35, bf16[12,256,16]{2,0,1:T(8,128)(2,1)} %copy.36), kind=kOutput, calls=%fused_computation.35 | convolution fusion | flops 1572864 | bytes 458752 | tf_op jit(solution)/shard_map/wki,wkj->ijk/dot_general | solution.py:37
  20.7 2.0 %fusion.15 = f32[256,16,16]{2,1,0:T(8,128)} fusion(bf16[12,256,16]{0,2,1:T(8,128)(2,1)S(1)} %copy.37, bf16[12,256,16]{2,0,1:T(8,128)(2,1)S(1)} %copy-done), kind=kOutput, calls=%fused_computation.36 | convolution fusion | flops 1572864 | bytes 458752 | tf_op jit(solution)/shard_map/wki,wkj->ijk/dot_general | solution.py:42
  22.7 0.8 %dynamic-slice_multiply_fusion = f32[256]{0:T(256)S(1)} fusion(f32[2048]{0:T(1024)} %param.6, s32[]{:T(128)S(6)} %select_n.31, f32[]{:T(128)S(6)} %sqrt.3), kind=kLoop, calls=%fused_computation.29 | loop fusion | flops 256 | bytes 2056 | tf_op jit(solution)/shard_map/mul | solution.py:28
  23.4 2.4 %fusion.7 = bf16[1,16,16,256]{2,1,3,0:T(8,128)(2,1)S(1)} fusion(f32[256,16,16]{2,1,0:T(8,128)} %fusion.14, bf16[12,256,16]{0,2,1:T(8,128)(2,1)S(1)} %copy.37, bf16[12,256,16]{2,0,1:T(8,128)(2,1)S(1)} %copy.38, f32[256]{0:T(256)S(1)} %dynamic-slice_multiply_fusion), kind=kOutput, calls=%fused_computation.16 | convolution fusion | flops 1769472 | bytes 590848 | tf_op jit(solution)/shard_map/wki,wkj->ijk/dot_general | solution.py:38
  25.9 0.7 fusion.8
  26.6 0.5 pad_maximum_fusion
  27.0 2.3 %copy.43 = bf16[2,16,16,256]{3,2,0,1:T(8,128)(2,1)} copy(bf16[2,16,16,256]{2,1,3,0:T(8,128)(2,1)S(1)} %pad_maximum_fusion) | data formatting | bytes 524288 | tf_op jit(solution)/shard_map/stack | solution.py:48
  29.3 7.2 %all-to-all-start = ((bf16[2,16,16,256]{3,2,0,1:T(8,128)(2,1)}), bf16[2,16,16,256]{3,2,0,1:T(8,128)(2,1)S(1)}, u32[]{:S(2)}, u32[]{:S(2)}) async-start(bf16[2,16,16,256]{3,2,0,1:T(8,128)(2,1)} %copy.43), calls=%async_computation | async-start | bytes 524288 | tf_op jit(solution)/shard_map/all_to_all | solution.py:47
  36.6 0.7 convert_bitcast_fusion
  37.4 0.1 convert_element_type.71
  37.5 0.1 compare_select_fusion
  37.5 18.1 %cosine_convert_fusion = (bf16[1,2048,512]{2,1,0:T(8,128)(2,1)S(1)}, bf16[1,2048,512]{2,1,0:T(8,128)(2,1)}) fusion(s32[512]{0:T(512)S(1)} %iota_add_fusion), kind=kLoop, calls=%fused_computation.8 | loop fusion | flops 17825792 | bytes 4196352 | tf_op jit(solution)/shard_map/convert
  55.7 0.1 copy.47
  55.8 0.1 reshape.160
  56.0 2.9 %fusion.10 = f32[2,16,512]{2,1,0:T(8,128)} fusion(bf16[2,16,2,2048]{3,1,0,2:T(8,128)(2,1)S(1)} %bitcast.43, bf16[1,2048,512]{2,1,0:T(8,128)(2,1)} %get-tuple-element.10, bf16[1,2048,512]{2,1,0:T(8,128)(2,1)S(1)} %get-tuple-element.9, f32[2,16]{1,0:T(2,128)S(1)} %compare_select_fusion), kind=kOutput, calls=%fused_computation.19 | convolution fusion | flops 136331264 | bytes 4522112 | tf_op jit(solution)/shard_map/cnk,ckt->nt/dot_general | solution.py:53
  58.9 9.0 %reduce-scatter.2.cloned.1.call-done = f32[2,16,256]{2,1,0:T(8,128)} async-done(((f32[2,16,512]{2,1,0:T(8,128)}), f32[2,16,256]{2,1,0:T(8,128)}) %reduce-scatter.2.cloned.1.call-update) | async-done | bytes 32784 | tf_op jit(solution)/shard_map/reduce_scatter | solution.py:64
  (10 shorter events, 0.1 us)
Async XLA Ops:
  17.3 3.3 %copy-start = (bf16[12,256,16]{2,0,1:T(8,128)(2,1)S(1)}, bf16[12,256,16]{2,0,1:T(8,128)(2,1)}, u32[]{:S(2)}) copy-start(bf16[12,256,16]{2,0,1:T(8,128)(2,1)} %copy.36) | copy-start | bytes 294916
  23.4 2.4 %copy-start.1 = (f32[256,16,16]{2,1,0:T(8,128)S(1)}, f32[256,16,16]{2,1,0:T(8,128)}, u32[]{:S(2)}) copy-start(f32[256,16,16]{2,1,0:T(8,128)} %fusion.15) | copy-start | bytes 786436
  29.3 26.4 %all-to-all-start = ((bf16[2,16,16,256]{3,2,0,1:T(8,128)(2,1)}), bf16[2,16,16,256]{3,2,0,1:T(8,128)(2,1)S(1)}, u32[]{:S(2)}, u32[]{:S(2)}) async-start(bf16[2,16,16,256]{3,2,0,1:T(8,128)(2,1)} %copy.43), calls=%async_computation | async-start | bytes 524288 | tf_op jit(solution)/shard_map/all_to_all | solution.py:47
  36.6 31.3 %reduce-scatter.2.cloned.1.call-start = ((), (), s32[]{:S(2)}) async-start(), calls=%async_computation.2 | async-start | bytes 98304 | tf_op jit(solution)/shard_map/reduce_scatter | solution.py:64
Sparse Core Ops, SparseCore 0:
  59.0 8.8 reduce-scatter.1
where the time goes:
time: 75.2 us; the launch traced here: 74.8 us
  other arithmetic  25.3 us (34%)
  between operations  14.2 us (19%)
  matrix products  11.3 us (15%)
  waiting for transfers between devices  9.03 us (12%)
  local copies, waits for them, and re-layouts  7.59 us (10%)
  starting transfers between devices  7.28 us (10%)
    another operation x1, other arithmetic  18.1 us
    reduce_scatter x1, waiting for transfers between devices, per_device(): return lax.psum_scatter(correlation, 'win', scatter_dimension=2, tiled=True)  9.01 us
    all_to_all x1, starting transfers between devices, per_device(): lax.all_to_all(jnp.stack((band_re, band_im)), 'sta', split_axis=1, concat...  7.24 us
    dot_general x1, matrix products, per_device(): jnp.einsum('wki,wkj->ijk', left_cos, own_cos, preferred_element_type=jnp....  3.31 us
    dot_general x1, matrix products, per_device(): jnp.einsum('cnk,ckt->nt', flat_spectra, transform, preferred_element_type...  2.92 us
    dot_general x1, matrix products, per_device(): jnp.einsum('wki,wkj->ijk', left_sin, own_sin, preferred_element_type=jnp....  2.42 us
    another operation x1, local copies, waits for them, and re-layouts, per_device(): jnp.stack((band_re, band_im))  2.28 us
    dot_general x1, matrix products, per_device(): jnp.einsum('wki,wkj->ijk', left_sin, own_cos, preferred_element_type=jnp....  1.98 us
  transfers between devices with their start and end apart: 2, of which 1 were waited for; matrix products, arithmetic and copies ran while one was open for 25% of the time, Pallas kernels for 0%

commit v1 on v0

v1 whole, which is shorter than its diff:
```python
import functools
import math

import jax
import jax.numpy as jnp
from jax import lax
from jax.experimental import pallas as pl
from jax.experimental.pallas import tpu as pltpu
from jax.sharding import PartitionSpec as P

LAGS = 512
VMEM = pl.BlockSpec(memory_space=pltpu.VMEM)
SMEM = pl.BlockSpec(memory_space=pltpu.SMEM)
PARAMS = pltpu.CompilerParams(vmem_limit_bytes=48 * 1024 * 1024)

COS_COEF = (
    0.9999999890590218,
    -0.49999989101070386,
    0.041666489217381156,
    -0.001388780359807859,
    2.476988355752502e-05,
    -2.707903082088142e-07,
    1.724509174527214e-09,
)
SIN_COEF = (
    0.9999997571451633,
    -0.06534424613196173,
    0.001711441007161203,
    -2.461450561671638e-05,
    1.977699154629728e-07,
)


def cos_sin(angle):
    square = angle * angle
    cosine = COS_COEF[-1]
    for coef in COS_COEF[-2::-1]:
        cosine = cosine * square + coef
    sine = SIN_COEF[-1]
    for coef in SIN_COEF[-2::-1]:
        sine = sine * square + coef
    sine = sine * (angle - angle * square * (1.0 / math.pi**2))
    return cosine, sine


def full_distances(blocks):
    half = blocks // 2
    return [(step, step + half) for step in range(1, half)]


def position():
    return lax.axis_index("sta"), lax.axis_index("win")


def cross_kernel(blocks, valid_ref, taper_ref, own_ref, other_ref, *refs):
    cos_ref, sin_ref = refs[-2:]
    own_part, far_part, *full_parts = refs[:-2]
    sta, win = position()
    windows, stations, bins = own_ref.shape
    rows = stations // blocks
    count = jnp.float32(0)
    for w in range(2 * windows):
        count += valid_ref[w].astype(jnp.float32)
    if bins % 128:
        taper = taper_ref[...]
    else:
        taper = taper_ref[:, pl.ds(pl.multiple_of(sta * bins, 128), bins)]
    total = jnp.maximum(jnp.full((1, bins), count, jnp.float32), 1.0)
    weight = taper * (1.0 / jnp.sqrt(blocks * bins * total))
    for group, phase_ref in enumerate((own_ref, other_ref)):
        first = (win if group == 0 else 1 - win) * windows

        def phasors(w, carry, group=group, phase_ref=phase_ref, first=first):
            cosine, sine = cos_sin(phase_ref[w].astype(jnp.float32))
            usable = valid_ref[first + w].astype(jnp.float32)
            cos_ref[group * windows + w] = cosine.astype(jnp.bfloat16).astype(jnp.float32) * usable
            sin_ref[group * windows + w] = sine.astype(jnp.bfloat16).astype(jnp.float32) * usable
            return carry

        lax.fori_loop(0, windows, phasors, 0, unroll=4)
    is_first = win == 0

    def row_of(ref, w, row):
        return ref[w, pl.ds(row, 1), :]

    def whole(out_ref, block):
        for r in range(rows):
            row = block * rows + r

            def add(w, sums, row=row):
                real, imag = sums
                row_cos, row_sin = row_of(cos_ref, w, row), row_of(sin_ref, w, row)
                cosine, sine = cos_ref[w], sin_ref[w]
                real = real + (row_cos * cosine + row_sin * sine)
                imag = imag + (row_sin * cosine - row_cos * sine)
                return real, imag

            zero = jnp.zeros((stations, bins), jnp.float32)
            real, imag = lax.fori_loop(0, 2 * windows, add, (zero, zero), unroll=8)
            out_ref[0, r] = (real * weight).astype(jnp.bfloat16)
            out_ref[1, r] = (imag * weight).astype(jnp.bfloat16)

    def part(out_ref, block):
        for r in range(rows):
            row = block * rows + r

            def add(w, total, row=row):
                row_cos, row_sin = row_of(cos_ref, w, row), row_of(sin_ref, w, row)
                left = jnp.where(is_first, row_cos, row_sin)
                right = jnp.where(is_first, row_sin, -row_cos)
                return total + (left * cos_ref[w] + right * sin_ref[w])

            zero = jnp.zeros((stations, bins), jnp.float32)
            total = lax.fori_loop(0, 2 * windows, add, zero, unroll=8)
            out_ref[r] = (total * weight).astype(jnp.bfloat16)

    for out_ref, pair in zip(full_parts, full_distances(blocks)):
        whole(out_ref, sta ^ jnp.where(is_first, pair[0], pair[1]))
    part(far_part, sta ^ (blocks // 2))
    part(own_part, sta)


def table_kernel(blocks, bins, part_ref, full_ref, row_cos, row_sin):
    sta, win = position()
    wrap = 2 * blocks * bins
    columns = part_ref.shape[-1]
    half = columns // 2
    step = 16
    column = lax.broadcasted_iota(jnp.int32, (step, columns), 1)
    mine_low = win == 0
    lag = jnp.where(mine_low, column - half, jnp.where(column < half, column, column - columns))

    def phasor(index):
        wrapped = ((index + wrap // 2) & (wrap - 1)) - wrap // 2
        return cos_sin(wrapped.astype(jnp.float32) * (2.0 * math.pi / wrap))

    fine = lax.broadcasted_iota(jnp.int32, (step, columns), 0)
    fine_cos, fine_sin = phasor(fine * lag)
    steps = bins // step
    full = full_distances(blocks)

    def band_rows(block, store):
        for start in range(0, steps, 16):
            count = min(16, steps - start)
            coarse = block * bins + (start + fine) * step
            coarse_cos, coarse_sin = phasor(coarse * lag)
            row_cos[...] = coarse_cos
            row_sin[...] = coarse_sin

            def fill(a, carry, start=start):
                left_cos = row_cos[pl.ds(a, 1), :]
                left_sin = row_sin[pl.ds(a, 1), :]
                cosine = left_cos * fine_cos - left_sin * fine_sin
                sine = left_sin * fine_cos + left_cos * fine_sin
                store(pl.ds(pl.multiple_of((start + a) * step, step), step), cosine, -sine)
                return carry

            lax.fori_loop(0, count, fill, 0, unroll=2)

    for slot, pair in enumerate(full):

        def store_full(place, cosine, sine, slot=slot):
            full_ref[slot, 0, place, :] = cosine.astype(jnp.bfloat16)
            full_ref[slot, 1, place, :] = sine.astype(jnp.bfloat16)

        band_rows(sta ^ jnp.where(mine_low, pair[0], pair[1]), store_full)
    for slot, distance in enumerate((0, blocks // 2)):

        def store_part(place, cosine, sine, slot=slot):
            part_ref[slot, place, :] = jnp.where(mine_low, cosine, sine).astype(jnp.bfloat16)

        band_rows(sta ^ distance, store_part)


def lag_kernel(blocks, mask_ref, part_ref, full_ref, own_ref, far_ref, *refs):
    mine_ref, theirs_ref = refs[-2:]
    sta, _ = position()
    rows, stations, bins = own_ref.shape
    pairs = rows * stations
    half = mine_ref.shape[-1]

    def times(spectra, table):
        return jnp.dot(spectra.reshape(pairs, bins), table, preferred_element_type=jnp.float32)

    total = times(own_ref[...], part_ref[0]) + times(far_ref[...], part_ref[1])
    for slot, spectra_ref in enumerate(refs[:-2]):
        for c in range(2):
            total = total + times(spectra_ref[c], full_ref[slot, c])
    source = lax.broadcasted_iota(jnp.int32, (stations, half), 0)
    kept = jnp.zeros((stations, half), jnp.float32)
    for block in range(blocks):
        kept = jnp.where(source // rows == block, mask_ref[sta, block].astype(jnp.float32), kept)
    for r in range(rows):
        keep = jnp.where(source == sta * rows + r, 0.0, kept)
        mine_ref[r] = total[r * stations : (r + 1) * stations, :half] * keep
        theirs_ref[r] = total[r * stations : (r + 1) * stations, half:] * keep


def per_device(phases, window_valid, freq_taper, pair_mask):
    blocks = lax.axis_size("sta")
    windows, bins, stations = phases.shape
    rows = stations // blocks
    full = full_distances(blocks)
    swap = [(0, 1), (1, 0)]
    own = jnp.transpose(phases, (0, 2, 1))
    other = lax.ppermute(own, "win", swap)
    if bins % 128:
        taper = lax.dynamic_slice_in_dim(freq_taper, lax.axis_index("sta") * bins, bins)
    else:
        taper = freq_taper
    part_shape = jax.ShapeDtypeStruct((rows, stations, bins), jnp.bfloat16)
    full_shape = jax.ShapeDtypeStruct((2, rows, stations, bins), jnp.bfloat16)
    part_table, full_table = pl.pallas_call(
        functools.partial(table_kernel, blocks, bins),
        out_shape=(
            jax.ShapeDtypeStruct((2, bins, LAGS), jnp.bfloat16),
            jax.ShapeDtypeStruct((len(full), 2, bins, LAGS), jnp.bfloat16),
        ),
        out_specs=(VMEM, VMEM),
        scratch_shapes=[pltpu.VMEM((16, LAGS), jnp.float32)] * 2,
        compiler_params=PARAMS,
        name="lag_table",
    )()
    own_part, far_part, *full_parts = pl.pallas_call(
        functools.partial(cross_kernel, blocks),
        out_shape=[part_shape, part_shape] + [full_shape] * len(full),
        in_specs=[SMEM, VMEM, VMEM, VMEM],
        out_specs=[VMEM] * (2 + len(full)),
        scratch_shapes=[pltpu.VMEM((2 * windows, stations, bins), jnp.float32)] * 2,
        compiler_params=PARAMS,
        name="cross_spectra",
    )(window_valid, taper.reshape(1, -1), own, other)
    axes = ("sta", "win")
    both = [(2 * b + w, 2 * (b ^ (blocks // 2)) + w) for b in range(blocks) for w in range(2)]
    far_part = lax.ppermute(far_part, axes, both)
    arrived = []
    for spectra, pair in zip(full_parts, full):
        moves = [(2 * b + w, 2 * (b ^ pair[w]) + w) for b in range(blocks) for w in range(2)]
        arrived.append(lax.ppermute(spectra, axes, moves))
    half_shape = jax.ShapeDtypeStruct((rows, stations, LAGS // 2), jnp.float32)
    mine, theirs = pl.pallas_call(
        functools.partial(lag_kernel, blocks),
        out_shape=(half_shape, half_shape),
        in_specs=[SMEM] + [VMEM] * (4 + len(full)),
        out_specs=(VMEM, VMEM),
        compiler_params=PARAMS,
        name="lag_sums",
    )(pair_mask, part_table, full_table, own_part, far_part, *arrived)
    return mine + lax.ppermute(theirs, "win", swap)


def solution(mesh):
    return jax.shard_map(
        per_device,
        mesh=mesh,
        in_specs=(P(("days", "win"), "sta", None), P("days"), P(), P()),
        out_specs=P(("days", "sta"), None, "win"),
        check_vma=False,
    )
```

time: 75.2 us -> 21.2 us (0.28)
  other arithmetic: 25.3 us -> 0.62 us
  between operations: 14.2 us -> 0.03 us
  matrix products: 11.3 us -> 0 us
  waiting for transfers between devices: 9.03 us -> 2.79 us
  local copies, waits for them, and re-layouts: 7.59 us -> 2.93 us
  Pallas kernels: 0 us -> 4.51 us
  starting transfers between devices: 7.28 us -> 10.1 us
    another operation x2 -> x0, other arithmetic: 18.6 us -> none
    dot_general x5 -> x0, matrix products: 11.3 us -> none  [the longest x1 3.31 us: per_device(): jnp.einsum('wki,wkj->ijk', left_cos, own_cos, preferred_element_type=jnp....]
    ppermute x0 -> x6, starting transfers between devices: none -> 10.1 us  [the longest x3 4.49 us: per_device(): arrived.append(lax.ppermute(spectra, axes, moves))]
    reduce_scatter x1 -> x0, waiting for transfers between devices: 9.01 us -> none  [per_device(): return lax.psum_scatter(correlation, 'win', scatter_dimension=2, tiled=True)]
    all_to_all x1 -> x0, starting transfers between devices: 7.24 us -> none  [per_device(): lax.all_to_all(jnp.stack((band_re, band_im)), 'sta', split_axis=1, concat...]
    pallas_call x0 -> x3, Pallas kernels: none -> 4.51 us  [the longest x1 2.16 us: per_device(): pl.pallas_call(functools.partial(cross_kernel, blocks), out_shape=[part_s...]
    convert_element_type x3 -> x0, other arithmetic: 3.02 us -> none  [the longest x1 1.59 us: per_device(): own_sin = jnp.sin(own_f).astype(jnp.bfloat16)]
    unnamed x4 -> x8, local copies, waits for them, and re-layouts: 0.01 us -> 2.93 us
  transfers between devices with their start and end apart: 2 -> 6, of which waited for: 1 -> 4; matrix products, arithmetic and copies ran while one was open for 25% -> 0% of each run, Pallas kernels for 0% -> 6%
where the time goes in v1:
time: 21.2 us; the launch traced here: 21 us
  starting transfers between devices  10.1 us (48%)
  Pallas kernels  4.51 us (21%)
  local copies, waits for them, and re-layouts  2.93 us (14%)
  waiting for transfers between devices  2.79 us (13%)
  other arithmetic  0.62 us (3%)
    ppermute x3, starting transfers between devices, per_device(): arrived.append(lax.ppermute(spectra, axes, moves))  4.49 us
    ppermute x1, starting transfers between devices, per_device(): far_part = lax.ppermute(far_part, axes, both)  3.07 us
    unnamed x8, local copies, waits for them, and re-layouts  2.93 us
    pallas_call x1, Pallas kernels, per_device(): pl.pallas_call(functools.partial(cross_kernel, blocks), out_shape=[part_s...  2.16 us
    ppermute x1, starting transfers between devices, per_device(): return mine + lax.ppermute(theirs, 'win', swap)  2.1 us
    pallas_call x1, Pallas kernels, per_device(): pl.pallas_call(functools.partial(table_kernel, blocks, bins), out_shape=(...  1.31 us
    ppermute x1, waiting for transfers between devices, per_device(): other = lax.ppermute(own, 'win', swap)  1.15 us
    pallas_call x1, Pallas kernels, per_device(): pl.pallas_call(functools.partial(lag_kernel, blocks), out_shape=(half_sha...  1.05 us
  transfers between devices with their start and end apart: 6, of which 4 were waited for; matrix products, arithmetic and copies ran while one was open for 0% of the time, Pallas kernels for 6%

profile of v1, /device:TPU:0, one launch (start us, length us, event | category | flops | bytes accessed | tf_op | source)
XLA Modules:
  0.0 21.0 jit_solution(16771853827378069915)
XLA Ops:
  0.0 0.5 %collective-permute-start = (bf16[12,16,256]{2,1,0:T(8,128)(2,1)}, bf16[12,16,256]{2,1,0:T(8,128)(2,1)S(1)}, u32[]{:S(2)}, u32[]{:S(2)}) collective-permute-start(bf16[12,16,256]{2,1,0:T(8,128)(2,1)} %bitcast.2), channel_id=1, source_target_pairs={{0,1},{1,0},{2,3},{3,2},{4,5},{5,4},{6,7},{7,6},{8,9},{9,8},{10,11... | collective-permute-start | bytes 294920 | tf_op jit(solution)/shard_map/ppermute | solution.py:206
  0.5 1.2 %collective-permute-done.other_ref = bf16[12,16,256]{2,1,0:T(8,128)(2,1)S(1)} collective-permute-done((bf16[12,16,256]{2,1,0:T(8,128)(2,1)}, bf16[12,16,256]{2,1,0:T(8,128)(2,1)S(1)}, u32[]{:S(2)}, u32[]{:S(2)}) %collective-permute-start) | collective-permute-done | bytes 98336 | tf_op jit(solution)/shard_map/ppermute | solution.py:206
  1.6 0.0 copy-start
  1.6 0.9 %copy-done = bf16[12,256,16]{1,2,0:T(8,128)(2,1)S(1)} copy-done((bf16[12,256,16]{1,2,0:T(8,128)(2,1)S(1)}, bf16[12,256,16]{1,2,0:T(8,128)(2,1)}, u32[]{:S(2)}) %copy-start) | copy-done | bytes 98328
  2.5 0.0 copy-start.1
  2.5 0.7 %copy-done.1 = f32[2048]{0:T(1024)S(1)} copy-done((f32[2048]{0:T(1024)S(1)}, f32[2048]{0:T(1024)}, u32[]{:S(2)}) %copy-start.1) | copy-done | bytes 8216
  3.2 0.0 copy-start.3
  3.2 0.7 %copy-done.3 = s32[24]{0:T(128)S(1)} copy-done((s32[24]{0:T(128)S(1)}, s32[24]{0:T(128)}, u32[]{:S(2)}) %copy-start.3) | copy-done | bytes 120
  3.9 2.2 %cross_spectra.1 = (bf16[2,16,256]{2,1,0:T(8,128)(2,1)S(1)}, bf16[2,16,256]{2,1,0:T(8,128)(2,1)S(1)}, bf16[2,2,16,256]{3,2,1,0:T(8,128)(2,1)S(1)}, bf16[2,2,16,2...) custom-call(s32[24]{0:T(128)S(1)} %copy-done.3, f32[1,2048]{1,0:T(1,128)S(1)} %bitcast.4, ...), custom_call_target="tpu_custom_call" | custom-call | tf_op jit(solution)/shard_map/cross_spectra/pallas_call | solution.py:224
  6.0 2.9 %collective-permute-start.2 = (bf16[2,2,16,256]{3,2,1,0:T(8,128)(2,1)S(1)}, bf16[2,2,16,256]{3,2,1,0:T(8,128)(2,1)S(1)}, u32[]{:S(2)}, u32[]{:S(2)}) collective-permute-start(bf16[2,2,16,256]{3,2,1,0:T(8,128)(2,1)S(1)} %get-tuple-element.18), channel_id=1, source_target_pairs={{0,2},{1,11},{2,0},{3,9},{4,6},{5,15},{6,4},{7,13},{8,10},{9,3},{1... | collective-permute-start | bytes 98312 | tf_op jit(solution)/shard_map/ppermute | solution.py:239
  8.9 1.6 %collective-permute-start.3 = (bf16[2,2,16,256]{3,2,1,0:T(8,128)(2,1)S(1)}, bf16[2,2,16,256]{3,2,1,0:T(8,128)(2,1)S(1)}, u32[]{:S(2)}, u32[]{:S(2)}) collective-permute-start(bf16[2,2,16,256]{3,2,1,0:T(8,128)(2,1)S(1)} %get-tuple-element.19), channel_id=1, source_target_pairs={{0,4},{1,13},{2,6},{3,15},{4,0},{5,9},{6,2},{7,11},{8,12},{9,5},{1... | collective-permute-start | bytes 98312 | tf_op jit(solution)/shard_map/ppermute | solution.py:239
  10.5 0.0 collective-permute-start.4
  10.5 3.1 %collective-permute-start.1 = (bf16[2,16,256]{2,1,0:T(8,128)(2,1)S(1)}, bf16[2,16,256]{2,1,0:T(8,128)(2,1)S(1)}, u32[]{:S(2)}, u32[]{:S(2)}) collective-permute-start(bf16[2,16,256]{2,1,0:T(8,128)(2,1)S(1)} %get-tuple-element.17), channel_id=1, source_target_pairs={{0,8},{1,9},{2,10},{3,11},{4,12},{5,13},{6,14},{7,15},{8,0},{9,1},... | collective-permute-start | bytes 49160 | tf_op jit(solution)/shard_map/ppermute | solution.py:235
  13.6 1.3 %lag_table.1 = (bf16[2,256,512]{2,1,0:T(8,128)(2,1)S(1)}, bf16[3,2,256,512]{3,2,1,0:T(8,128)(2,1)S(1)}) custom-call(), custom_call_target="tpu_custom_call" | custom-call | tf_op jit(solution)/shard_map/lag_table/pallas_call | solution.py:213
  14.9 0.4 %collective-permute-done.1.far_ref = bf16[2,16,256]{2,1,0:T(8,128)(2,1)S(1)} collective-permute-done((bf16[2,16,256]{2,1,0:T(8,128)(2,1)S(1)}, bf16[2,16,256]{2,1,0:T(8,128)(2,1)S(1)}, u32[]{:S(2)}, u32[]{:S(2)}) %collective-permute-start.1) | collective-permute-done | bytes 16416 | tf_op jit(solution)/shard_map/ppermute | solution.py:235
  15.3 0.0 collective-permute-done.2.refs_0_
  15.3 0.0 collective-permute-done.3.refs_1_
  15.3 0.3 %collective-permute-done.4.refs_2_ = bf16[2,2,16,256]{3,2,1,0:T(8,128)(2,1)S(1)} collective-permute-done((bf16[2,2,16,256]{3,2,1,0:T(8,128)(2,1)S(1)}, bf16[2,2,16,256]{3,2,1,0:T(8,128)(2,1)S(1)}, u32[]{:S(2)}, u32[]{:S(2)}) %collective-permute-start.4) | collective-permute-done | bytes 32800 | tf_op jit(solution)/shard_map/ppermute | solution.py:239
  15.7 0.0 copy-start.2
  15.7 0.7 %copy-done.2 = s32[8,8]{1,0:T(8,128)S(1)} copy-done((s32[8,8]{1,0:T(8,128)S(1)}, s32[8,8]{1,0:T(8,128)}, u32[]{:S(2)}) %copy-start.2) | copy-done | bytes 280
  16.4 1.0 %lag_sums.1 = (f32[2,16,256]{2,1,0:T(8,128)S(1)}, f32[2,16,256]{2,1,0:T(8,128)S(1)}) custom-call(s32[8,8]{1,0:T(8,128)S(1)} %copy-done.2, bf16[2,256,512]{2,1,0:T(8,128)(2,1)S(1)} %get-tuple-element.14.part_ref, bf16[3,2,256,512]{3,2,1,0:T(8,128)(2,1)S(1)} %get-tuple-element.15.full_ref, bf16[2,16,256]{2,1,0:T(8,128)(2,1)S(1)} %get-tuple-element.16.own_ref, ...), custom_call_target="tpu_custom_call" | custom-call | tf_op jit(solution)/shard_map/lag_sums/pallas_call | solution.py:241
  17.4 2.1 %collective-permute-start.5 = (f32[2,16,256]{2,1,0:T(8,128)S(1)}, f32[2,16,256]{2,1,0:T(8,128)S(1)}, u32[]{:S(2)}, u32[]{:S(2)}) collective-permute-start(f32[2,16,256]{2,1,0:T(8,128)S(1)} %get-tuple-element.22), channel_id=1, source_target_pairs={{0,1},{1,0},{2,3},{3,2},{4,5},{5,4},{6,7},{7,6},{8,9},{9,8},{10,11... | collective-permute-start | bytes 98312 | tf_op jit(solution)/shard_map/ppermute | solution.py:249
  19.5 0.9 %collective-permute-done.5 = f32[2,16,256]{2,1,0:T(8,128)S(1)} collective-permute-done((f32[2,16,256]{2,1,0:T(8,128)S(1)}, f32[2,16,256]{2,1,0:T(8,128)S(1)}, u32[]{:S(2)}, u32[]{:S(2)}) %collective-permute-start.5) | collective-permute-done | bytes 32800 | tf_op jit(solution)/shard_map/ppermute | solution.py:249
  20.4 0.6 %add.3 = f32[2,16,256]{2,1,0:T(8,128)} add(f32[2,16,256]{2,1,0:T(8,128)S(1)} %get-tuple-element.21, f32[2,16,256]{2,1,0:T(8,128)S(1)} %collective-permute-done.5) | non-fusion elementwise | flops 8192 | bytes 98304 | tf_op jit(solution)/shard_map/add | solution.py:249
Async XLA Ops:
  0.0 1.6 %collective-permute-start = (bf16[12,16,256]{2,1,0:T(8,128)(2,1)}, bf16[12,16,256]{2,1,0:T(8,128)(2,1)S(1)}, u32[]{:S(2)}, u32[]{:S(2)}) collective-permute-start(bf16[12,16,256]{2,1,0:T(8,128)(2,1)} %bitcast.2), channel_id=1, source_target_pairs={{0,1},{1,0},{2,3},{3,2},{4,5},{5,4},{6,7},{7,6},{8,9},{9,8},{10,11... | collective-permute-start | bytes 294920 | tf_op jit(solution)/shard_map/ppermute | solution.py:206
  1.6 0.9 %copy-start = (bf16[12,256,16]{1,2,0:T(8,128)(2,1)S(1)}, bf16[12,256,16]{1,2,0:T(8,128)(2,1)}, u32[]{:S(2)}) copy-start(bf16[12,256,16]{1,2,0:T(8,128)(2,1)} %param.4) | copy-start | bytes 294916
  2.5 0.7 %copy-start.1 = (f32[2048]{0:T(1024)S(1)}, f32[2048]{0:T(1024)}, u32[]{:S(2)}) copy-start(f32[2048]{0:T(1024)} %param.6) | copy-start | bytes 24580
  3.2 0.7 %copy-start.3 = (s32[24]{0:T(128)S(1)}, s32[24]{0:T(128)}, u32[]{:S(2)}) copy-start(s32[24]{0:T(128)} %valid_ref.1) | copy-start | bytes 292
  6.0 9.3 %collective-permute-start.2 = (bf16[2,2,16,256]{3,2,1,0:T(8,128)(2,1)S(1)}, bf16[2,2,16,256]{3,2,1,0:T(8,128)(2,1)S(1)}, u32[]{:S(2)}, u32[]{:S(2)}) collective-permute-start(bf16[2,2,16,256]{3,2,1,0:T(8,128)(2,1)S(1)} %get-tuple-element.18), channel_id=1, source_target_pairs={{0,2},{1,11},{2,0},{3,9},{4,6},{5,15},{6,4},{7,13},{8,10},{9,3},{1... | collective-permute-start | bytes 98312 | tf_op jit(solution)/shard_map/ppermute | solution.py:239
  8.9 6.4 %collective-permute-start.3 = (bf16[2,2,16,256]{3,2,1,0:T(8,128)(2,1)S(1)}, bf16[2,2,16,256]{3,2,1,0:T(8,128)(2,1)S(1)}, u32[]{:S(2)}, u32[]{:S(2)}) collective-permute-start(bf16[2,2,16,256]{3,2,1,0:T(8,128)(2,1)S(1)} %get-tuple-element.19), channel_id=1, source_target_pairs={{0,4},{1,13},{2,6},{3,15},{4,0},{5,9},{6,2},{7,11},{8,12},{9,5},{1... | collective-permute-start | bytes 98312 | tf_op jit(solution)/shard_map/ppermute | solution.py:239
  10.5 5.2 %collective-permute-start.4 = (bf16[2,2,16,256]{3,2,1,0:T(8,128)(2,1)S(1)}, bf16[2,2,16,256]{3,2,1,0:T(8,128)(2,1)S(1)}, u32[]{:S(2)}, u32[]{:S(2)}) collective-permute-start(bf16[2,2,16,256]{3,2,1,0:T(8,128)(2,1)S(1)} %get-tuple-element.20), channel_id=1, source_target_pairs={{0,6},{1,15},{2,4},{3,13},{4,2},{5,11},{6,0},{7,9},{8,14},{9,7},{1... | collective-permute-start | bytes 98312 | tf_op jit(solution)/shard_map/ppermute | solution.py:239
  10.5 4.8 %collective-permute-start.1 = (bf16[2,16,256]{2,1,0:T(8,128)(2,1)S(1)}, bf16[2,16,256]{2,1,0:T(8,128)(2,1)S(1)}, u32[]{:S(2)}, u32[]{:S(2)}) collective-permute-start(bf16[2,16,256]{2,1,0:T(8,128)(2,1)S(1)} %get-tuple-element.17), channel_id=1, source_target_pairs={{0,8},{1,9},{2,10},{3,11},{4,12},{5,13},{6,14},{7,15},{8,0},{9,1},... | collective-permute-start | bytes 49160 | tf_op jit(solution)/shard_map/ppermute | solution.py:235
  15.7 0.7 %copy-start.2 = (s32[8,8]{1,0:T(8,128)S(1)}, s32[8,8]{1,0:T(8,128)}, u32[]{:S(2)}) copy-start(s32[8,8]{1,0:T(8,128)} %mask_ref.1) | copy-start | bytes 772
  17.4 3.0 %collective-permute-start.5 = (f32[2,16,256]{2,1,0:T(8,128)S(1)}, f32[2,16,256]{2,1,0:T(8,128)S(1)}, u32[]{:S(2)}, u32[]{:S(2)}) collective-permute-start(f32[2,16,256]{2,1,0:T(8,128)S(1)} %get-tuple-element.22), channel_id=1, source_target_pairs={{0,1},{1,0},{2,3},{3,2},{4,5},{5,4},{6,7},{7,6},{8,9},{9,8},{10,11... | collective-permute-start | bytes 98312 | tf_op jit(solution)/shard_map/ppermute | solution.py:249

commit v2 on v1

v2 whole, which is shorter than its diff:
```python
import functools
import math

import jax
import jax.numpy as jnp
from jax import lax
from jax.experimental import pallas as pl
from jax.experimental.pallas import tpu as pltpu
from jax.sharding import PartitionSpec as P

LAGS = 512
VMEM = pl.BlockSpec(memory_space=pltpu.VMEM)
ANY = pl.BlockSpec(memory_space=pl.ANY)
PARAMS = pltpu.CompilerParams(vmem_limit_bytes=48 * 1024 * 1024)

COS_COEF = (
    0.9999999890590218,
    -0.49999989101070386,
    0.041666489217381156,
    -0.001388780359807859,
    2.476988355752502e-05,
    -2.707903082088142e-07,
    1.724509174527214e-09,
)
SIN_COEF = (
    0.9999997571451633,
    -0.06534424613196173,
    0.001711441007161203,
    -2.461450561671638e-05,
    1.977699154629728e-07,
)


def cos_sin(angle):
    square = angle * angle
    cosine = COS_COEF[-1]
    for coef in COS_COEF[-2::-1]:
        cosine = cosine * square + coef
    sine = SIN_COEF[-1]
    for coef in SIN_COEF[-2::-1]:
        sine = sine * square + coef
    sine = sine * (angle - angle * square * (1.0 / math.pi**2))
    return cosine, sine


def full_distances(blocks):
    half = blocks // 2
    return [(step, step + half) for step in range(1, half)]


def in_hbm(array):
    return pltpu.with_memory_space_constraint(array, pltpu.HBM)


def position():
    return lax.axis_index("sta"), lax.axis_index("win")


def store_phasors(w, phase, usable, cos_ref, sin_ref, sum_ref, gap_ref):
    cosine, sine = cos_sin(phase.astype(jnp.float32))
    cosine = cosine.astype(jnp.bfloat16).astype(jnp.float32) * usable
    sine = sine.astype(jnp.bfloat16).astype(jnp.float32) * usable
    cos_ref[w] = cosine
    sin_ref[w] = sine
    sum_ref[w] = cosine + sine
    gap_ref[w] = cosine - sine


def prepare_kernel(blocks, phase_hbm, valid_hbm, taper_hbm, mask_hbm, *refs):
    own, (usable_ref, weight_ref, keep_ref) = refs[:4], refs[4:7]
    phase_ref, valid_ref, taper_ref, mask_ref, sems = refs[7:]
    sta, win = position()
    windows, stations, bins = phase_ref.shape
    rows = stations // blocks
    if taper_hbm.shape[1] > bins:
        taper_hbm = taper_hbm.at[:, pl.ds(pl.multiple_of(sta * bins, 128), bins)]
    copies = [
        pltpu.make_async_copy(source, target, sems.at[c])
        for c, (source, target) in enumerate(
            (
                (phase_hbm, phase_ref),
                (valid_hbm, valid_ref),
                (taper_hbm, taper_ref),
                (mask_hbm, mask_ref),
            )
        )
    ]
    for copy in copies:
        copy.start()
    for copy in copies[1:]:
        copy.wait()
    count = jnp.float32(0)
    for w in range(2 * windows):
        count += valid_ref[w].astype(jnp.float32)
    total = jnp.maximum(jnp.full((1, bins), count, jnp.float32), 1.0)
    weight_ref[...] = taper_ref[...] * (1.0 / jnp.sqrt(blocks * bins * total))
    for w in range(windows):
        usable = valid_ref[(1 - win) * windows + w].astype(jnp.float32)
        usable_ref[w] = jnp.full((1, bins), usable, jnp.float32)
    source = lax.broadcasted_iota(jnp.int32, keep_ref.shape[1:], 0)
    kept = jnp.zeros(keep_ref.shape[1:], jnp.float32)
    for block in range(blocks):
        kept = jnp.where(source // rows == block, mask_ref[sta, block].astype(jnp.float32), kept)
    for r in range(rows):
        keep_ref[r] = jnp.where(source == sta * rows + r, 0.0, kept)
    copies[0].wait()

    def phasors(w, carry):
        usable = valid_ref[win * windows + w].astype(jnp.float32)
        store_phasors(w, phase_ref[w], usable, *own)
        return carry

    lax.fori_loop(0, windows, phasors, 0, unroll=4)


def part_sums(out_ref, block, is_first, groups, weight):
    rows, stations, bins = out_ref.shape
    totals = [jnp.zeros((stations, bins), jnp.float32)] * rows
    for cos_ref, sin_ref, *_ in groups:

        def add(w, totals, cos_ref=cos_ref, sin_ref=sin_ref):
            cosine, sine = cos_ref[w], sin_ref[w]
            added = []
            for r in range(rows):
                row_cos = cos_ref[w, pl.ds(block * rows + r, 1), :]
                row_sin = sin_ref[w, pl.ds(block * rows + r, 1), :]
                left = jnp.where(is_first, row_cos, row_sin)
                right = jnp.where(is_first, row_sin, -row_cos)
                added.append(totals[r] + (left * cosine + right * sine))
            return added

        totals = lax.fori_loop(0, cos_ref.shape[0], add, totals, unroll=6)
    for r in range(rows):
        out_ref[r] = (totals[r] * weight).astype(jnp.bfloat16)


def full_sums(out_ref, block, groups, weight):
    _, rows, stations, bins = out_ref.shape
    totals = [(jnp.zeros((stations, bins), jnp.float32),) * 3] * rows
    for cos_ref, sin_ref, sum_ref, gap_ref in groups:

        def add(w, totals, cos_ref=cos_ref, sin_ref=sin_ref, sum_ref=sum_ref, gap_ref=gap_ref):
            cosine, plus, gap = cos_ref[w], sum_ref[w], gap_ref[w]
            added = []
            for r in range(rows):
                row = pl.ds(block * rows + r, 1)
                both, left, right = totals[r]
                added.append(
                    (
                        both + sum_ref[w, row, :] * cosine,
                        left + sin_ref[w, row, :] * gap,
                        right + cos_ref[w, row, :] * plus,
                    )
                )
            return added

        totals = lax.fori_loop(0, cos_ref.shape[0], add, totals, unroll=6)
    for r in range(rows):
        both, left, right = totals[r]
        out_ref[0, r] = ((both - left) * weight).astype(jnp.bfloat16)
        out_ref[1, r] = ((both - right) * weight).astype(jnp.bfloat16)


def cross_kernel(blocks, phase_ref, usable_ref, weight_ref, *refs):
    own, other, (far_part, *full_parts) = refs[:4], refs[4:8], refs[8:]
    sta, win = position()
    is_first = win == 0

    def phasors(w, carry):
        store_phasors(w, phase_ref[w], usable_ref[w], *other)
        return carry

    lax.fori_loop(0, phase_ref.shape[0], phasors, 0, unroll=4)
    weight = weight_ref[...]
    for out_ref, pair in zip(full_parts, full_distances(blocks)):
        full_sums(out_ref, sta ^ jnp.where(is_first, pair[0], pair[1]), (own, other), weight)
    part_sums(far_part, sta ^ (blocks // 2), is_first, (own, other), weight)


def table_kernel(blocks, weight_ref, *refs):
    own, other, (own_part, part_ref, full_ref, row_cos, row_sin) = refs[:4], refs[4:8], refs[8:]
    sta, win = position()
    bins, columns = part_ref.shape[1:]
    wrap = 2 * blocks * bins
    half = columns // 2
    step = 16
    column = lax.broadcasted_iota(jnp.int32, (step, columns), 1)
    is_first = win == 0
    lag = jnp.where(is_first, column - half, jnp.where(column < half, column, column - columns))

    def phasor(index):
        wrapped = ((index + wrap // 2) & (wrap - 1)) - wrap // 2
        return cos_sin(wrapped.astype(jnp.float32) * (2.0 * math.pi / wrap))

    fine = lax.broadcasted_iota(jnp.int32, (step, columns), 0)
    fine_cos, fine_sin = phasor(fine * lag)
    steps = bins // step

    def band_rows(block, store):
        for start in range(0, steps, step):
            coarse = block * bins + (start + fine) * step
            row_cos[...], row_sin[...] = phasor(coarse * lag)

            def fill(a, carry, start=start):
                left_cos = row_cos[pl.ds(a, 1), :]
                left_sin = row_sin[pl.ds(a, 1), :]
                cosine = left_cos * fine_cos - left_sin * fine_sin
                sine = left_sin * fine_cos + left_cos * fine_sin
                store(pl.ds(pl.multiple_of((start + a) * step, step), step), cosine, -sine)
                return carry

            lax.fori_loop(0, min(step, steps - start), fill, 0, unroll=2)

    for slot, pair in enumerate(full_distances(blocks)):

        def store_full(place, cosine, sine, slot=slot):
            full_ref[slot, 0, place, :] = cosine.astype(jnp.bfloat16)
            full_ref[slot, 1, place, :] = sine.astype(jnp.bfloat16)

        band_rows(sta ^ jnp.where(is_first, pair[0], pair[1]), store_full)
    for slot, distance in enumerate((0, blocks // 2)):

        def store_part(place, cosine, sine, slot=slot):
            part_ref[slot, place, :] = jnp.where(is_first, cosine, sine).astype(jnp.bfloat16)

        band_rows(sta ^ distance, store_part)
    part_sums(own_part, sta, is_first, (own, other), weight_ref[...])


def times(spectra, table):
    pairs = spectra.shape[0] * spectra.shape[1]
    return jnp.dot(spectra.reshape(pairs, -1), table, preferred_element_type=jnp.float32)


def early_kernel(part_ref, full_ref, own_ref, *refs):
    total = times(own_ref[...], part_ref[0])
    for slot, spectra_ref in enumerate(refs[:-1]):
        for c in range(2):
            total = total + times(spectra_ref[c], full_ref[slot, c])
    refs[-1][...] = total


def late_kernel(side, keep_ref, part_ref, full_ref, early_ref, far_ref, last_ref, out_ref):
    rows, stations, half = out_ref.shape
    lags = pl.ds(side * half, half)
    total = early_ref[:, lags] + times(far_ref[...], part_ref[1, :, lags])
    slot = full_ref.shape[0] - 1
    for c in range(2):
        total = total + times(last_ref[c], full_ref[slot, c, :, lags])
    out_ref[...] = total.reshape(rows, stations, half) * keep_ref[...]


def per_device(phases, window_valid, freq_taper, pair_mask):
    blocks = lax.axis_size("sta")
    windows, bins, stations = phases.shape
    rows = stations // blocks
    half = LAGS // 2
    full = full_distances(blocks)
    swap = [(0, 1), (1, 0)]

    def kernel(body, name, outs, ins, scratch=()):
        return pl.pallas_call(
            body,
            out_shape=[jax.ShapeDtypeStruct(shape, dtype) for shape, dtype in outs],
            in_specs=ins,
            out_specs=[VMEM] * len(outs),
            scratch_shapes=list(scratch),
            compiler_params=PARAMS,
            name=name,
        )

    f32, bf16 = jnp.float32, jnp.bfloat16
    phasor_set = [((windows, stations, bins), f32)] * 4
    part_shape = ((rows, stations, bins), bf16)
    full_shape = ((2, rows, stations, bins), bf16)
    half_shape = ((rows, stations, half), f32)
    phases = jnp.transpose(phases, (0, 2, 1))
    arriving = lax.ppermute(phases, "win", swap)
    taper = freq_taper
    if bins % 128:
        taper = lax.dynamic_slice_in_dim(freq_taper, lax.axis_index("sta") * bins, bins)
    *own, usable, weight, keep = kernel(
        functools.partial(prepare_kernel, blocks),
        "own_phasors",
        phasor_set + [((windows, 1, bins), f32), ((1, bins), f32), half_shape],
        [ANY] * 4,
        [
            pltpu.VMEM((windows, stations, bins), bf16),
            pltpu.SMEM(window_valid.shape, jnp.int32),
            pltpu.VMEM((1, bins), f32),
            pltpu.SMEM(pair_mask.shape, jnp.int32),
            pltpu.SemaphoreType.DMA((4,)),
        ],
    )(*(in_hbm(array) for array in (phases, window_valid, taper.reshape(1, -1), pair_mask)))
    cross = kernel(
        functools.partial(cross_kernel, blocks),
        "cross_spectra",
        phasor_set + [part_shape] + [full_shape] * len(full),
        [VMEM] * 7,
    )(arriving, usable, weight, *own)
    other, far_part, full_parts = cross[:4], cross[4], cross[5:]
    axes = ("sta", "win")

    def send(spectra, pair):
        moves = [(2 * b + w, 2 * (b ^ pair[w]) + w) for b in range(blocks) for w in range(2)]
        return lax.ppermute(spectra, axes, moves)

    arrived = [send(spectra, pair) for spectra, pair in zip(full_parts, full)]
    far_part = send(far_part, (blocks // 2, blocks // 2))
    own_part, part_table, full_table = kernel(
        functools.partial(table_kernel, blocks),
        "lag_table",
        [part_shape, ((2, bins, LAGS), bf16), ((len(full), 2, bins, LAGS), bf16)],
        [VMEM] * 9,
        [pltpu.VMEM((16, LAGS), f32)] * 2,
    )(weight, *own, *other)
    (early,) = kernel(
        early_kernel,
        "lag_sums_early",
        [((rows * stations, LAGS), f32)],
        [VMEM] * (2 + len(full)),
    )(part_table, full_table, own_part, *arrived[:-1])

    def late(side):
        return kernel(
            functools.partial(late_kernel, side), "lag_sums_late", [half_shape], [VMEM] * 6
        )(keep, part_table, full_table, early, far_part, arrived[-1])[0]

    theirs = lax.ppermute(late(1), "win", swap)
    return late(0) + theirs


def solution(mesh):
    return jax.shard_map(
        per_device,
        mesh=mesh,
        in_specs=(P(("days", "win"), "sta", None), P("days"), P(), P()),
        out_specs=P(("days", "sta"), None, "win"),
        check_vma=False,
    )
```

time: 21.2 us -> 16.2 us (0.76)
  local copies, waits for them, and re-layouts: 2.93 us -> 0 us
  waiting for transfers between devices: 2.79 us -> 0.69 us
    unnamed x8 -> x0, local copies, waits for them, and re-layouts: 2.93 us -> none
    ppermute x6, waiting for transfers between devices: 2.79 us -> 0.69 us  [the longest x1 0.67 us: per_device(): theirs = lax.ppermute(late(1), 'win', swap)]
    pallas_call x3 -> x6, Pallas kernels: 4.51 us -> 4.39 us  [the longest x1 1.49 us: per_device(): kernel(functools.partial(table_kernel, blocks), 'lag_table', [part_shape,...]
  transfers between devices with their start and end apart: 6 -> 6, of which waited for: 4 -> 1; matrix products, arithmetic and copies ran while one was open for 0% -> 0% of each run, Pallas kernels for 6% -> 20%
where the time goes in v2:
time: 16.2 us; the launch traced here: 16.1 us
  starting transfers between devices  10.3 us (64%)
  Pallas kernels  4.39 us (27%)
  waiting for transfers between devices  0.69 us (4%)
  other arithmetic  0.62 us (4%)
    ppermute x4, starting transfers between devices, send(): return lax.ppermute(spectra, axes, moves)  7.5 us
    ppermute x1, starting transfers between devices, per_device(): theirs = lax.ppermute(late(1), 'win', swap)  2.35 us
    pallas_call x1, Pallas kernels, per_device(): kernel(functools.partial(table_kernel, blocks), 'lag_table', [part_shape,...  1.49 us
    pallas_call x1, Pallas kernels, per_device(): kernel(functools.partial(prepare_kernel, blocks), 'own_phasors', phasor_s...  1.17 us
    pallas_call x1, Pallas kernels, per_device(): kernel(functools.partial(cross_kernel, blocks), 'cross_spectra', phasor_s...  1.03 us
    ppermute x1, waiting for transfers between devices, per_device(): theirs = lax.ppermute(late(1), 'win', swap)  0.67 us
    add x1, other arithmetic, per_device(): return late(0) + theirs  0.62 us
    ppermute x1, starting transfers between devices, per_device(): arriving = lax.ppermute(phases, 'win', swap)  0.45 us
  transfers between devices with their start and end apart: 6, of which 1 were waited for; matrix products, arithmetic and copies ran while one was open for 0% of the time, Pallas kernels for 20%

profile of v2, /device:TPU:0, one launch (start us, length us, event | category | flops | bytes accessed | tf_op | source)
XLA Modules:
  0.0 16.1 jit_solution(8766750127002211269)
XLA Ops:
  0.0 0.5 %collective-permute-start = (bf16[12,16,256]{2,1,0:T(8,128)(2,1)}, bf16[12,16,256]{2,1,0:T(8,128)(2,1)S(1)}, u32[]{:S(2)}, u32[]{:S(2)}) collective-permute-start(bf16[12,16,256]{2,1,0:T(8,128)(2,1)} %bitcast.2), channel_id=1, source_target_pairs={{0,1},{1,0},{2,3},{3,2},{4,5},{5,4},{6,7},{7,6},{8,9},{9,8},{10,11... | collective-permute-start | bytes 294920 | tf_op jit(solution)/shard_map/ppermute | solution.py:278
  0.5 1.2 %own_phasors.1 = (f32[12,16,256]{2,1,0:T(8,128)S(1)}, f32[12,16,256]{2,1,0:T(8,128)S(1)}, f32[12,16,256]{2,1,0:T(8,128)S(1)}, f32[12,16,256]{2,1,0:T(8,128)S(1)}...) custom-call(bf16[12,16,256]{2,1,0:T(8,128)(2,1)} %bitcast.3, s32[24]{0:T(128)} %valid_hbm.1, ...), custom_call_target="tpu_custom_call" | custom-call | tf_op jit(solution)/shard_map/own_phasors/pallas_call | solution.py:282
  1.6 0.0 collective-permute-done.phase_ref
  1.6 1.0 %cross_spectra.1 = (f32[12,16,256]{2,1,0:T(8,128)S(1)}, f32[12,16,256]{2,1,0:T(8,128)S(1)}, f32[12,16,256]{2,1,0:T(8,128)S(1)}, f32[12,16,256]{2,1,0:T(8,128)S(1...) custom-call(bf16[12,16,256]{2,1,0:T(8,128)(2,1)S(1)} %collective-per, ...), custom_call_target="tpu_custom_call" | custom-call | tf_op jit(solution)/shard_map/cross_spectra/pallas_call | solution.py:295
  2.7 2.9 %collective-permute-start.1 = (bf16[2,2,16,256]{3,2,1,0:T(8,128)(2,1)S(1)}, bf16[2,2,16,256]{3,2,1,0:T(8,128)(2,1)S(1)}, u32[]{:S(2)}, u32[]{:S(2)}) collective-permute-start(bf16[2,2,16,256]{3,2,1,0:T(8,128)(2,1)S(1)} %get-tuple-element.37), channel_id=1, source_target_pairs={{0,2},{1,11},{2,0},{3,9},{4,6},{5,15},{6,4},{7,13},{8,10},{9,3},{1... | collective-permute-start | bytes 98312 | tf_op jit(solution)/shard_map/ppermute | solution.py:306
  5.5 1.6 %collective-permute-start.2 = (bf16[2,2,16,256]{3,2,1,0:T(8,128)(2,1)S(1)}, bf16[2,2,16,256]{3,2,1,0:T(8,128)(2,1)S(1)}, u32[]{:S(2)}, u32[]{:S(2)}) collective-permute-start(bf16[2,2,16,256]{3,2,1,0:T(8,128)(2,1)S(1)} %get-tuple-element.38), channel_id=1, source_target_pairs={{0,4},{1,13},{2,6},{3,15},{4,0},{5,9},{6,2},{7,11},{8,12},{9,5},{1... | collective-permute-start | bytes 98312 | tf_op jit(solution)/shard_map/ppermute | solution.py:306
  7.1 0.0 collective-permute-start.4
  7.1 3.1 %collective-permute-start.3 = (bf16[2,16,256]{2,1,0:T(8,128)(2,1)S(1)}, bf16[2,16,256]{2,1,0:T(8,128)(2,1)S(1)}, u32[]{:S(2)}, u32[]{:S(2)}) collective-permute-start(bf16[2,16,256]{2,1,0:T(8,128)(2,1)S(1)} %get-tuple-element.39), channel_id=1, source_target_pairs={{0,8},{1,9},{2,10},{3,11},{4,12},{5,13},{6,14},{7,15},{8,0},{9,1},... | collective-permute-start | bytes 49160 | tf_op jit(solution)/shard_map/ppermute | solution.py:306
  10.2 1.5 %lag_table.1 = (bf16[2,16,256]{2,1,0:T(8,128)(2,1)S(1)}, bf16[2,256,512]{2,1,0:T(8,128)(2,1)S(1)}, bf16[3,2,256,512]{3,2,1,0:T(8,128)(2,1)S(1)}) custom-call(f32[1,256]{1,0:T(1,128)S(1)} %get-tuple-element.24.weight_ref, f32[12,16,256]{2,1,0:T(8,128)S(1)} %get-tuple-element.25.refs_0_, f32[12,16,256]{2,1,0:T(8,128)S(1)} %get-tuple-element.26.refs_1_, ...), custom_call_target="tpu_custom_call" | custom-call | tf_op jit(solution)/shard_map/lag_table/pallas_call | solution.py:310
  11.7 0.0 collective-permute-done.1.refs_0_
  11.7 0.0 collective-permute-done.2.refs_1_
  11.7 0.3 %lag_sums_early.1.early_ref = f32[32,512]{1,0:T(8,128)S(1)} custom-call(bf16[2,256,512]{2,1,0:T(8,128)(2,1)S(1)} %get-tuple-element.34.part_ref, bf16[3,2,256,512]{3,2,1,0:T(8,128)(2,1)S(1)} %get-tuple-element.35.full_ref, bf16[2,16,256]{2,1,0:T(8,128)(2,1)S(1)} %get-tuple-element.36.own_ref, bf16[2,2,16,256]{3,2,1,0:T(8,128)(2,1)S(1)} %collective-permute-done.1.refs_0_, ...), custom_call_target="tpu_custom_call" | custom-call | tf_op jit(solution)/shard_map/lag_sums_early/pallas_call | solution.py:317
  12.0 0.0 collective-permute-done.3.far_ref
  12.0 0.0 collective-permute-done.4.last_ref
  12.0 0.2 %lag_sums_late.3 = f32[2,16,256]{2,1,0:T(8,128)S(1)} custom-call(f32[2,16,256]{2,1,0:T(8,128)S(1)} %get-tuple-element.23.keep_ref, bf16[2,256,512]{2,1,0:T(8,128)(2,1)S(1)} %get-tuple-element.34.part_ref, bf16[3,2,256,512]{3,2,1,0:T(8,128)(2,1)S(1)} %get-tuple-element.35.full_ref, f32[32,512]{1,0:T(8,128)S(1)} %lag_sums_early.1.early_ref, ...), custom_call_target="tpu_custom_call" | custom-call | tf_op jit(solution)/shard_map/lag_sums_late/pallas_call | solution.py:325
  12.2 2.4 %collective-permute-start.5 = (f32[2,16,256]{2,1,0:T(8,128)S(1)}, f32[2,16,256]{2,1,0:T(8,128)S(1)}, u32[]{:S(2)}, u32[]{:S(2)}) collective-permute-start(f32[2,16,256]{2,1,0:T(8,128)S(1)} %lag_sums_late.3), channel_id=1, source_target_pairs={{0,1},{1,0},{2,3},{3,2},{4,5},{5,4},{6,7},{7,6},{8,9},{9,8},{10,11... | collective-permute-start | bytes 98312 | tf_op jit(solution)/shard_map/ppermute | solution.py:329
  14.6 0.2 %lag_sums_late.2 = f32[2,16,256]{2,1,0:T(8,128)S(1)} custom-call(f32[2,16,256]{2,1,0:T(8,128)S(1)} %get-tuple-element.23.keep_ref, bf16[2,256,512]{2,1,0:T(8,128)(2,1)S(1)} %get-tuple-element.34.part_ref, bf16[3,2,256,512]{3,2,1,0:T(8,128)(2,1)S(1)} %get-tuple-element.35.full_ref, f32[32,512]{1,0:T(8,128)S(1)} %lag_sums_early.1.early_ref, ...), custom_call_target="tpu_custom_call" | custom-call | tf_op jit(solution)/shard_map/lag_sums_late/pallas_call | solution.py:325
  14.8 0.7 %collective-permute-done.5 = f32[2,16,256]{2,1,0:T(8,128)S(1)} collective-permute-done((f32[2,16,256]{2,1,0:T(8,128)S(1)}, f32[2,16,256]{2,1,0:T(8,128)S(1)}, u32[]{:S(2)}, u32[]{:S(2)}) %collective-permute-start.5) | collective-permute-done | bytes 32800 | tf_op jit(solution)/shard_map/ppermute | solution.py:329
  15.5 0.6 %add.3 = f32[2,16,256]{2,1,0:T(8,128)} add(f32[2,16,256]{2,1,0:T(8,128)S(1)} %lag_sums_late.2, f32[2,16,256]{2,1,0:T(8,128)S(1)} %collective-permute-done.5) | non-fusion elementwise | flops 8192 | bytes 98304 | tf_op jit(solution)/shard_map/add | solution.py:330
Async XLA Ops:
  0.0 1.6 %collective-permute-start = (bf16[12,16,256]{2,1,0:T(8,128)(2,1)}, bf16[12,16,256]{2,1,0:T(8,128)(2,1)S(1)}, u32[]{:S(2)}, u32[]{:S(2)}) collective-permute-start(bf16[12,16,256]{2,1,0:T(8,128)(2,1)} %bitcast.2), channel_id=1, source_target_pairs={{0,1},{1,0},{2,3},{3,2},{4,5},{5,4},{6,7},{7,6},{8,9},{9,8},{10,11... | collective-permute-start | bytes 294920 | tf_op jit(solution)/shard_map/ppermute | solution.py:278
  2.7 9.0 %collective-permute-start.1 = (bf16[2,2,16,256]{3,2,1,0:T(8,128)(2,1)S(1)}, bf16[2,2,16,256]{3,2,1,0:T(8,128)(2,1)S(1)}, u32[]{:S(2)}, u32[]{:S(2)}) collective-permute-start(bf16[2,2,16,256]{3,2,1,0:T(8,128)(2,1)S(1)} %get-tuple-element.37), channel_id=1, source_target_pairs={{0,2},{1,11},{2,0},{3,9},{4,6},{5,15},{6,4},{7,13},{8,10},{9,3},{1... | collective-permute-start | bytes 98312 | tf_op jit(solution)/shard_map/ppermute | solution.py:306
  5.5 6.2 %collective-permute-start.2 = (bf16[2,2,16,256]{3,2,1,0:T(8,128)(2,1)S(1)}, bf16[2,2,16,256]{3,2,1,0:T(8,128)(2,1)S(1)}, u32[]{:S(2)}, u32[]{:S(2)}) collective-permute-start(bf16[2,2,16,256]{3,2,1,0:T(8,128)(2,1)S(1)} %get-tuple-element.38), channel_id=1, source_target_pairs={{0,4},{1,13},{2,6},{3,15},{4,0},{5,9},{6,2},{7,11},{8,12},{9,5},{1... | collective-permute-start | bytes 98312 | tf_op jit(solution)/shard_map/ppermute | solution.py:306
  7.1 4.9 %collective-permute-start.4 = (bf16[2,2,16,256]{3,2,1,0:T(8,128)(2,1)S(1)}, bf16[2,2,16,256]{3,2,1,0:T(8,128)(2,1)S(1)}, u32[]{:S(2)}, u32[]{:S(2)}) collective-permute-start(bf16[2,2,16,256]{3,2,1,0:T(8,128)(2,1)S(1)} %get-tuple-element.40), channel_id=1, source_target_pairs={{0,6},{1,15},{2,4},{3,13},{4,2},{5,11},{6,0},{7,9},{8,14},{9,7},{1... | collective-permute-start | bytes 98312 | tf_op jit(solution)/shard_map/ppermute | solution.py:306
  7.1 4.9 %collective-permute-start.3 = (bf16[2,16,256]{2,1,0:T(8,128)(2,1)S(1)}, bf16[2,16,256]{2,1,0:T(8,128)(2,1)S(1)}, u32[]{:S(2)}, u32[]{:S(2)}) collective-permute-start(bf16[2,16,256]{2,1,0:T(8,128)(2,1)S(1)} %get-tuple-element.39), channel_id=1, source_target_pairs={{0,8},{1,9},{2,10},{3,11},{4,12},{5,13},{6,14},{7,15},{8,0},{9,1},... | collective-permute-start | bytes 49160 | tf_op jit(solution)/shard_map/ppermute | solution.py:306
  12.2 3.2 %collective-permute-start.5 = (f32[2,16,256]{2,1,0:T(8,128)S(1)}, f32[2,16,256]{2,1,0:T(8,128)S(1)}, u32[]{:S(2)}, u32[]{:S(2)}) collective-permute-start(f32[2,16,256]{2,1,0:T(8,128)S(1)} %lag_sums_late.3), channel_id=1, source_target_pairs={{0,1},{1,0},{2,3},{3,2},{4,5},{5,4},{6,7},{7,6},{8,9},{9,8},{10,11... | collective-permute-start | bytes 98312 | tf_op jit(solution)/shard_map/ppermute | solution.py:329

commit v3 on v2

--- a/solution.py
+++ b/solution.py
@@ -9,6 +9,10 @@
 from jax.sharding import PartitionSpec as P
 
 LAGS = 512
+LATE = 2
+CHAIN = True
+RING = (1, 2, 0, 3)
+SHIFTS = (3, 1, 2)
 VMEM = pl.BlockSpec(memory_space=pltpu.VMEM)
 ANY = pl.BlockSpec(memory_space=pl.ANY)
 PARAMS = pltpu.CompilerParams(vmem_limit_bytes=48 * 1024 * 1024)
@@ -43,9 +47,32 @@
     return cosine, sine
 
 
-def full_distances(blocks):
-    half = blocks // 2
-    return [(step, step + half) for step in range(1, half)]
+def rounds_of(blocks):
+    pairs = blocks // 2
+    ring, shifts = (RING, SHIFTS) if len(RING) == pairs else (range(pairs), range(1, pairs))
+    place = {pair: index for index, pair in enumerate(ring)}
+
+    def receivers(shift, flip):
+        moved = [ring[(place[b // 2] + shift) % pairs] for b in range(blocks)]
+        return tuple(2 * pair + (b % 2 ^ flip) for b, pair in enumerate(moved))
+
+    rounds = [(True, (receivers(shift, 0), receivers(shift, 1))) for shift in shifts]
+    return rounds + [(False, (receivers(0, 1), receivers(0, 1)))]
+
+
+def lookup(values, sta):
+    found = jnp.int32(values[0])
+    for b, value in enumerate(values[1:], 1):
+        found = jnp.where(sta == b, value, found)
+    return found
+
+
+def peer(targets, sta, is_first):
+    return jnp.where(is_first, lookup(targets[0], sta), lookup(targets[1], sta))
+
+
+def sources(targets):
+    return tuple(tuple(sorted(range(len(side)), key=lambda b: side[b])) for side in targets)
 
 
 def in_hbm(array):
@@ -161,23 +188,30 @@
         out_ref[1, r] = ((both - right) * weight).astype(jnp.bfloat16)
 
 
-def cross_kernel(blocks, phase_ref, usable_ref, weight_ref, *refs):
-    own, other, (far_part, *full_parts) = refs[:4], refs[4:8], refs[8:]
-    sta, win = position()
-    is_first = win == 0
-
+def other_kernel(phase_ref, usable_ref, *other):
     def phasors(w, carry):
         store_phasors(w, phase_ref[w], usable_ref[w], *other)
         return carry
 
     lax.fori_loop(0, phase_ref.shape[0], phasors, 0, unroll=4)
-    weight = weight_ref[...]
-    for out_ref, pair in zip(full_parts, full_distances(blocks)):
-        full_sums(out_ref, sta ^ jnp.where(is_first, pair[0], pair[1]), (own, other), weight)
-    part_sums(far_part, sta ^ (blocks // 2), is_first, (own, other), weight)
-
-
-def table_kernel(blocks, weight_ref, *refs):
+
+
+def cross_kernel(rounds, first, phase_ref, usable_ref, weight_ref, *refs):
+    own, other, outs = refs[:4], refs[4:8], refs[8:]
+    if first:
+        other_kernel(phase_ref, usable_ref, *other)
+    else:
+        outs = outs[1:]
+    sta, win = position()
+    for (whole, targets), out_ref in zip(rounds, outs):
+        block = peer(targets, sta, win == 0)
+        if whole:
+            full_sums(out_ref, block, (own, other), weight_ref[...])
+        else:
+            part_sums(out_ref, block, win == 0, (own, other), weight_ref[...])
+
+
+def table_kernel(blocks, rounds, weight_ref, *refs):
     own, other, (own_part, part_ref, full_ref, row_cos, row_sin) = refs[:4], refs[4:8], refs[8:]
     sta, win = position()
     bins, columns = part_ref.shape[1:]
@@ -211,19 +245,21 @@
 
             lax.fori_loop(0, min(step, steps - start), fill, 0, unroll=2)
 
-    for slot, pair in enumerate(full_distances(blocks)):
+    full = [sources(targets) for whole, targets in rounds if whole]
+    (shared,) = [sources(targets) for whole, targets in rounds if not whole]
+    for slot, targets in enumerate(full):
 
         def store_full(place, cosine, sine, slot=slot):
             full_ref[slot, 0, place, :] = cosine.astype(jnp.bfloat16)
             full_ref[slot, 1, place, :] = sine.astype(jnp.bfloat16)
 
-        band_rows(sta ^ jnp.where(is_first, pair[0], pair[1]), store_full)
-    for slot, distance in enumerate((0, blocks // 2)):
+        band_rows(peer(targets, sta, is_first), store_full)
+    for slot, block in enumerate((sta, peer(shared, sta, is_first))):
 
         def store_part(place, cosine, sine, slot=slot):
             part_ref[slot, place, :] = jnp.where(is_first, cosine, sine).astype(jnp.bfloat16)
 
-        band_rows(sta ^ distance, store_part)
+        band_rows(block, store_part)
     part_sums(own_part, sta, is_first, (own, other), weight_ref[...])
 
 
@@ -232,21 +268,27 @@
     return jnp.dot(spectra.reshape(pairs, -1), table, preferred_element_type=jnp.float32)
 
 
-def early_kernel(part_ref, full_ref, own_ref, *refs):
-    total = times(own_ref[...], part_ref[0])
-    for slot, spectra_ref in enumerate(refs[:-1]):
-        for c in range(2):
-            total = total + times(spectra_ref[c], full_ref[slot, c])
-    refs[-1][...] = total
-
-
-def late_kernel(side, keep_ref, part_ref, full_ref, early_ref, far_ref, last_ref, out_ref):
+def add_slot(total, spectra_ref, slot, part_ref, full_ref, lags):
+    if slot < 0:
+        return total + times(spectra_ref[...], part_ref[-slot, :, lags])
+    for c in range(2):
+        total = total + times(spectra_ref[c], full_ref[slot, c, :, lags])
+    return total
+
+
+def early_kernel(slot, before, part_ref, full_ref, before_ref, spectra_ref, out_ref):
+    lags = pl.ds(0, out_ref.shape[-1])
+    total = before_ref[...] if before else times(before_ref[...], part_ref[0])
+    out_ref[...] = add_slot(total, spectra_ref, slot, part_ref, full_ref, lags)
+
+
+def late_kernel(slots, side, keep_ref, part_ref, full_ref, early_ref, *refs):
+    out_ref = refs[-1]
     rows, stations, half = out_ref.shape
     lags = pl.ds(side * half, half)
-    total = early_ref[:, lags] + times(far_ref[...], part_ref[1, :, lags])
-    slot = full_ref.shape[0] - 1
-    for c in range(2):
-        total = total + times(last_ref[c], full_ref[slot, c, :, lags])
+    total = early_ref[:, lags]
+    for slot, spectra_ref in zip(slots, refs[:-1]):
+        total = add_slot(total, spectra_ref, slot, part_ref, full_ref, lags)
     out_ref[...] = total.reshape(rows, stations, half) * keep_ref[...]
 
 
@@ -255,7 +297,7 @@
     windows, bins, stations = phases.shape
     rows = stations // blocks
     half = LAGS // 2
-    full = full_distances(blocks)
+    rounds = rounds_of(blocks)
     swap = [(0, 1), (1, 0)]
 
     def kernel(body, name, outs, ins, scratch=()):
@@ -292,39 +334,52 @@
             pltpu.SemaphoreType.DMA((4,)),
         ],
     )(*(in_hbm(array) for array in (phases, window_valid, taper.reshape(1, -1), pair_mask)))
-    cross = kernel(
-        functools.partial(cross_kernel, blocks),
-        "cross_spectra",
-        phasor_set + [part_shape] + [full_shape] * len(full),
-        [VMEM] * 7,
-    )(arriving, usable, weight, *own)
-    other, far_part, full_parts = cross[:4], cross[4], cross[5:]
     axes = ("sta", "win")
-
-    def send(spectra, pair):
-        moves = [(2 * b + w, 2 * (b ^ pair[w]) + w) for b in range(blocks) for w in range(2)]
-        return lax.ppermute(spectra, axes, moves)
-
-    arrived = [send(spectra, pair) for spectra, pair in zip(full_parts, full)]
-    far_part = send(far_part, (blocks // 2, blocks // 2))
+    sent, shapes = [], {True: full_shape, False: part_shape}
+    for first, group in enumerate([[r] for r in rounds] if CHAIN else [rounds]):
+        outs = [shapes[whole] for whole, _ in group]
+        if not first:
+            *other, made = kernel(
+                functools.partial(cross_kernel, group, True), "cross_spectra", phasor_set + outs, [VMEM] * 7
+            )(arriving, usable, weight, *own)
+            sent.append(made)
+        else:
+            (made,) = kernel(
+                functools.partial(cross_kernel, group, False), "cross_spectra", outs, [VMEM] * 12
+            )(arriving, usable, weight, *own, *other, sent[-1])
+            sent.append(made)
+    arrived = []
+    for spectra, (_, targets) in zip(sent, rounds):
+        moves = [(2 * b + w, 2 * targets[w][b] + w) for b in range(blocks) for w in range(2)]
+        arrived.append(lax.ppermute(spectra, axes, moves))
     own_part, part_table, full_table = kernel(
-        functools.partial(table_kernel, blocks),
+        functools.partial(table_kernel, blocks, rounds),
         "lag_table",
-        [part_shape, ((2, bins, LAGS), bf16), ((len(full), 2, bins, LAGS), bf16)],
+        [part_shape, ((2, bins, LAGS), bf16), ((len(rounds) - 1, 2, bins, LAGS), bf16)],
         [VMEM] * 9,
         [pltpu.VMEM((16, LAGS), f32)] * 2,
     )(weight, *own, *other)
-    (early,) = kernel(
-        early_kernel,
-        "lag_sums_early",
-        [((rows * stations, LAGS), f32)],
-        [VMEM] * (2 + len(full)),
-    )(part_table, full_table, own_part, *arrived[:-1])
+    slots, slot = [], 0
+    for whole, _ in rounds:
+        slots.append(slot if whole else -1)
+        slot += whole
+    ahead = len(rounds) - LATE
+    early = own_part
+    for index in range(ahead):
+        (early,) = kernel(
+            functools.partial(early_kernel, slots[index], index),
+            "lag_sums_early",
+            [((rows * stations, LAGS), f32)],
+            [VMEM] * 4,
+        )(part_table, full_table, early, arrived[index])
 
     def late(side):
         return kernel(
-            functools.partial(late_kernel, side), "lag_sums_late", [half_shape], [VMEM] * 6
-        )(keep, part_table, full_table, early, far_part, arrived[-1])[0]
+            functools.partial(late_kernel, slots[ahead:], side),
+            "lag_sums_late",
+            [half_shape],
+            [VMEM] * (4 + LATE),
+        )(keep, part_table, full_table, early, *arrived[ahead:])[0]
 
     theirs = lax.ppermute(late(1), "win", swap)
     return late(0) + theirs

time: 16.2 us -> 14.6 us (0.901)
  starting transfers between devices: 10.3 us -> 8.13 us
  waiting for transfers between devices: 0.69 us -> 1.09 us
    ppermute x1, starting transfers between devices: 2.35 us -> 0.47 us  [per_device(): theirs = lax.ppermute(late(1), 'win', swap)]
    ppermute x4, waiting for transfers between devices: 0.02 us -> 0.42 us  [per_device(): arrived.append(lax.ppermute(spectra, axes, moves))]
    ppermute x4, starting transfers between devices: 7.5 us -> 7.21 us  [per_device(): arrived.append(lax.ppermute(spectra, axes, moves))]
    pallas_call x5 -> x9, Pallas kernels: 3.22 us -> 3.36 us  [the longest x1 1.49 us: per_device(): kernel(functools.partial(table_kernel, blocks, rounds), 'lag_table', [par...]
  transfers between devices with their start and end apart: 6 -> 6, of which waited for: 1 -> 2; matrix products, arithmetic and copies ran while one was open for 0% -> 0% of each run, Pallas kernels for 20% -> 27%
where the time goes in v3:
time: 14.6 us; the launch traced here: 14.4 us
  starting transfers between devices  8.13 us (56%)
  Pallas kernels  4.54 us (31%)
  waiting for transfers between devices  1.09 us (7%)
  other arithmetic  0.62 us (4%)
    ppermute x4, starting transfers between devices, per_device(): arrived.append(lax.ppermute(spectra, axes, moves))  7.21 us
    pallas_call x1, Pallas kernels, per_device(): kernel(functools.partial(table_kernel, blocks, rounds), 'lag_table', [par...  1.49 us
    pallas_call x1, Pallas kernels, per_device(): kernel(functools.partial(prepare_kernel, blocks), 'own_phasors', phasor_s...  1.17 us
    ppermute x1, waiting for transfers between devices, per_device(): theirs = lax.ppermute(late(1), 'win', swap)  0.67 us
    add x1, other arithmetic, per_device(): return late(0) + theirs  0.62 us
    pallas_call x3, Pallas kernels, per_device(): kernel(functools.partial(cross_kernel, group, False), 'cross_spectra', ou...  0.59 us
    ppermute x1, starting transfers between devices, per_device(): theirs = lax.ppermute(late(1), 'win', swap)  0.47 us
    pallas_call x1, Pallas kernels, per_device(): kernel(functools.partial(cross_kernel, group, True), 'cross_spectra', pha...  0.47 us
  transfers between devices with their start and end apart: 6, of which 2 were waited for; matrix products, arithmetic and copies ran while one was open for 0% of the time, Pallas kernels for 27%

profile of v3, /device:TPU:0, one launch (start us, length us, event | category | flops | bytes accessed | tf_op | source)
XLA Modules:
  0.0 14.4 jit_solution(3967592546505936853)
XLA Ops:
  0.0 0.5 %collective-permute-start = (bf16[12,16,256]{2,1,0:T(8,128)(2,1)}, bf16[12,16,256]{2,1,0:T(8,128)(2,1)S(1)}, u32[]{:S(2)}, u32[]{:S(2)}) collective-permute-start(bf16[12,16,256]{2,1,0:T(8,128)(2,1)} %bitcast.2), channel_id=1, source_target_pairs={{0,1},{1,0},{2,3},{3,2},{4,5},{5,4},{6,7},{7,6},{8,9},{9,8},{10,11... | collective-permute-start | bytes 294920 | tf_op jit(solution)/shard_map/ppermute | solution.py:320
  0.5 1.2 %own_phasors.1 = (f32[12,16,256]{2,1,0:T(8,128)S(1)}, f32[12,16,256]{2,1,0:T(8,128)S(1)}, f32[12,16,256]{2,1,0:T(8,128)S(1)}, f32[12,16,256]{2,1,0:T(8,128)S(1)}...) custom-call(bf16[12,16,256]{2,1,0:T(8,128)(2,1)} %bitcast.3, s32[24]{0:T(128)} %valid_hbm.1, ...), custom_call_target="tpu_custom_call" | custom-call | tf_op jit(solution)/shard_map/own_phasors/pallas_call | solution.py:324
  1.6 0.0 collective-permute-done.phase_ref
  1.6 0.5 %cross_spectra.4 = (f32[12,16,256]{2,1,0:T(8,128)S(1)}, f32[12,16,256]{2,1,0:T(8,128)S(1)}, f32[12,16,256]{2,1,0:T(8,128)S(1)}, f32[12,16,256]{2,1,0:T(8,128)S(1)}, bf16[2,2,16,256]{3,2,1,0:T(8,128)(2,1)S(1)}) custom-call(bf16[12,16,256]{2,1,0:T(8,128)(2,1)S(1)} %collective-permute-done.phase_ref, f32[12,1,256]{2,1,0:T(1,128)S(1)} %get-tuple-element.26.usable_ref, ...), custom_call_target="tpu_custom_call" | custom-call | tf_op jit(solution)/shard_map/cross_spectra/pallas_call | solution.py:342
  2.1 3.9 %collective-permute-start.1 = (bf16[2,2,16,256]{3,2,1,0:T(8,128)(2,1)S(1)}, bf16[2,2,16,256]{3,2,1,0:T(8,128)(2,1)S(1)}, u32[]{:S(2)}, u32[]{:S(2)}) collective-permute-start(bf16[2,2,16,256]{3,2,1,0:T(8,128)(2,1)S(1)} %get-tuple-element.34.refs_8_), channel_id=1, source_target_pairs={{0,8},{1,11},{2,10},{3,9},{4,12},{5,15},{6,14},{7,13},{8,4},{9,7},... | collective-permute-start | bytes 98312 | tf_op jit(solution)/shard_map/ppermute | solution.py:354
  6.0 0.2 %cross_spectra.5.refs_8_ = bf16[2,2,16,256]{3,2,1,0:T(8,128)(2,1)S(1)} custom-call(bf16[12,16,256]{2,1,0:T(8,128)(2,1)S(1)} %collective-permute-done.phase_ref, f32[12,1,256]{2,1,0:T(1,128)S(1)} %get-tuple-element.26.usable_ref, f32[1,256]{1,0:T(1,128)S(1)} %get-tuple-element.21.weight_ref, f32[12,16,256]{2,1,0:T(8,128)S(1)} %get-tuple-element.22.refs_0_, ...), custom_call_target="tpu_custom_call" | custom-call | tf_op jit(solution)/shard_map/cross_spectra/pallas_call | solution.py:347
  6.3 1.1 %collective-permute-start.2 = (bf16[2,2,16,256]{3,2,1,0:T(8,128)(2,1)S(1)}, bf16[2,2,16,256]{3,2,1,0:T(8,128)(2,1)S(1)}, u32[]{:S(2)}, u32[]{:S(2)}) collective-permute-start(bf16[2,2,16,256]{3,2,1,0:T(8,128)(2,1)S(1)} %cross_spectra.5.refs_8_), channel_id=1, source_target_pairs={{0,12},{1,15},{2,14},{3,13},{4,8},{5,11},{6,10},{7,9},{8,0},{9,3},... | collective-permute-start | bytes 98312 | tf_op jit(solution)/shard_map/ppermute | solution.py:354
  7.3 0.2 %cross_spectra.6.refs_8_ = bf16[2,2,16,256]{3,2,1,0:T(8,128)(2,1)S(1)} custom-call(bf16[12,16,256]{2,1,0:T(8,128)(2,1)S(1)} %collective-permute-done.phase_ref, f32[12,1,256]{2,1,0:T(1,128)S(1)} %get-tuple-element.26.usable_ref, f32[1,256]{1,0:T(1,128)S(1)} %get-tuple-element.21.weight_ref, f32[12,16,256]{2,1,0:T(8,128)S(1)} %get-tuple-element.22.refs_0_, ...), custom_call_target="tpu_custom_call" | custom-call | tf_op jit(solution)/shard_map/cross_spectra/pallas_call | solution.py:347
  7.5 0.7 %collective-permute-start.3 = (bf16[2,2,16,256]{3,2,1,0:T(8,128)(2,1)S(1)}, bf16[2,2,16,256]{3,2,1,0:T(8,128)(2,1)S(1)}, u32[]{:S(2)}, u32[]{:S(2)}) collective-permute-start(bf16[2,2,16,256]{3,2,1,0:T(8,128)(2,1)S(1)} %cross_spectra.6.refs_8_), channel_id=1, source_target_pairs={{0,4},{1,7},{2,6},{3,5},{4,0},{5,3},{6,2},{7,1},{8,12},{9,15},{10,... | collective-permute-start | bytes 98312 | tf_op jit(solution)/shard_map/ppermute | solution.py:354
  8.2 0.2 %cross_spectra.7 = bf16[2,16,256]{2,1,0:T(8,128)(2,1)S(1)} custom-call(bf16[12,16,256]{2,1,0:T(8,128)(2,1)S(1)} %collective-permute-done.phase_ref, f32[12,1,256]{2,1,0:T(1,128)S(1)} %get-tuple-element.26.usable_ref, f32[1,256]{1,0:T(1,128)S(1)} %get-tuple-element.21.weight_ref, f32[12,16,256]{2,1,0:T(8,128)S(1)} %get-tuple-element.22.refs_0_, ...), custom_call_target="tpu_custom_call" | custom-call | tf_op jit(solution)/shard_map/cross_spectra/pallas_call | solution.py:347
  8.4 1.6 %collective-permute-start.4 = (bf16[2,16,256]{2,1,0:T(8,128)(2,1)S(1)}, bf16[2,16,256]{2,1,0:T(8,128)(2,1)S(1)}, u32[]{:S(2)}, u32[]{:S(2)}) collective-permute-start(bf16[2,16,256]{2,1,0:T(8,128)(2,1)S(1)} %cross_spectra.7), channel_id=1, source_target_pairs={{0,2},{1,3},{2,0},{3,1},{4,6},{5,7},{6,4},{7,5},{8,10},{9,11},{10,... | collective-permute-start | bytes 49160 | tf_op jit(solution)/shard_map/ppermute | solution.py:354
  9.9 1.5 %lag_table.1 = (bf16[2,16,256]{2,1,0:T(8,128)(2,1)S(1)}, bf16[2,256,512]{2,1,0:T(8,128)(2,1)S(1)}, bf16[3,2,256,512]{3,2,1,0:T(8,128)(2,1)S(1)}) custom-call(f32[1,256]{1,0:T(1,128)S(1)} %get-tuple-element.21.weight_ref, f32[12,16,256]{2,1,0:T(8,128)S(1)} %get-tuple-element.22.refs_0_, f32[12,16,256]{2,1,0:T(8,128)S(1)} %get-tuple-element.23.refs_1_, ...), custom_call_target="tpu_custom_call" | custom-call | tf_op jit(solution)/shard_map/lag_table/pallas_call | solution.py:355
  11.4 0.0 collective-permute-done.1.spectra_ref
  11.4 0.2 %lag_sums_early.2.before_ref = f32[32,512]{1,0:T(8,128)S(1)} custom-call(bf16[2,256,512]{2,1,0:T(8,128)(2,1)S(1)} %get-tuple-element.31.part_ref, bf16[3,2,256,512]{3,2,1,0:T(8,128)(2,1)S(1)} %get-tuple-element.32.full_ref, bf16[2,16,256]{2,1,0:T(8,128)(2,1)S(1)} %get-tuple-element.33.before_ref, bf16[2,2,16,256]{3,2,1,0:T(8,128)(2,1)S(1)} %collective-permute-done.1.spectra_ref), custom_call_target="tpu_custom_call" | custom-call | tf_op jit(solution)/shard_map/lag_sums_early/pallas_call | solution.py:369
  11.7 0.0 collective-permute-done.2.spectra_ref
  11.7 0.2 %lag_sums_early.3.early_ref = f32[32,512]{1,0:T(8,128)S(1)} custom-call(bf16[2,256,512]{2,1,0:T(8,128)(2,1)S(1)} %get-tuple-element.31.part_ref, bf16[3,2,256,512]{3,2,1,0:T(8,128)(2,1)S(1)} %get-tuple-element.32.full_ref, f32[32,512]{1,0:T(8,128)S(1)} %lag_sums_early.2.before_ref, bf16[2,2,16,256]{3,2,1,0:T(8,128)(2,1)S(1)} %collective-permute-done.2.spectra_ref), custom_call_target="tpu_custom_call" | custom-call | tf_op jit(solution)/shard_map/lag_sums_early/pallas_call | solution.py:369
  11.9 0.4 %collective-permute-done.4.refs_1_ = bf16[2,16,256]{2,1,0:T(8,128)(2,1)S(1)} collective-permute-done((bf16[2,16,256]{2,1,0:T(8,128)(2,1)S(1)}, bf16[2,16,256]{2,1,0:T(8,128)(2,1)S(1)}, u32[]{:S(2)}, u32[]{:S(2)}) %collective-permute-start.4) | collective-permute-done | bytes 16416 | tf_op jit(solution)/shard_map/ppermute | solution.py:354
  12.3 0.0 collective-permute-done.3.refs_0_
  12.3 0.2 %lag_sums_late.3 = f32[2,16,256]{2,1,0:T(8,128)S(1)} custom-call(f32[2,16,256]{2,1,0:T(8,128)S(1)} %get-tuple-element.20.keep_ref, bf16[2,256,512]{2,1,0:T(8,128)(2,1)S(1)} %get-tuple-element.31.part_ref, bf16[3,2,256,512]{3,2,1,0:T(8,128)(2,1)S(1)} %get-tuple-element.32.full_ref, f32[32,512]{1,0:T(8,128)S(1)} %lag_sums_early.3.early_ref, ...), custom_call_target="tpu_custom_call" | custom-call | tf_op jit(solution)/shard_map/lag_sums_late/pallas_call | solution.py:377
  12.5 0.5 %collective-permute-start.5 = (f32[2,16,256]{2,1,0:T(8,128)S(1)}, f32[2,16,256]{2,1,0:T(8,128)S(1)}, u32[]{:S(2)}, u32[]{:S(2)}) collective-permute-start(f32[2,16,256]{2,1,0:T(8,128)S(1)} %lag_sums_late.3), channel_id=1, source_target_pairs={{0,1},{1,0},{2,3},{3,2},{4,5},{5,4},{6,7},{7,6},{8,9},{9,8},{10,11... | collective-permute-start | bytes 98312 | tf_op jit(solution)/shard_map/ppermute | solution.py:384
  13.0 0.2 %lag_sums_late.2 = f32[2,16,256]{2,1,0:T(8,128)S(1)} custom-call(f32[2,16,256]{2,1,0:T(8,128)S(1)} %get-tuple-element.20.keep_ref, bf16[2,256,512]{2,1,0:T(8,128)(2,1)S(1)} %get-tuple-element.31.part_ref, bf16[3,2,256,512]{3,2,1,0:T(8,128)(2,1)S(1)} %get-tuple-element.32.full_ref, f32[32,512]{1,0:T(8,128)S(1)} %lag_sums_early.3.early_ref, ...), custom_call_target="tpu_custom_call" | custom-call | tf_op jit(solution)/shard_map/lag_sums_late/pallas_call | solution.py:377
  13.2 0.7 %collective-permute-done.5 = f32[2,16,256]{2,1,0:T(8,128)S(1)} collective-permute-done((f32[2,16,256]{2,1,0:T(8,128)S(1)}, f32[2,16,256]{2,1,0:T(8,128)S(1)}, u32[]{:S(2)}, u32[]{:S(2)}) %collective-permute-start.5) | collective-permute-done | bytes 32800 | tf_op jit(solution)/shard_map/ppermute | solution.py:384
  13.8 0.6 %add.3 = f32[2,16,256]{2,1,0:T(8,128)} add(f32[2,16,256]{2,1,0:T(8,128)S(1)} %lag_sums_late.2, f32[2,16,256]{2,1,0:T(8,128)S(1)} %collective-permute-done.5) | non-fusion elementwise | flops 8192 | bytes 98304 | tf_op jit(solution)/shard_map/add | solution.py:385
Async XLA Ops:
  0.0 1.6 %collective-permute-start = (bf16[12,16,256]{2,1,0:T(8,128)(2,1)}, bf16[12,16,256]{2,1,0:T(8,128)(2,1)S(1)}, u32[]{:S(2)}, u32[]{:S(2)}) collective-permute-start(bf16[12,16,256]{2,1,0:T(8,128)(2,1)} %bitcast.2), channel_id=1, source_target_pairs={{0,1},{1,0},{2,3},{3,2},{4,5},{5,4},{6,7},{7,6},{8,9},{9,8},{10,11... | collective-permute-start | bytes 294920 | tf_op jit(solution)/shard_map/ppermute | solution.py:320
  2.1 9.3 %collective-permute-start.1 = (bf16[2,2,16,256]{3,2,1,0:T(8,128)(2,1)S(1)}, bf16[2,2,16,256]{3,2,1,0:T(8,128)(2,1)S(1)}, u32[]{:S(2)}, u32[]{:S(2)}) collective-permute-start(bf16[2,2,16,256]{3,2,1,0:T(8,128)(2,1)S(1)} %get-tuple-element.34.refs_8_), channel_id=1, source_target_pairs={{0,8},{1,11},{2,10},{3,9},{4,12},{5,15},{6,14},{7,13},{8,4},{9,7},... | collective-permute-start | bytes 98312 | tf_op jit(solution)/shard_map/ppermute | solution.py:354
  6.3 5.4 %collective-permute-start.2 = (bf16[2,2,16,256]{3,2,1,0:T(8,128)(2,1)S(1)}, bf16[2,2,16,256]{3,2,1,0:T(8,128)(2,1)S(1)}, u32[]{:S(2)}, u32[]{:S(2)}) collective-permute-start(bf16[2,2,16,256]{3,2,1,0:T(8,128)(2,1)S(1)} %cross_spectra.5.refs_8_), channel_id=1, source_target_pairs={{0,12},{1,15},{2,14},{3,13},{4,8},{5,11},{6,10},{7,9},{8,0},{9,3},... | collective-permute-start | bytes 98312 | tf_op jit(solution)/shard_map/ppermute | solution.py:354
  7.5 4.8 %collective-permute-start.3 = (bf16[2,2,16,256]{3,2,1,0:T(8,128)(2,1)S(1)}, bf16[2,2,16,256]{3,2,1,0:T(8,128)(2,1)S(1)}, u32[]{:S(2)}, u32[]{:S(2)}) collective-permute-start(bf16[2,2,16,256]{3,2,1,0:T(8,128)(2,1)S(1)} %cross_spectra.6.refs_8_), channel_id=1, source_target_pairs={{0,4},{1,7},{2,6},{3,5},{4,0},{5,3},{6,2},{7,1},{8,12},{9,15},{10,... | collective-permute-start | bytes 98312 | tf_op jit(solution)/shard_map/ppermute | solution.py:354
  8.4 3.9 %collective-permute-start.4 = (bf16[2,16,256]{2,1,0:T(8,128)(2,1)S(1)}, bf16[2,16,256]{2,1,0:T(8,128)(2,1)S(1)}, u32[]{:S(2)}, u32[]{:S(2)}) collective-permute-start(bf16[2,16,256]{2,1,0:T(8,128)(2,1)S(1)} %cross_spectra.7), channel_id=1, source_target_pairs={{0,2},{1,3},{2,0},{3,1},{4,6},{5,7},{6,4},{7,5},{8,10},{9,11},{10,... | collective-permute-start | bytes 49160 | tf_op jit(solution)/shard_map/ppermute | solution.py:354
  12.5 1.3 %collective-permute-start.5 = (f32[2,16,256]{2,1,0:T(8,128)S(1)}, f32[2,16,256]{2,1,0:T(8,128)S(1)}, u32[]{:S(2)}, u32[]{:S(2)}) collective-permute-start(f32[2,16,256]{2,1,0:T(8,128)S(1)} %lag_sums_late.3), channel_id=1, source_target_pairs={{0,1},{1,0},{2,3},{3,2},{4,5},{5,4},{6,7},{7,6},{8,9},{9,8},{10,11... | collective-permute-start | bytes 98312 | tf_op jit(solution)/shard_map/ppermute | solution.py:384

commit v4 on v3

--- a/solution.py
+++ b/solution.py
@@ -10,9 +10,13 @@
 
 LAGS = 512
 LATE = 2
-CHAIN = True
-RING = (1, 2, 0, 3)
-SHIFTS = (3, 1, 2)
+BEGUN = 2
+ROUNDS = (
+    ((3, 5, 1, 7, 2, 6, 0, 4), (5, 7, 4, 6, 1, 2, 3, 0)),
+    ((4, 2, 6, 0, 7, 1, 5, 3), (6, 4, 7, 1, 3, 0, 2, 5)),
+    ((2, 0, 3, 5, 6, 4, 7, 1), (7, 6, 5, 4, 0, 3, 1, 2)),
+    ((1, 3, 0, 2, 5, 7, 4, 6), (1, 3, 0, 2, 5, 7, 4, 6)),
+)
 VMEM = pl.BlockSpec(memory_space=pltpu.VMEM)
 ANY = pl.BlockSpec(memory_space=pl.ANY)
 PARAMS = pltpu.CompilerParams(vmem_limit_bytes=48 * 1024 * 1024)
@@ -48,16 +52,11 @@
 
 
 def rounds_of(blocks):
-    pairs = blocks // 2
-    ring, shifts = (RING, SHIFTS) if len(RING) == pairs else (range(pairs), range(1, pairs))
-    place = {pair: index for index, pair in enumerate(ring)}
-
-    def receivers(shift, flip):
-        moved = [ring[(place[b // 2] + shift) % pairs] for b in range(blocks)]
-        return tuple(2 * pair + (b % 2 ^ flip) for b, pair in enumerate(moved))
-
-    rounds = [(True, (receivers(shift, 0), receivers(shift, 1))) for shift in shifts]
-    return rounds + [(False, (receivers(0, 1), receivers(0, 1)))]
+    rounds = ROUNDS
+    if blocks != len(ROUNDS[0][0]):
+        steps = [(step, step ^ 1) for step in range(2, blocks, 2)] + [(1, 1)]
+        rounds = [tuple(tuple(b ^ step for b in range(blocks)) for step in pair) for pair in steps]
+    return [(pair[0] != pair[1], pair) for pair in rounds]
 
 
 def lookup(values, sta):
@@ -93,9 +92,10 @@
     gap_ref[w] = cosine - sine
 
 
-def prepare_kernel(blocks, phase_hbm, valid_hbm, taper_hbm, mask_hbm, *refs):
+def prepare_kernel(blocks, begun, phase_hbm, valid_hbm, taper_hbm, mask_hbm, *refs):
     own, (usable_ref, weight_ref, keep_ref) = refs[:4], refs[4:7]
-    phase_ref, valid_ref, taper_ref, mask_ref, sems = refs[7:]
+    begun_refs = refs[7 : 7 + len(begun)]
+    phase_ref, valid_ref, taper_ref, mask_ref, sems = refs[7 + len(begun) :]
     sta, win = position()
     windows, stations, bins = phase_ref.shape
     rows = stations // blocks
@@ -137,7 +137,13 @@
         store_phasors(w, phase_ref[w], usable, *own)
         return carry
 
-    lax.fori_loop(0, windows, phasors, 0, unroll=4)
+    lax.fori_loop(0, windows, phasors, 0, unroll=12)
+    for targets, begun_ref in zip(begun, begun_refs):
+        block = peer(targets, sta, win == 0)
+        totals = add_full(start_full(rows, stations, bins), block, own)
+        for r in range(rows):
+            for part in range(3):
+                begun_ref[r, part] = totals[r][part]
 
 
 def part_sums(out_ref, block, is_first, groups, weight):
@@ -161,27 +167,39 @@
         out_ref[r] = (totals[r] * weight).astype(jnp.bfloat16)
 
 
-def full_sums(out_ref, block, groups, weight):
+def add_full(totals, block, group):
+    cos_ref, sin_ref, sum_ref, gap_ref = group
+    rows = len(totals)
+
+    def add(w, totals):
+        cosine, plus, gap = cos_ref[w], sum_ref[w], gap_ref[w]
+        added = []
+        for r in range(rows):
+            row = pl.ds(block * rows + r, 1)
+            both, left, right = totals[r]
+            added.append(
+                (
+                    both + sum_ref[w, row, :] * cosine,
+                    left + sin_ref[w, row, :] * gap,
+                    right + cos_ref[w, row, :] * plus,
+                )
+            )
+        return added
+
+    return lax.fori_loop(0, cos_ref.shape[0], add, totals, unroll=6)
+
+
+def start_full(rows, stations, bins):
+    return [(jnp.zeros((stations, bins), jnp.float32),) * 3] * rows
+
+
+def full_sums(out_ref, block, own, other, weight, begun_ref=None):
     _, rows, stations, bins = out_ref.shape
-    totals = [(jnp.zeros((stations, bins), jnp.float32),) * 3] * rows
-    for cos_ref, sin_ref, sum_ref, gap_ref in groups:
-
-        def add(w, totals, cos_ref=cos_ref, sin_ref=sin_ref, sum_ref=sum_ref, gap_ref=gap_ref):
-            cosine, plus, gap = cos_ref[w], sum_ref[w], gap_ref[w]
-            added = []
-            for r in range(rows):
-                row = pl.ds(block * rows + r, 1)
-                both, left, right = totals[r]
-                added.append(
-                    (
-                        both + sum_ref[w, row, :] * cosine,
-                        left + sin_ref[w, row, :] * gap,
-                        right + cos_ref[w, row, :] * plus,
-                    )
-                )
-            return added
-
-        totals = lax.fori_loop(0, cos_ref.shape[0], add, totals, unroll=6)
+    if begun_ref is None:
+        totals = add_full(start_full(rows, stations, bins), block, own)
+    else:
+        totals = [tuple(begun_ref[r, part] for part in range(3)) for r in range(rows)]
+    totals = add_full(totals, block, other)
     for r in range(rows):
         both, left, right = totals[r]
         out_ref[0, r] = ((both - left) * weight).astype(jnp.bfloat16)
@@ -193,73 +211,80 @@
         store_phasors(w, phase_ref[w], usable_ref[w], *other)
         return carry
 
-    lax.fori_loop(0, phase_ref.shape[0], phasors, 0, unroll=4)
-
-
-def cross_kernel(rounds, first, phase_ref, usable_ref, weight_ref, *refs):
-    own, other, outs = refs[:4], refs[4:8], refs[8:]
+    lax.fori_loop(0, phase_ref.shape[0], phasors, 0, unroll=12)
+
+
+def cross_kernel(round_, first, begun, weight_ref, *refs):
+    refs = list(refs)
+    own, other = [refs.pop(0) for _ in range(4)], None
+    begun_ref = refs.pop(0) if begun else None
     if first:
+        phase_ref, usable_ref = refs.pop(0), refs.pop(0)
+        other = [refs.pop(0) for _ in range(4)]
         other_kernel(phase_ref, usable_ref, *other)
     else:
-        outs = outs[1:]
+        other = [refs.pop(0) for _ in range(4)]
+    out_ref = refs[-1]
     sta, win = position()
-    for (whole, targets), out_ref in zip(rounds, outs):
-        block = peer(targets, sta, win == 0)
-        if whole:
-            full_sums(out_ref, block, (own, other), weight_ref[...])
-        else:
-            part_sums(out_ref, block, win == 0, (own, other), weight_ref[...])
+    whole, targets = round_
+    block = peer(targets, sta, win == 0)
+    if whole:
+        full_sums(out_ref, block, own, other, weight_ref[...], begun_ref)
+    else:
+        part_sums(out_ref, block, win == 0, (own, other), weight_ref[...])
 
 
 def table_kernel(blocks, rounds, weight_ref, *refs):
-    own, other, (own_part, part_ref, full_ref, row_cos, row_sin) = refs[:4], refs[4:8], refs[8:]
+    own, other = refs[:4], refs[4:8]
+    own_part, part_ref, full_ref, band_cos, band_sin, row_cos, row_sin = refs[8:]
     sta, win = position()
     bins, columns = part_ref.shape[1:]
     wrap = 2 * blocks * bins
     half = columns // 2
     step = 16
-    column = lax.broadcasted_iota(jnp.int32, (step, columns), 1)
     is_first = win == 0
-    lag = jnp.where(is_first, column - half, jnp.where(column < half, column, column - columns))
+
+    def lags(rows):
+        column = lax.broadcasted_iota(jnp.int32, (rows, columns), 1)
+        return jnp.where(is_first, column - half, jnp.where(column < half, column, column - columns))
 
     def phasor(index):
         wrapped = ((index + wrap // 2) & (wrap - 1)) - wrap // 2
         return cos_sin(wrapped.astype(jnp.float32) * (2.0 * math.pi / wrap))
 
-    fine = lax.broadcasted_iota(jnp.int32, (step, columns), 0)
-    fine_cos, fine_sin = phasor(fine * lag)
+    row = lax.broadcasted_iota(jnp.int32, (step, columns), 0)
+    fine_cos, fine_sin = phasor(row * lags(step))
+    full = [peer(sources(targets), sta, is_first) for whole, targets in rounds if whole]
+    part = [sta] + [peer(sources(targets), sta, is_first) for whole, targets in rounds if not whole]
+    band = lax.broadcasted_iota(jnp.int32, band_cos.shape, 0)
+    first_bin = jnp.zeros(band_cos.shape, jnp.int32)
+    for slot, block in enumerate(full + part):
+        first_bin = jnp.where(band == slot, block * bins, first_bin)
+    band_cos[...], band_sin[...] = phasor(first_bin * lags(band_cos.shape[0]))
     steps = bins // step
-
-    def band_rows(block, store):
-        for start in range(0, steps, step):
-            coarse = block * bins + (start + fine) * step
-            row_cos[...], row_sin[...] = phasor(coarse * lag)
-
-            def fill(a, carry, start=start):
-                left_cos = row_cos[pl.ds(a, 1), :]
-                left_sin = row_sin[pl.ds(a, 1), :]
-                cosine = left_cos * fine_cos - left_sin * fine_sin
-                sine = left_sin * fine_cos + left_cos * fine_sin
-                store(pl.ds(pl.multiple_of((start + a) * step, step), step), cosine, -sine)
+    for start in range(0, steps, step):
+        coarse_cos, coarse_sin = phasor((start + row) * step * lags(step))
+        for slot in range(len(full) + len(part)):
+            left_cos, left_sin = band_cos[slot : slot + 1, :], band_sin[slot : slot + 1, :]
+            row_cos[...] = left_cos * coarse_cos - left_sin * coarse_sin
+            row_sin[...] = -(left_sin * coarse_cos + left_cos * coarse_sin)
+
+            def fill(a, carry, start=start, slot=slot):
+                cosine, minus = row_cos[pl.ds(a, 1), :], row_sin[pl.ds(a, 1), :]
+                place = pl.ds(pl.multiple_of((start + a) * step, step), step)
+                if slot < len(full):
+                    value = cosine * fine_cos + minus * fine_sin
+                    full_ref[slot, 0, place, :] = value.astype(jnp.bfloat16)
+                    value = minus * fine_cos - cosine * fine_sin
+                    full_ref[slot, 1, place, :] = value.astype(jnp.bfloat16)
+                else:
+                    one = jnp.where(is_first, cosine, minus)
+                    two = jnp.where(is_first, minus, -cosine)
+                    value = one * fine_cos + two * fine_sin
+                    part_ref[slot - len(full), place, :] = value.astype(jnp.bfloat16)
                 return carry
 
-            lax.fori_loop(0, min(step, steps - start), fill, 0, unroll=2)
-
-    full = [sources(targets) for whole, targets in rounds if whole]
-    (shared,) = [sources(targets) for whole, targets in rounds if not whole]
-    for slot, targets in enumerate(full):
-
-        def store_full(place, cosine, sine, slot=slot):
-            full_ref[slot, 0, place, :] = cosine.astype(jnp.bfloat16)
-            full_ref[slot, 1, place, :] = sine.astype(jnp.bfloat16)
-
-        band_rows(peer(targets, sta, is_first), store_full)
-    for slot, block in enumerate((sta, peer(shared, sta, is_first))):
-
-        def store_part(place, cosine, sine, slot=slot):
-            part_ref[slot, place, :] = jnp.where(is_first, cosine, sine).astype(jnp.bfloat16)
-
-        band_rows(block, store_part)
+            lax.fori_loop(0, min(step, steps - start), fill, 0, unroll=4)
     part_sums(own_part, sta, is_first, (own, other), weight_ref[...])
 
 
@@ -290,6 +315,16 @@
     for slot, spectra_ref in zip(slots, refs[:-1]):
         total = add_slot(total, spectra_ref, slot, part_ref, full_ref, lags)
     out_ref[...] = total.reshape(rows, stations, half) * keep_ref[...]
+
+
+def final_kernel(mine_ref, theirs_ref, out_hbm, out_ref, sems):
+    copies = []
+    for r in range(out_ref.shape[0]):
+        out_ref[r] = mine_ref[r] + theirs_ref[r]
+        copies.append(pltpu.make_async_copy(out_ref.at[r], out_hbm.at[r], sems.at[r]))
+        copies[-1].start()
+    for copy in copies:
+        copy.wait()
 
 
 def per_device(phases, window_valid, freq_taper, pair_mask):
@@ -321,10 +356,13 @@
     taper = freq_taper
     if bins % 128:
         taper = lax.dynamic_slice_in_dim(freq_taper, lax.axis_index("sta") * bins, bins)
-    *own, usable, weight, keep = kernel(
-        functools.partial(prepare_kernel, blocks),
+    begun = [targets for whole, targets in rounds[:BEGUN] if whole]
+    made = kernel(
+        functools.partial(prepare_kernel, blocks, begun),
         "own_phasors",
-        phasor_set + [((windows, 1, bins), f32), ((1, bins), f32), half_shape],
+        phasor_set
+        + [((windows, 1, bins), f32), ((1, bins), f32), half_shape]
+        + [((rows, 3, stations, bins), f32)] * len(begun),
         [ANY] * 4,
         [
             pltpu.VMEM((windows, stations, bins), bf16),
@@ -334,20 +372,26 @@
             pltpu.SemaphoreType.DMA((4,)),
         ],
     )(*(in_hbm(array) for array in (phases, window_valid, taper.reshape(1, -1), pair_mask)))
+    own, (usable, weight, keep), started = made[:4], made[4:7], list(made[7:])
     axes = ("sta", "win")
-    sent, shapes = [], {True: full_shape, False: part_shape}
-    for first, group in enumerate([[r] for r in rounds] if CHAIN else [rounds]):
-        outs = [shapes[whole] for whole, _ in group]
-        if not first:
-            *other, made = kernel(
-                functools.partial(cross_kernel, group, True), "cross_spectra", phasor_set + outs, [VMEM] * 7
-            )(arriving, usable, weight, *own)
-            sent.append(made)
+    sent, other = [], None
+    for index, round_ in enumerate(rounds):
+        early = round_[0] and index < BEGUN
+        args = [weight, *own] + ([started.pop(0)] if early else [])
+        outs = [full_shape if round_[0] else part_shape]
+        if not index:
+            args += [arriving, usable]
+            outs = phasor_set + outs
         else:
-            (made,) = kernel(
-                functools.partial(cross_kernel, group, False), "cross_spectra", outs, [VMEM] * 12
-            )(arriving, usable, weight, *own, *other, sent[-1])
-            sent.append(made)
+            args += [*other, sent[-1]]
+        *made, payload = kernel(
+            functools.partial(cross_kernel, round_, not index, early),
+            "cross_spectra",
+            outs,
+            [VMEM] * len(args),
+        )(*args)
+        other = other or made
+        sent.append(payload)
     arrived = []
     for spectra, (_, targets) in zip(sent, rounds):
         moves = [(2 * b + w, 2 * targets[w][b] + w) for b in range(blocks) for w in range(2)]
@@ -357,7 +401,8 @@
         "lag_table",
         [part_shape, ((2, bins, LAGS), bf16), ((len(rounds) - 1, 2, bins, LAGS), bf16)],
         [VMEM] * 9,
-        [pltpu.VMEM((16, LAGS), f32)] * 2,
+        [pltpu.VMEM((-(-(len(rounds) + 1) // 8) * 8, LAGS), f32)] * 2
+        + [pltpu.VMEM((16, LAGS), f32)] * 2,
     )(weight, *own, *other)
     slots, slot = [], 0
     for whole, _ in rounds:
@@ -382,7 +427,15 @@
         )(keep, part_table, full_table, early, *arrived[ahead:])[0]
 
     theirs = lax.ppermute(late(1), "win", swap)
-    return late(0) + theirs
+    return pl.pallas_call(
+        final_kernel,
+        out_shape=jax.ShapeDtypeStruct(*half_shape),
+        in_specs=[VMEM] * 2,
+        out_specs=ANY,
+        scratch_shapes=[pltpu.VMEM(*half_shape), pltpu.SemaphoreType.DMA((rows,))],
+        compiler_params=PARAMS,
+        name="correlations",
+    )(late(0), theirs)
 
 
 def solution(mesh):

time: 14.6 us -> 14.2 us (0.973)
  waiting for transfers between devices: 1.09 us -> 2 us
  starting transfers between devices: 8.13 us -> 7.27 us
  other arithmetic: 0.62 us -> 0 us
  Pallas kernels: 4.54 us -> 4.72 us
    ppermute x4, waiting for transfers between devices: 0.42 us -> 1.33 us  [per_device(): arrived.append(lax.ppermute(spectra, axes, moves))]
    ppermute x4, starting transfers between devices: 7.21 us -> 6.38 us  [per_device(): arrived.append(lax.ppermute(spectra, axes, moves))]
    add x1 -> x0, other arithmetic: 0.62 us -> none  [per_device(): return late(0) + theirs]
    pallas_call x5 -> x6, Pallas kernels: 2.23 us -> 2.81 us  [the longest x1 1.37 us: per_device(): kernel(functools.partial(prepare_kernel, blocks, begun), 'own_phasors', p...]
    pallas_call x1, Pallas kernels: 1.49 us -> 1.12 us  [per_device(): kernel(functools.partial(table_kernel, blocks, rounds), 'lag_table', [par...]
  transfers between devices with their start and end apart: 6 -> 6, of which waited for: 2 -> 3; matrix products, arithmetic and copies ran while one was open for 0% -> 0% of each run, Pallas kernels for 27% -> 25%
where the time goes in v4:
time: 14.2 us; the launch traced here: 14.1 us
  starting transfers between devices  7.27 us (51%)
  Pallas kernels  4.72 us (33%)
  waiting for transfers between devices  2 us (14%)
    ppermute x4, starting transfers between devices, per_device(): arrived.append(lax.ppermute(spectra, axes, moves))  6.38 us
    pallas_call x1, Pallas kernels, per_device(): kernel(functools.partial(prepare_kernel, blocks, begun), 'own_phasors', p...  1.37 us
    ppermute x4, waiting for transfers between devices, per_device(): arrived.append(lax.ppermute(spectra, axes, moves))  1.33 us
    pallas_call x1, Pallas kernels, per_device(): kernel(functools.partial(table_kernel, blocks, rounds), 'lag_table', [par...  1.12 us
    pallas_call x4, Pallas kernels, per_device(): kernel(functools.partial(cross_kernel, round_, not index, early), 'cross_...  0.81 us
    ppermute x1, waiting for transfers between devices, per_device(): theirs = lax.ppermute(late(1), 'win', swap)  0.67 us
    pallas_call x1, Pallas kernels, per_device(): pl.pallas_call(final_kernel, out_shape=jax.ShapeDtypeStruct(*half_shape),...  0.63 us
    ppermute x1, starting transfers between devices, per_device(): arriving = lax.ppermute(phases, 'win', swap)  0.45 us
  transfers between devices with their start and end apart: 6, of which 3 were waited for; matrix products, arithmetic and copies ran while one was open for 0% of the time, Pallas kernels for 25%

profile of v4, /device:TPU:0, one launch (start us, length us, event | category | flops | bytes accessed | tf_op | source)
XLA Modules:
  0.0 14.1 jit_solution(174032005957114298)
XLA Ops:
  0.0 0.5 %collective-permute-start = (bf16[12,16,256]{2,1,0:T(8,128)(2,1)}, bf16[12,16,256]{2,1,0:T(8,128)(2,1)S(1)}, u32[]{:S(2)}, u32[]{:S(2)}) collective-permute-start(bf16[12,16,256]{2,1,0:T(8,128)(2,1)} %bitcast.2), channel_id=1, source_target_pairs={{0,1},{1,0},{2,3},{3,2},{4,5},{5,4},{6,7},{7,6},{8,9},{9,8},{10,11... | collective-permute-start | bytes 294920 | tf_op jit(solution)/shard_map/ppermute | solution.py:355
  0.5 1.4 %own_phasors.1 = (f32[12,16,256]{2,1,0:T(8,128)S(1)}, f32[12,16,256]{2,1,0:T(8,128)S(1)}, f32[12,16,256]{2,1,0:T(8,128)S(1)}, f32[12,16,256]{2,1,0:T(8,128)S(1)}...) custom-call(bf16[12,16,256]{2,1,0:T(8,128)(2,1)} %bitcast.3, ...), custom_call_target="tpu_custom_call" | custom-call | tf_op jit(solution)/shard_map/own_phasors/pallas_call | solution.py:360
  1.8 0.0 collective-permute-done.refs_5_
  1.8 0.3 %cross_spectra.4 = (f32[12,16,256]{2,1,0:T(8,128)S(1)}, f32[12,16,256]{2,1,0:T(8,128)S(1)}, f32[12,16,256]{2,1,0:T(8,128)S(1)}, f32[12,16,256]{2,1,0:T(8,128)S(1)}, bf16[2,2,16,256]{3,2,1,0:T(8,128)(2,1)S(1)}) custom-call(f32[1,256]{1,0:T(1,128)S(1)} %get-tuple-element.23.weight_ref, f32[12,16,256]{2,1,0:T(8,128)S(1)} %get-tuple-element.24.refs_0_, ...), custom_call_target="tpu_custom_call" | custom-call | tf_op jit(solution)/shard_map/cross_spectra/pallas_call | solution.py:387
  2.2 3.7 %collective-permute-start.1 = (bf16[2,2,16,256]{3,2,1,0:T(8,128)(2,1)S(1)}, bf16[2,2,16,256]{3,2,1,0:T(8,128)(2,1)S(1)}, u32[]{:S(2)}, u32[]{:S(2)}) collective-permute-start(bf16[2,2,16,256]{3,2,1,0:T(8,128)(2,1)S(1)} %get-tuple-element.37.refs_9_), channel_id=1, source_target_pairs={{0,6},{1,11},{2,10},{3,15},{4,2},{5,9},{6,14},{7,13},{8,4},{9,3},{... | collective-permute-start | bytes 98312 | tf_op jit(solution)/shard_map/ppermute | solution.py:398
  5.9 0.1 cross_spectra.5.refs_8_
  6.0 0.6 %collective-permute-start.2 = (bf16[2,2,16,256]{3,2,1,0:T(8,128)(2,1)S(1)}, bf16[2,2,16,256]{3,2,1,0:T(8,128)(2,1)S(1)}, u32[]{:S(2)}, u32[]{:S(2)}) collective-permute-start(bf16[2,2,16,256]{3,2,1,0:T(8,128)(2,1)S(1)} %cross_spectra.5.refs_8_), channel_id=1, source_target_pairs={{0,8},{1,13},{2,4},{3,9},{4,12},{5,15},{6,0},{7,3},{8,14},{9,7},{1... | collective-permute-start | bytes 98312 | tf_op jit(solution)/shard_map/ppermute | solution.py:398
  6.6 0.2 %cross_spectra.6.refs_8_ = bf16[2,2,16,256]{3,2,1,0:T(8,128)(2,1)S(1)} custom-call(f32[1,256]{1,0:T(1,128)S(1)} %get-tuple-element.23.weight_ref, f32[12,16,256]{2,1,0:T(8,128)S(1)} %get-tuple-element.24.refs_0_, f32[12,16,256]{2,1,0:T(8,128)S(1)} %get-tuple-element.25.refs_1_, f32[12,16,256]{2,1,0:T(8,128)S(1)} %get-tuple-element.26.refs_2_, ...), custom_call_target="tpu_custom_call" | custom-call | tf_op jit(solution)/shard_map/cross_spectra/pallas_call | solution.py:387
  6.8 1.2 %collective-permute-start.3 = (bf16[2,2,16,256]{3,2,1,0:T(8,128)(2,1)S(1)}, bf16[2,2,16,256]{3,2,1,0:T(8,128)(2,1)S(1)}, u32[]{:S(2)}, u32[]{:S(2)}) collective-permute-start(bf16[2,2,16,256]{3,2,1,0:T(8,128)(2,1)S(1)} %cross_spectra.6.refs_8_), channel_id=1, source_target_pairs={{0,4},{1,15},{2,0},{3,13},{4,6},{5,11},{6,10},{7,9},{8,12},{9,1},{... | collective-permute-start | bytes 98312 | tf_op jit(solution)/shard_map/ppermute | solution.py:398
  8.0 0.2 %cross_spectra.7 = bf16[2,16,256]{2,1,0:T(8,128)(2,1)S(1)} custom-call(f32[1,256]{1,0:T(1,128)S(1)} %get-tuple-element.23.weight_ref, f32[12,16,256]{2,1,0:T(8,128)S(1)} %get-tuple-element.24.refs_0_, f32[12,16,256]{2,1,0:T(8,128)S(1)} %get-tuple-element.25.refs_1_, f32[12,16,256]{2,1,0:T(8,128)S(1)} %get-tuple-element.26.refs_2_, ...), custom_call_target="tpu_custom_call" | custom-call | tf_op jit(solution)/shard_map/cross_spectra/pallas_call | solution.py:387
  8.1 0.9 %collective-permute-start.4 = (bf16[2,16,256]{2,1,0:T(8,128)(2,1)S(1)}, bf16[2,16,256]{2,1,0:T(8,128)(2,1)S(1)}, u32[]{:S(2)}, u32[]{:S(2)}) collective-permute-start(bf16[2,16,256]{2,1,0:T(8,128)(2,1)S(1)} %cross_spectra.7), channel_id=1, source_target_pairs={{0,2},{1,3},{2,6},{3,7},{4,0},{5,1},{6,4},{7,5},{8,10},{9,11},{10,... | collective-permute-start | bytes 49160 | tf_op jit(solution)/shard_map/ppermute | solution.py:398
  9.1 1.1 %lag_table.1 = (bf16[2,16,256]{2,1,0:T(8,128)(2,1)S(1)}, bf16[2,256,512]{2,1,0:T(8,128)(2,1)S(1)}, bf16[3,2,256,512]{3,2,1,0:T(8,128)(2,1)S(1)}) custom-call(f32[1,256]{1,0:T(1,128)S(1)} %get-tuple-element.23.weight_ref, f32[12,16,256]{2,1,0:T(8,128)S(1)} %get-tuple-element.24.refs_0_, f32[12,16,256]{2,1,0:T(8,128)S(1)} %get-tuple-element.25.refs_1_, ...), custom_call_target="tpu_custom_call" | custom-call | tf_op jit(solution)/shard_map/lag_table/pallas_call | solution.py:399
  10.2 0.0 collective-permute-done.1.spectra_ref
  10.2 0.2 %lag_sums_early.2.before_ref = f32[32,512]{1,0:T(8,128)S(1)} custom-call(bf16[2,256,512]{2,1,0:T(8,128)(2,1)S(1)} %get-tuple-element.34.part_ref, bf16[3,2,256,512]{3,2,1,0:T(8,128)(2,1)S(1)} %get-tuple-element.35.full_ref, bf16[2,16,256]{2,1,0:T(8,128)(2,1)S(1)} %get-tuple-element.36.before_ref, bf16[2,2,16,256]{3,2,1,0:T(8,128)(2,1)S(1)} %collective-permute-done.1.spectra_ref), custom_call_target="tpu_custom_call" | custom-call | tf_op jit(solution)/shard_map/lag_sums_early/pallas_call | solution.py:414
  10.4 0.5 %collective-permute-done.2.spectra_ref = bf16[2,2,16,256]{3,2,1,0:T(8,128)(2,1)S(1)} collective-permute-done((bf16[2,2,16,256]{3,2,1,0:T(8,128)(2,1)S(1)}, bf16[2,2,16,256]{3,2,1,0:T(8,128)(2,1)S(1)}, u32[]{:S(2)}, u32[]{:S(2)}) %collective-permute-start.2) | collective-permute-done | bytes 32800 | tf_op jit(solution)/shard_map/ppermute | solution.py:398
  10.9 0.2 %lag_sums_early.3.early_ref = f32[32,512]{1,0:T(8,128)S(1)} custom-call(bf16[2,256,512]{2,1,0:T(8,128)(2,1)S(1)} %get-tuple-element.34.part_ref, bf16[3,2,256,512]{3,2,1,0:T(8,128)(2,1)S(1)} %get-tuple-element.35.full_ref, f32[32,512]{1,0:T(8,128)S(1)} %lag_sums_early.2.before_ref, bf16[2,2,16,256]{3,2,1,0:T(8,128)(2,1)S(1)} %collective-permute-done.2.spectra_ref), custom_call_target="tpu_custom_call" | custom-call | tf_op jit(solution)/shard_map/lag_sums_early/pallas_call | solution.py:414
  11.1 0.8 %collective-permute-done.4.refs_1_ = bf16[2,16,256]{2,1,0:T(8,128)(2,1)S(1)} collective-permute-done((bf16[2,16,256]{2,1,0:T(8,128)(2,1)S(1)}, bf16[2,16,256]{2,1,0:T(8,128)(2,1)S(1)}, u32[]{:S(2)}, u32[]{:S(2)}) %collective-permute-start.4) | collective-permute-done | bytes 16416 | tf_op jit(solution)/shard_map/ppermute | solution.py:398
  11.9 0.0 collective-permute-done.3.refs_0_
  11.9 0.2 %lag_sums_late.3 = f32[2,16,256]{2,1,0:T(8,128)S(1)} custom-call(f32[2,16,256]{2,1,0:T(8,128)S(1)} %get-tuple-element.22.keep_ref, bf16[2,256,512]{2,1,0:T(8,128)(2,1)S(1)} %get-tuple-element.34.part_ref, bf16[3,2,256,512]{3,2,1,0:T(8,128)(2,1)S(1)} %get-tuple-element.35.full_ref, f32[32,512]{1,0:T(8,128)S(1)} %lag_sums_early.3.early_ref, ...), custom_call_target="tpu_custom_call" | custom-call | tf_op jit(solution)/shard_map/lag_sums_late/pallas_call | solution.py:422
  12.1 0.4 %collective-permute-start.5 = (f32[2,16,256]{2,1,0:T(8,128)S(1)}, f32[2,16,256]{2,1,0:T(8,128)S(1)}, u32[]{:S(2)}, u32[]{:S(2)}) collective-permute-start(f32[2,16,256]{2,1,0:T(8,128)S(1)} %lag_sums_late.3), channel_id=1, source_target_pairs={{0,1},{1,0},{2,3},{3,2},{4,5},{5,4},{6,7},{7,6},{8,9},{9,8},{10,11... | collective-permute-start | bytes 98312 | tf_op jit(solution)/shard_map/ppermute | solution.py:429
  12.6 0.2 %lag_sums_late.2.mine_ref = f32[2,16,256]{2,1,0:T(8,128)S(1)} custom-call(f32[2,16,256]{2,1,0:T(8,128)S(1)} %get-tuple-element.22.keep_ref, bf16[2,256,512]{2,1,0:T(8,128)(2,1)S(1)} %get-tuple-element.34.part_ref, bf16[3,2,256,512]{3,2,1,0:T(8,128)(2,1)S(1)} %get-tuple-element.35.full_ref, f32[32,512]{1,0:T(8,128)S(1)} %lag_sums_early.3.early_ref, ...), custom_call_target="tpu_custom_call" | custom-call | tf_op jit(solution)/shard_map/lag_sums_late/pallas_call | solution.py:422
  12.7 0.7 %collective-permute-done.5.theirs_ref = f32[2,16,256]{2,1,0:T(8,128)S(1)} collective-permute-done((f32[2,16,256]{2,1,0:T(8,128)S(1)}, f32[2,16,256]{2,1,0:T(8,128)S(1)}, u32[]{:S(2)}, u32[]{:S(2)}) %collective-permute-start.5) | collective-permute-done | bytes 32800 | tf_op jit(solution)/shard_map/ppermute | solution.py:429
  13.4 0.6 %correlations.1 = f32[2,16,256]{2,1,0:T(8,128)} custom-call(f32[2,16,256]{2,1,0:T(8,128)S(1)} %lag_sums_late.2.mine_ref, f32[2,16,256]{2,1,0:T(8,128)S(1)} %collective-permute-done.5.theirs_ref), custom_call_target="tpu_custom_call" | custom-call | tf_op jit(solution)/shard_map/correlations/pallas_call | solution.py:430
Async XLA Ops:
  0.0 1.8 %collective-permute-start = (bf16[12,16,256]{2,1,0:T(8,128)(2,1)}, bf16[12,16,256]{2,1,0:T(8,128)(2,1)S(1)}, u32[]{:S(2)}, u32[]{:S(2)}) collective-permute-start(bf16[12,16,256]{2,1,0:T(8,128)(2,1)} %bitcast.2), channel_id=1, source_target_pairs={{0,1},{1,0},{2,3},{3,2},{4,5},{5,4},{6,7},{7,6},{8,9},{9,8},{10,11... | collective-permute-start | bytes 294920 | tf_op jit(solution)/shard_map/ppermute | solution.py:355
  2.2 8.0 %collective-permute-start.1 = (bf16[2,2,16,256]{3,2,1,0:T(8,128)(2,1)S(1)}, bf16[2,2,16,256]{3,2,1,0:T(8,128)(2,1)S(1)}, u32[]{:S(2)}, u32[]{:S(2)}) collective-permute-start(bf16[2,2,16,256]{3,2,1,0:T(8,128)(2,1)S(1)} %get-tuple-element.37.refs_9_), channel_id=1, source_target_pairs={{0,6},{1,11},{2,10},{3,15},{4,2},{5,9},{6,14},{7,13},{8,4},{9,3},{... | collective-permute-start | bytes 98312 | tf_op jit(solution)/shard_map/ppermute | solution.py:398
  6.0 5.0 %collective-permute-start.2 = (bf16[2,2,16,256]{3,2,1,0:T(8,128)(2,1)S(1)}, bf16[2,2,16,256]{3,2,1,0:T(8,128)(2,1)S(1)}, u32[]{:S(2)}, u32[]{:S(2)}) collective-permute-start(bf16[2,2,16,256]{3,2,1,0:T(8,128)(2,1)S(1)} %cross_spectra.5.refs_8_), channel_id=1, source_target_pairs={{0,8},{1,13},{2,4},{3,9},{4,12},{5,15},{6,0},{7,3},{8,14},{9,7},{1... | collective-permute-start | bytes 98312 | tf_op jit(solution)/shard_map/ppermute | solution.py:398
  6.8 5.2 %collective-permute-start.3 = (bf16[2,2,16,256]{3,2,1,0:T(8,128)(2,1)S(1)}, bf16[2,2,16,256]{3,2,1,0:T(8,128)(2,1)S(1)}, u32[]{:S(2)}, u32[]{:S(2)}) collective-permute-start(bf16[2,2,16,256]{3,2,1,0:T(8,128)(2,1)S(1)} %cross_spectra.6.refs_8_), channel_id=1, source_target_pairs={{0,4},{1,15},{2,0},{3,13},{4,6},{5,11},{6,10},{7,9},{8,12},{9,1},{... | collective-permute-start | bytes 98312 | tf_op jit(solution)/shard_map/ppermute | solution.py:398
  8.1 3.8 %collective-permute-start.4 = (bf16[2,16,256]{2,1,0:T(8,128)(2,1)S(1)}, bf16[2,16,256]{2,1,0:T(8,128)(2,1)S(1)}, u32[]{:S(2)}, u32[]{:S(2)}) collective-permute-start(bf16[2,16,256]{2,1,0:T(8,128)(2,1)S(1)} %cross_spectra.7), channel_id=1, source_target_pairs={{0,2},{1,3},{2,6},{3,7},{4,0},{5,1},{6,4},{7,5},{8,10},{9,11},{10,... | collective-permute-start | bytes 49160 | tf_op jit(solution)/shard_map/ppermute | solution.py:398
  12.1 1.3 %collective-permute-start.5 = (f32[2,16,256]{2,1,0:T(8,128)S(1)}, f32[2,16,256]{2,1,0:T(8,128)S(1)}, u32[]{:S(2)}, u32[]{:S(2)}) collective-permute-start(f32[2,16,256]{2,1,0:T(8,128)S(1)} %lag_sums_late.3), channel_id=1, source_target_pairs={{0,1},{1,0},{2,3},{3,2},{4,5},{5,4},{6,7},{7,6},{8,9},{9,8},{10,11... | collective-permute-start | bytes 98312 | tf_op jit(solution)/shard_map/ppermute | solution.py:429

commit v5 on v4

v5 whole, which is shorter than its diff:
```python
import functools
import math

import jax
import jax.numpy as jnp
from jax import lax
from jax.experimental import pallas as pl
from jax.experimental.pallas import tpu as pltpu
from jax.sharding import PartitionSpec as P

LAGS = 512
BEGUN = 2
SMALL = 1000
ROUNDS = (
    ((3, 2, 6, 7, 5, 1, 0, 4), (4, 7, 1, 5, 3, 6, 2, 0)),
    ((6, 5, 7, 4, 0, 2, 1, 3), (7, 4, 5, 6, 1, 0, 3, 2)),
    ((1, 0, 4, 2, 7, 3, 5, 6), (5, 6, 3, 0, 2, 7, 4, 1)),
    ((2, 3, 0, 1, 6, 4, 7, 5), (2, 3, 0, 1, 6, 4, 7, 5)),
)
VMEM = pl.BlockSpec(memory_space=pltpu.VMEM)
ANY = pl.BlockSpec(memory_space=pl.ANY)
PARAMS = pltpu.CompilerParams(vmem_limit_bytes=48 * 1024 * 1024)

COS_COEF = (
    0.9999999890590218,
    -0.49999989101070386,
    0.041666489217381156,
    -0.001388780359807859,
    2.476988355752502e-05,
    -2.707903082088142e-07,
    1.724509174527214e-09,
)
SIN_COEF = (
    0.9999997571451633,
    -0.06534424613196173,
    0.001711441007161203,
    -2.461450561671638e-05,
    1.977699154629728e-07,
)


def cos_sin(angle):
    square = angle * angle
    cosine = COS_COEF[-1]
    for coef in COS_COEF[-2::-1]:
        cosine = cosine * square + coef
    sine = SIN_COEF[-1]
    for coef in SIN_COEF[-2::-1]:
        sine = sine * square + coef
    sine = sine * (angle - angle * square * (1.0 / math.pi**2))
    return cosine, sine


def rounds_of(blocks):
    if blocks == len(ROUNDS[0][0]):
        return ROUNDS
    steps = [(step, step ^ 1) for step in range(2, blocks, 2)] + [(1, 1)]
    return tuple(tuple(tuple(b ^ step for b in range(blocks)) for step in pair) for pair in steps)


def lookup(values, sta):
    found = jnp.int32(values[0])
    for b, value in enumerate(values[1:], 1):
        found = jnp.where(sta == b, value, found)
    return found


def peer(targets, sta, is_first):
    return jnp.where(is_first, lookup(targets[0], sta), lookup(targets[1], sta))


def sources(targets):
    return tuple(tuple(sorted(range(len(side)), key=lambda b: side[b])) for side in targets)


def in_hbm(array):
    return pltpu.with_memory_space_constraint(array, pltpu.HBM)


def position():
    return lax.axis_index("sta"), lax.axis_index("win")


def store_phasors(w, phase, usable, cos_ref, sin_ref, sum_ref, gap_ref):
    cosine, sine = cos_sin(phase.astype(jnp.float32))
    cosine = cosine.astype(jnp.bfloat16).astype(jnp.float32) * usable
    sine = sine.astype(jnp.bfloat16).astype(jnp.float32) * usable
    cos_ref[w] = cosine
    sin_ref[w] = sine
    sum_ref[w] = cosine + sine
    gap_ref[w] = cosine - sine


def prepare_kernel(blocks, begun, phase_hbm, valid_hbm, taper_hbm, mask_hbm, *refs):
    own, (usable_ref, weight_ref, keep_ref) = refs[:4], refs[4:7]
    begun_refs = refs[7 : 7 + len(begun)]
    phase_ref, valid_ref, taper_ref, mask_ref, sems = refs[7 + len(begun) :]
    sta, win = position()
    windows, stations, bins = phase_ref.shape
    rows = stations // blocks
    if taper_hbm.shape[1] > bins:
        taper_hbm = taper_hbm.at[:, pl.ds(pl.multiple_of(sta * bins, 128), bins)]
    copies = [
        pltpu.make_async_copy(source, target, sems.at[c])
        for c, (source, target) in enumerate(
            (
                (phase_hbm, phase_ref),
                (valid_hbm, valid_ref),
                (taper_hbm, taper_ref),
                (mask_hbm, mask_ref),
            )
        )
    ]
    for copy in copies:
        copy.start()
    for copy in copies[1:]:
        copy.wait()
    count = jnp.float32(0)
    for w in range(2 * windows):
        count += valid_ref[w].astype(jnp.float32)
    total = jnp.maximum(jnp.full((1, bins), count, jnp.float32), 1.0)
    weight_ref[...] = taper_ref[...] * (1.0 / jnp.sqrt(blocks * bins * total))
    for w in range(windows):
        usable = valid_ref[(1 - win) * windows + w].astype(jnp.float32)
        usable_ref[w] = jnp.full((1, bins), usable, jnp.float32)
    source = lax.broadcasted_iota(jnp.int32, keep_ref.shape[1:], 0)
    kept = jnp.zeros(keep_ref.shape[1:], jnp.float32)
    for block in range(blocks):
        kept = jnp.where(source // rows == block, mask_ref[sta, block].astype(jnp.float32), kept)
    for r in range(rows):
        keep_ref[r] = jnp.where(source == sta * rows + r, 0.0, kept)
    copies[0].wait()

    def phasors(w, carry):
        usable = valid_ref[win * windows + w].astype(jnp.float32)
        store_phasors(w, phase_ref[w], usable, *own)
        return carry

    lax.fori_loop(0, windows, phasors, 0, unroll=4)
    for targets, begun_ref in zip(begun, begun_refs):
        block = peer(targets, sta, win == 0)
        totals = add_full(start_full(rows, stations, bins), block, own)
        for r in range(rows):
            for part in range(3):
                begun_ref[r, part] = totals[r][part]


def add_full(totals, block, group):
    cos_ref, sin_ref, sum_ref, gap_ref = group
    rows = len(totals)

    def add(w, totals):
        cosine, plus, gap = cos_ref[w], sum_ref[w], gap_ref[w]
        added = []
        for r in range(rows):
            row = pl.ds(block * rows + r, 1)
            both, left, right = totals[r]
            added.append(
                (
                    both + sum_ref[w, row, :] * cosine,
                    left + sin_ref[w, row, :] * gap,
                    right + cos_ref[w, row, :] * plus,
                )
            )
        return added

    return lax.fori_loop(0, cos_ref.shape[0], add, totals, unroll=6)


def start_full(rows, stations, bins):
    return [(jnp.zeros((stations, bins), jnp.float32),) * 3] * rows


def full_sums(out_ref, block, own, other, weight, begun_ref=None):
    _, rows, stations, bins = out_ref.shape
    if begun_ref is None:
        totals = add_full(start_full(rows, stations, bins), block, own)
    else:
        totals = [tuple(begun_ref[r, part] for part in range(3)) for r in range(rows)]
    totals = add_full(totals, block, other)
    for r in range(rows):
        both, left, right = totals[r]
        out_ref[0, r] = ((both - left) * weight).astype(jnp.bfloat16).astype(out_ref.dtype)
        out_ref[1, r] = ((both - right) * weight).astype(jnp.bfloat16).astype(out_ref.dtype)


def other_kernel(phase_ref, usable_ref, *other):
    def phasors(w, carry):
        store_phasors(w, phase_ref[w], usable_ref[w], *other)
        return carry

    lax.fori_loop(0, phase_ref.shape[0], phasors, 0, unroll=12)


def cross_kernel(targets, first, begun, weight_ref, *refs):
    refs = list(refs)
    own, other = [refs.pop(0) for _ in range(4)], None
    begun_ref = refs.pop(0) if begun else None
    if first:
        phase_ref, usable_ref = refs.pop(0), refs.pop(0)
        other = [refs.pop(0) for _ in range(4)]
        other_kernel(phase_ref, usable_ref, *other)
    else:
        other = [refs.pop(0) for _ in range(4)]
    out_ref = refs[-1]
    sta, win = position()
    block = peer(targets, sta, win == 0)
    full_sums(out_ref, block, own, other, weight_ref[...], begun_ref)


def fill_tables(blocks, bands, table_ref, band_cos, band_sin, row_cos, row_sin):
    _, win = position()
    bins, columns = table_ref.shape[2:]
    wrap = 2 * blocks * bins
    half = LAGS // 2
    step = 16
    is_first = win == 0

    def lags(rows):
        column = lax.broadcasted_iota(jnp.int32, (rows, columns), 1)
        return jnp.where(is_first, column - half, jnp.where(column < half, column, column - LAGS))

    def phasor(index):
        wrapped = ((index + wrap // 2) & (wrap - 1)) - wrap // 2
        return cos_sin(wrapped.astype(jnp.float32) * (2.0 * math.pi / wrap))

    row = lax.broadcasted_iota(jnp.int32, (step, columns), 0)
    fine_cos, fine_sin = phasor(row * lags(step))
    band = lax.broadcasted_iota(jnp.int32, band_cos.shape, 0)
    first_bin = jnp.zeros(band_cos.shape, jnp.int32)
    for slot, block in enumerate(bands):
        first_bin = jnp.where(band == slot, block * bins, first_bin)
    band_cos[...], band_sin[...] = phasor(first_bin * lags(band_cos.shape[0]))
    steps = bins // step
    for start in range(0, steps, step):
        coarse_cos, coarse_sin = phasor((start + row) * step * lags(step))
        for slot in range(len(bands)):
            left_cos, left_sin = band_cos[slot : slot + 1, :], band_sin[slot : slot + 1, :]
            row_cos[...] = left_cos * coarse_cos - left_sin * coarse_sin
            row_sin[...] = -(left_sin * coarse_cos + left_cos * coarse_sin)

            def fill(a, carry, start=start, slot=slot):
                cosine, minus = row_cos[pl.ds(a, 1), :], row_sin[pl.ds(a, 1), :]
                place = pl.ds(pl.multiple_of((start + a) * step, step), step)
                value = cosine * fine_cos + minus * fine_sin
                table_ref[slot, 0, place, :] = value.astype(jnp.bfloat16)
                value = minus * fine_cos - cosine * fine_sin
                table_ref[slot, 1, place, :] = value.astype(jnp.bfloat16)
                return carry

            lax.fori_loop(0, min(step, steps - start), fill, 0, unroll=4)


def split_table_kernel(blocks, rounds, after_ref, table_ref, *scratch):
    sta, win = position()
    bands = [peer(sources(targets), sta, win == 0) for targets in rounds[:-1]]
    fill_tables(blocks, bands, table_ref, *scratch)


def whole_table_kernel(blocks, rounds, weight_ref, *refs):
    own, other, (after_ref, own_ref, table_ref, *scratch) = refs[:4], refs[4:8], refs[8:]
    sta, win = position()
    bands = [peer(sources(rounds[-1]), sta, win == 0), sta]
    fill_tables(blocks, bands, table_ref, *scratch)
    full_sums(own_ref, sta, own, other, weight_ref[...])


def times(spectra_ref, table_ref):
    _, rows, stations, bins = spectra_ref.shape
    total = 0.0
    for c in range(2):
        spectra = spectra_ref[c].reshape(rows * stations, bins).astype(jnp.bfloat16)
        total = total + jnp.dot(spectra, table_ref[c], preferred_element_type=jnp.float32)
    return total


def split_kernel(slot, end, table_ref, *refs):
    outs = 2 if end else 1
    spectra_ref, *before = refs[:-outs]
    total = times(spectra_ref, table_ref.at[slot])
    for before_ref in before:
        total = total + before_ref[...]
    if end:
        mine_ref, theirs_ref = refs[-2:]
        half = mine_ref.shape[-1]
        mine_ref[...], theirs_ref[...] = total[:, :half], total[:, half:].astype(theirs_ref.dtype)
    else:
        refs[-1][...] = total


def whole_kernel(slot, table_ref, spectra_ref, before_ref, out_ref):
    out_ref[...] = before_ref[...] + times(spectra_ref, table_ref.at[slot])


def final_kernel(keep_ref, mine_ref, theirs_ref, out_hbm, out_ref, sems):
    rows, stations, half = out_ref.shape
    copies = []
    for r in range(rows):
        row = pl.ds(r * stations, stations)
        out_ref[r] = (mine_ref[row] + theirs_ref[row].astype(jnp.float32)) * keep_ref[r]
        copies.append(pltpu.make_async_copy(out_ref.at[r], out_hbm.at[r], sems.at[r]))
        copies[-1].start()
    for copy in copies:
        copy.wait()


def per_device(phases, window_valid, freq_taper, pair_mask):
    blocks = lax.axis_size("sta")
    windows, bins, stations = phases.shape
    rows = stations // blocks
    half = LAGS // 2
    rounds = rounds_of(blocks)
    swap = [(0, 1), (1, 0)]

    def kernel(body, name, outs, ins, scratch=(), flops=None):
        return pl.pallas_call(
            body,
            out_shape=[jax.ShapeDtypeStruct(shape, dtype) for shape, dtype in outs],
            in_specs=ins,
            out_specs=[VMEM] * len(outs),
            scratch_shapes=list(scratch),
            compiler_params=PARAMS,
            cost_estimate=flops and pl.CostEstimate(flops=flops, bytes_accessed=1000, transcendentals=0),
            name=name,
        )

    f32, bf16 = jnp.float32, jnp.bfloat16
    phasor_set = [((windows, stations, bins), f32)] * 4
    full_shape = ((2, rows, stations, bins), bf16)
    half_shape = ((rows, stations, half), f32)
    phases = jnp.transpose(phases, (0, 2, 1))
    arriving = lax.ppermute(phases, "win", swap)
    taper = freq_taper
    if bins % 128:
        taper = lax.dynamic_slice_in_dim(freq_taper, lax.axis_index("sta") * bins, bins)
    begun = rounds[:BEGUN]
    made = kernel(
        functools.partial(prepare_kernel, blocks, begun),
        "own_phasors",
        phasor_set
        + [((windows, 1, bins), f32), ((1, bins), f32), half_shape]
        + [((rows, 3, stations, bins), f32)] * len(begun),
        [ANY] * 4,
        [
            pltpu.VMEM((windows, stations, bins), bf16),
            pltpu.SMEM(window_valid.shape, jnp.int32),
            pltpu.VMEM((1, bins), f32),
            pltpu.SMEM(pair_mask.shape, jnp.int32),
            pltpu.SemaphoreType.DMA((4,)),
        ],
    )(*(in_hbm(array) for array in (phases, window_valid, taper.reshape(1, -1), pair_mask)))
    own, (usable, weight, keep), started = made[:4], made[4:7], made[7:]
    axes = ("sta", "win")
    sent, other = [], None
    for index, targets in enumerate(rounds):
        args = [weight, *own, *started[index : index + 1]]
        args += [*other, sent[-1]] if index else [arriving, usable]
        *made, payload = kernel(
            functools.partial(cross_kernel, targets, not index, index < len(begun)),
            "cross_spectra",
            ([] if index else phasor_set) + [full_shape],
            [VMEM] * len(args),
        )(*args)
        other = other or made
        sent.append(payload)
    arrived = []
    for spectra, targets in zip(sent, rounds):
        moves = [(2 * b + w, 2 * targets[w][b] + w) for b in range(blocks) for w in range(2)]
        arrived.append(lax.ppermute(spectra, axes, moves))
    split = len(rounds) - 1
    def scratch(slots, lags):
        return [pltpu.VMEM((-(-slots // 8) * 8, lags), f32)] * 2 + [pltpu.VMEM((16, lags), f32)] * 2

    (split_table,) = kernel(
        functools.partial(split_table_kernel, blocks, rounds),
        "split_lag_table",
        [((split, 2, bins, LAGS), bf16)],
        [VMEM],
        scratch(split, LAGS),
    )(sent[-1])
    pairs, sums = rows * stations, []
    for slot in range(split):
        end = slot == split - 1
        sums = kernel(
            functools.partial(split_kernel, slot, end),
            "split_lag_sums",
            [((pairs, half), f32)] * 2 if end else [((pairs, LAGS), f32)],
            [VMEM] * (2 + len(sums)),
            flops=SMALL,
        )(split_table, arrived[slot], *sums)
    mine, theirs = sums
    theirs = lax.ppermute(theirs, "win", swap)
    own_spectra, whole_table = kernel(
        functools.partial(whole_table_kernel, blocks, rounds),
        "whole_lag_table",
        [full_shape, ((2, 2, bins, half), bf16)],
        [VMEM] * 10,
        scratch(2, half),
    )(weight, *own, *other, mine)
    for slot, spectra in ((1, own_spectra), (0, arrived[-1])):
        (mine,) = kernel(
            functools.partial(whole_kernel, slot),
            "whole_lag_sums",
            [((pairs, half), f32)],
            [VMEM] * 3,
            flops=SMALL,
        )(whole_table, spectra, mine)
    return pl.pallas_call(
        final_kernel,
        out_shape=jax.ShapeDtypeStruct(*half_shape),
        in_specs=[VMEM] * 3,
        out_specs=ANY,
        scratch_shapes=[pltpu.VMEM(*half_shape), pltpu.SemaphoreType.DMA((rows,))],
        compiler_params=PARAMS,
        name="correlations",
    )(keep, mine, theirs)


def solution(mesh):
    return jax.shard_map(
        per_device,
        mesh=mesh,
        in_specs=(P(("days", "win"), "sta", None), P("days"), P(), P()),
        out_specs=P(("days", "sta"), None, "win"),
        check_vma=False,
    )
```

time: 14.2 us -> 14 us (0.986)
  waiting for transfers between devices: 2 us -> 0.53 us
  starting transfers between devices: 7.27 us -> 8.41 us
    ppermute x4, starting transfers between devices: 6.38 us -> 7.31 us  [per_device(): arrived.append(lax.ppermute(spectra, axes, moves))]
    ppermute x4, waiting for transfers between devices: 1.33 us -> 0.42 us  [per_device(): arrived.append(lax.ppermute(spectra, axes, moves))]
    ppermute x1, waiting for transfers between devices: 0.67 us -> 0.1 us  [per_device(): theirs = lax.ppermute(theirs, 'win', swap)]
    ppermute x1, starting transfers between devices: 0.43 us -> 0.65 us  [per_device(): theirs = lax.ppermute(theirs, 'win', swap)]
    pallas_call x9 -> x11, Pallas kernels: 2.72 us -> 2.78 us  [the longest x4 0.83 us: per_device(): kernel(functools.partial(cross_kernel, targets, not index, index < len(be...]
  transfers between devices with their start and end apart: 6 -> 6, of which waited for: 3 -> 3; matrix products, arithmetic and copies ran while one was open for 0% -> 0% of each run, Pallas kernels for 25% -> 28%
where the time goes in v5:
time: 14 us; the launch traced here: 13.8 us
  starting transfers between devices  8.41 us (60%)
  Pallas kernels  4.81 us (34%)
  waiting for transfers between devices  0.53 us (4%)
    ppermute x4, starting transfers between devices, per_device(): arrived.append(lax.ppermute(spectra, axes, moves))  7.31 us
    pallas_call x1, Pallas kernels, per_device(): kernel(functools.partial(prepare_kernel, blocks, begun), 'own_phasors', p...  1.4 us
    pallas_call x4, Pallas kernels, per_device(): kernel(functools.partial(cross_kernel, targets, not index, index < len(be...  0.83 us
    pallas_call x1, Pallas kernels, per_device(): kernel(functools.partial(split_table_kernel, blocks, rounds), 'split_lag_...  0.67 us
    ppermute x1, starting transfers between devices, per_device(): theirs = lax.ppermute(theirs, 'win', swap)  0.65 us
    pallas_call x1, Pallas kernels, per_device(): pl.pallas_call(final_kernel, out_shape=jax.ShapeDtypeStruct(*half_shape),...  0.63 us
    pallas_call x3, Pallas kernels, per_device(): kernel(functools.partial(split_kernel, slot, end), 'split_lag_sums', [((p...  0.55 us
    ppermute x1, starting transfers between devices, per_device(): arriving = lax.ppermute(phases, 'win', swap)  0.45 us
  transfers between devices with their start and end apart: 6, of which 3 were waited for; matrix products, arithmetic and copies ran while one was open for 0% of the time, Pallas kernels for 28%

profile of v5, /device:TPU:0, one launch (start us, length us, event | category | flops | bytes accessed | tf_op | source)
XLA Modules:
  0.0 13.8 jit_solution(8461089188898703462)
XLA Ops:
  0.0 0.5 %collective-permute-start = (bf16[12,16,256]{2,1,0:T(8,128)(2,1)}, bf16[12,16,256]{2,1,0:T(8,128)(2,1)S(1)}, u32[]{:S(2)}, u32[]{:S(2)}) collective-permute-start(bf16[12,16,256]{2,1,0:T(8,128)(2,1)} %bitcast.2), channel_id=1, source_target_pairs={{0,1},{1,0},{2,3},{3,2},{4,5},{5,4},{6,7},{7,6},{8,9},{9,8},{10,11... | collective-permute-start | bytes 294920 | tf_op jit(solution)/shard_map/ppermute | solution.py:332
  0.5 1.4 %own_phasors.1 = (f32[12,16,256]{2,1,0:T(8,128)S(1)}, f32[12,16,256]{2,1,0:T(8,128)S(1)}, f32[12,16,256]{2,1,0:T(8,128)S(1)}, f32[12,16,256]{2,1,0:T(8,128)S(1)}...) custom-call(bf16[12,16,256]{2,1,0:T(8,128)(2,1)} %bitcast.3, ...), custom_call_target="tpu_custom_call" | custom-call | tf_op jit(solution)/shard_map/own_phasors/pallas_call | solution.py:337
  1.9 0.3 %cross_spectra.4 = (f32[12,16,256]{2,1,0:T(8,128)S(1)}, f32[12,16,256]{2,1,0:T(8,128)S(1)}, f32[12,16,256]{2,1,0:T(8,128)S(1)}, f32[12,16,256]{2,1,0:T(8,128)S(1)}, bf16[2,2,16,256]{3,2,1,0:T(8,128)(2,1)S(1)}) custom-call(f32[1,256]{1,0:T(1,128)S(1)} %get-tuple-element.24.weight_ref, f32[12,16,256]{2,1,0:T(8,128)S(1)} %get-tuple-element.25.refs_0_, ...), custom_call_target="tpu_custom_call" | custom-call | tf_op jit(solution)/shard_map/cross_spectra/pallas_call | solution.py:358
  2.2 3.7 %collective-permute-start.3 = (bf16[2,2,16,256]{3,2,1,0:T(8,128)(2,1)S(1)}, bf16[2,2,16,256]{3,2,1,0:T(8,128)(2,1)S(1)}, u32[]{:S(2)}, u32[]{:S(2)}) collective-permute-start(bf16[2,2,16,256]{3,2,1,0:T(8,128)(2,1)S(1)} %get-tuple-element.36.refs_9_), channel_id=1, source_target_pairs={{0,6},{1,9},{2,4},{3,15},{4,12},{5,3},{6,14},{7,11},{8,10},{9,7},{... | collective-permute-start | bytes 98312 | tf_op jit(solution)/shard_map/ppermute | solution.py:369
  5.9 0.1 cross_spectra.5.refs_8_
  6.0 1.2 %collective-permute-start.2 = (bf16[2,2,16,256]{3,2,1,0:T(8,128)(2,1)S(1)}, bf16[2,2,16,256]{3,2,1,0:T(8,128)(2,1)S(1)}, u32[]{:S(2)}, u32[]{:S(2)}) collective-permute-start(bf16[2,2,16,256]{3,2,1,0:T(8,128)(2,1)S(1)} %cross_spectra.5.refs_8_), channel_id=1, source_target_pairs={{0,12},{1,15},{2,10},{3,9},{4,14},{5,11},{6,8},{7,13},{8,0},{9,3},... | collective-permute-start | bytes 98312 | tf_op jit(solution)/shard_map/ppermute | solution.py:369
  7.1 0.2 %cross_spectra.6.refs_8_ = bf16[2,2,16,256]{3,2,1,0:T(8,128)(2,1)S(1)} custom-call(f32[1,256]{1,0:T(1,128)S(1)} %get-tuple-element.24.weight_ref, f32[12,16,256]{2,1,0:T(8,128)S(1)} %get-tuple-element.25.refs_0_, f32[12,16,256]{2,1,0:T(8,128)S(1)} %get-tuple-element.26.refs_1_, f32[12,16,256]{2,1,0:T(8,128)S(1)} %get-tuple-element.27.refs_2_, ...), custom_call_target="tpu_custom_call" | custom-call | tf_op jit(solution)/shard_map/cross_spectra/pallas_call | solution.py:358
  7.3 0.8 %collective-permute-start.1 = (bf16[2,2,16,256]{3,2,1,0:T(8,128)(2,1)S(1)}, bf16[2,2,16,256]{3,2,1,0:T(8,128)(2,1)S(1)}, u32[]{:S(2)}, u32[]{:S(2)}) collective-permute-start(bf16[2,2,16,256]{3,2,1,0:T(8,128)(2,1)S(1)} %cross_spectra.6.refs_8_), channel_id=1, source_target_pairs={{0,2},{1,11},{2,0},{3,13},{4,8},{5,7},{6,4},{7,1},{8,14},{9,5},{10... | collective-permute-start | bytes 98312 | tf_op jit(solution)/shard_map/ppermute | solution.py:369
  8.2 0.2 %cross_spectra.7.after_ref = bf16[2,2,16,256]{3,2,1,0:T(8,128)(2,1)S(1)} custom-call(f32[1,256]{1,0:T(1,128)S(1)} %get-tuple-element.24.weight_ref, f32[12,16,256]{2,1,0:T(8,128)S(1)} %get-tuple-element.25.refs_0_, f32[12,16,256]{2,1,0:T(8,128)S(1)} %get-tuple-element.26.refs_1_, f32[12,16,256]{2,1,0:T(8,128)S(1)} %get-tuple-element.27.refs_2_, ...), custom_call_target="tpu_custom_call" | custom-call | tf_op jit(solution)/shard_map/cross_spectra/pallas_call | solution.py:358
  8.4 1.7 %collective-permute-start.4 = (bf16[2,2,16,256]{3,2,1,0:T(8,128)(2,1)S(1)}, bf16[2,2,16,256]{3,2,1,0:T(8,128)(2,1)S(1)}, u32[]{:S(2)}, u32[]{:S(2)}) collective-permute-start(bf16[2,2,16,256]{3,2,1,0:T(8,128)(2,1)S(1)} %cross_spectra.7.after_ref), channel_id=1, source_target_pairs={{0,4},{1,5},{2,6},{3,7},{4,0},{5,1},{6,2},{7,3},{8,12},{9,13},{10,... | collective-permute-start | bytes 98312 | tf_op jit(solution)/shard_map/ppermute | solution.py:369
  10.0 0.7 %split_lag_table.1.table_ref = bf16[3,2,256,512]{3,2,1,0:T(8,128)(2,1)S(1)} custom-call(bf16[2,2,16,256]{3,2,1,0:T(8,128)(2,1)S(1)} %cross_spectra.7.after_ref), custom_call_target="tpu_custom_call" | custom-call | tf_op jit(solution)/shard_map/split_lag_table/pallas_call | solution.py:374
  10.7 0.0 collective-permute-done.3.refs_0_
  10.7 0.2 %split_lag_sums.3.refs_1_ = f32[32,512]{1,0:T(8,128)S(1)} custom-call(bf16[3,2,256,512]{3,2,1,0:T(8,128)(2,1)S(1)} %split_lag_table.1.table_ref, bf16[2,2,16,256]{3,2,1,0:T(8,128)(2,1)S(1)} %collective-permute-done.3.refs_0_), custom_call_target="tpu_custom_call" | custom-call | flops 1000 | bytes 1000 | tf_op jit(solution)/shard_map/split_lag_sums/pallas_call | solution.py:384
  10.9 0.3 %collective-permute-done.2.refs_0_ = bf16[2,2,16,256]{3,2,1,0:T(8,128)(2,1)S(1)} collective-permute-done((bf16[2,2,16,256]{3,2,1,0:T(8,128)(2,1)S(1)}, bf16[2,2,16,256]{3,2,1,0:T(8,128)(2,1)S(1)}, u32[]{:S(2)}, u32[]{:S(2)}) %collective-permute-start.2) | collective-permute-done | bytes 32800 | tf_op jit(solution)/shard_map/ppermute | solution.py:369
  11.2 0.2 %split_lag_sums.4.refs_1_ = f32[32,512]{1,0:T(8,128)S(1)} custom-call(bf16[3,2,256,512]{3,2,1,0:T(8,128)(2,1)S(1)} %split_lag_table.1.table_ref, bf16[2,2,16,256]{3,2,1,0:T(8,128)(2,1)S(1)} %collective-permute-done.2.refs_0_, f32[32,512]{1,0:T(8,128)S(1)} %split_lag_sums.3.refs_1_), custom_call_target="tpu_custom_call" | custom-call | flops 1000 | bytes 1000 | tf_op jit(solution)/shard_map/split_lag_sums/pallas_call | solution.py:384
  11.4 0.1 collective-permute-done.1.refs_0_
  11.5 0.2 %split_lag_sums.5 = (f32[32,256]{1,0:T(8,128)S(1)}, f32[32,256]{1,0:T(8,128)S(1)}) custom-call(bf16[3,2,256,512]{3,2,1,0:T(8,128)(2,1)S(1)} %split_lag_table.1.table_ref, bf16[2,2,16,256]{3,2,1,0:T(8,128)(2,1)S(1)} %collective-permute-done.1.refs_0_, f32[32,512]{1,0:T(8,128)S(1)} %split_lag_sums.4.refs_1_), custom_call_target="tpu_custom_call" | custom-call | flops 1000 | bytes 1000 | tf_op jit(solution)/shard_map/split_lag_sums/pallas_call | solution.py:384
  11.7 0.6 %collective-permute-start.5 = (f32[32,256]{1,0:T(8,128)S(1)}, f32[32,256]{1,0:T(8,128)S(1)}, u32[]{:S(2)}, u32[]{:S(2)}) collective-permute-start(f32[32,256]{1,0:T(8,128)S(1)} %get-tuple-element.40), channel_id=1, source_target_pairs={{0,1},{1,0},{2,3},{3,2},{4,5},{5,4},{6,7},{7,6},{8,9},{9,8},{10,11... | collective-permute-start | bytes 98312 | tf_op jit(solution)/shard_map/ppermute | solution.py:392
  12.3 0.4 %whole_lag_table.1 = (bf16[2,2,16,256]{3,2,1,0:T(8,128)(2,1)S(1)}, bf16[2,2,256,256]{3,2,1,0:T(8,128)(2,1)S(1)}) custom-call(f32[1,256]{1,0:T(1,128)S(1)} %get-tuple-element.24.weight_ref, f32[12,16,256]{2,1,0:T(8,128)S(1)} %get-tuple-element.25.refs_0_, f32[12,16,256]{2,1,0:T(8,128)S(1)} %get-tuple-element.26.refs_1_, ...), custom_call_target="tpu_custom_call" | custom-call | tf_op jit(solution)/shard_map/whole_lag_table/pallas_call | solution.py:393
  12.8 0.1 %whole_lag_sums.2.before_ref = f32[32,256]{1,0:T(8,128)S(1)} custom-call(bf16[2,2,256,256]{3,2,1,0:T(8,128)(2,1)S(1)} %get-tuple-element.38.table_ref, bf16[2,2,16,256]{3,2,1,0:T(8,128)(2,1)S(1)} %get-tuple-element.39.spectra_ref, f32[32,256]{1,0:T(8,128)S(1)} %get-tuple-element.37.refs_8_.before_ref), custom_call_target="tpu_custom_call" | custom-call | flops 1000 | bytes 1000 | tf_op jit(solution)/shard_map/whole_lag_sums/pallas_call | solution.py:401
  12.9 0.0 collective-permute-done.4.spectra_ref
  12.9 0.1 %whole_lag_sums.3.mine_ref = f32[32,256]{1,0:T(8,128)S(1)} custom-call(bf16[2,2,256,256]{3,2,1,0:T(8,128)(2,1)S(1)} %get-tuple-element.38.table_ref, bf16[2,2,16,256]{3,2,1,0:T(8,128)(2,1)S(1)} %collective-permute-done.4.spectra_ref, f32[32,256]{1,0:T(8,128)S(1)} %whole_lag_sums.2.before_ref), custom_call_target="tpu_custom_call" | custom-call | flops 1000 | bytes 1000 | tf_op jit(solution)/shard_map/whole_lag_sums/pallas_call | solution.py:401
  13.1 0.1 collective-permute-done.5.theirs_ref
  13.2 0.6 %correlations.1 = f32[2,16,256]{2,1,0:T(8,128)} custom-call(f32[2,16,256]{2,1,0:T(8,128)S(1)} %get-tuple-element.23.keep_ref, f32[32,256]{1,0:T(8,128)S(1)} %whole_lag_sums.3.mine_ref, f32[32,256]{1,0:T(8,128)S(1)} %collective-permute-done.5.theirs_ref), custom_call_target="tpu_custom_call" | custom-call | tf_op jit(solution)/shard_map/correlations/pallas_call | solution.py:408
  (1 shorter events, 0.0 us)
Async XLA Ops:
  0.0 1.9 %collective-permute-start = (bf16[12,16,256]{2,1,0:T(8,128)(2,1)}, bf16[12,16,256]{2,1,0:T(8,128)(2,1)S(1)}, u32[]{:S(2)}, u32[]{:S(2)}) collective-permute-start(bf16[12,16,256]{2,1,0:T(8,128)(2,1)} %bitcast.2), channel_id=1, source_target_pairs={{0,1},{1,0},{2,3},{3,2},{4,5},{5,4},{6,7},{7,6},{8,9},{9,8},{10,11... | collective-permute-start | bytes 294920 | tf_op jit(solution)/shard_map/ppermute | solution.py:332
  2.2 8.5 %collective-permute-start.3 = (bf16[2,2,16,256]{3,2,1,0:T(8,128)(2,1)S(1)}, bf16[2,2,16,256]{3,2,1,0:T(8,128)(2,1)S(1)}, u32[]{:S(2)}, u32[]{:S(2)}) collective-permute-start(bf16[2,2,16,256]{3,2,1,0:T(8,128)(2,1)S(1)} %get-tuple-element.36.refs_9_), channel_id=1, source_target_pairs={{0,6},{1,9},{2,4},{3,15},{4,12},{5,3},{6,14},{7,11},{8,10},{9,7},{... | collective-permute-start | bytes 98312 | tf_op jit(solution)/shard_map/ppermute | solution.py:369
  6.0 5.2 %collective-permute-start.2 = (bf16[2,2,16,256]{3,2,1,0:T(8,128)(2,1)S(1)}, bf16[2,2,16,256]{3,2,1,0:T(8,128)(2,1)S(1)}, u32[]{:S(2)}, u32[]{:S(2)}) collective-permute-start(bf16[2,2,16,256]{3,2,1,0:T(8,128)(2,1)S(1)} %cross_spectra.5.refs_8_), channel_id=1, source_target_pairs={{0,12},{1,15},{2,10},{3,9},{4,14},{5,11},{6,8},{7,13},{8,0},{9,3},... | collective-permute-start | bytes 98312 | tf_op jit(solution)/shard_map/ppermute | solution.py:369
  7.3 4.2 %collective-permute-start.1 = (bf16[2,2,16,256]{3,2,1,0:T(8,128)(2,1)S(1)}, bf16[2,2,16,256]{3,2,1,0:T(8,128)(2,1)S(1)}, u32[]{:S(2)}, u32[]{:S(2)}) collective-permute-start(bf16[2,2,16,256]{3,2,1,0:T(8,128)(2,1)S(1)} %cross_spectra.6.refs_8_), channel_id=1, source_target_pairs={{0,2},{1,11},{2,0},{3,13},{4,8},{5,7},{6,4},{7,1},{8,14},{9,5},{10... | collective-permute-start | bytes 98312 | tf_op jit(solution)/shard_map/ppermute | solution.py:369
  8.4 4.6 %collective-permute-start.4 = (bf16[2,2,16,256]{3,2,1,0:T(8,128)(2,1)S(1)}, bf16[2,2,16,256]{3,2,1,0:T(8,128)(2,1)S(1)}, u32[]{:S(2)}, u32[]{:S(2)}) collective-permute-start(bf16[2,2,16,256]{3,2,1,0:T(8,128)(2,1)S(1)} %cross_spectra.7.after_ref), channel_id=1, source_target_pairs={{0,4},{1,5},{2,6},{3,7},{4,0},{5,1},{6,2},{7,3},{8,12},{9,13},{10,... | collective-permute-start | bytes 98312 | tf_op jit(solution)/shard_map/ppermute | solution.py:369
  11.7 1.5 %collective-permute-start.5 = (f32[32,256]{1,0:T(8,128)S(1)}, f32[32,256]{1,0:T(8,128)S(1)}, u32[]{:S(2)}, u32[]{:S(2)}) collective-permute-start(f32[32,256]{1,0:T(8,128)S(1)} %get-tuple-element.40), channel_id=1, source_target_pairs={{0,1},{1,0},{2,3},{3,2},{4,5},{5,4},{6,7},{7,6},{8,9},{9,8},{10,11... | collective-permute-start | bytes 98312 | tf_op jit(solution)/shard_map/ppermute | solution.py:392

commit v6 on v5

--- a/solution.py
+++ b/solution.py
@@ -12,10 +12,10 @@
 BEGUN = 2
 SMALL = 1000
 ROUNDS = (
-    ((3, 2, 6, 7, 5, 1, 0, 4), (4, 7, 1, 5, 3, 6, 2, 0)),
-    ((6, 5, 7, 4, 0, 2, 1, 3), (7, 4, 5, 6, 1, 0, 3, 2)),
-    ((1, 0, 4, 2, 7, 3, 5, 6), (5, 6, 3, 0, 2, 7, 4, 1)),
-    ((2, 3, 0, 1, 6, 4, 7, 5), (2, 3, 0, 1, 6, 4, 7, 5)),
+    ((2, 3, 6, 5, 1, 7, 4, 0), (4, 6, 5, 0, 7, 3, 1, 2)),
+    ((6, 4, 7, 1, 2, 0, 3, 5), (5, 7, 1, 4, 6, 2, 0, 3)),
+    ((3, 0, 4, 2, 5, 1, 7, 6), (7, 5, 3, 6, 0, 4, 2, 1)),
+    ((1, 2, 0, 7, 3, 6, 5, 4), (1, 2, 0, 7, 3, 6, 5, 4)),
 )
 VMEM = pl.BlockSpec(memory_space=pltpu.VMEM)
 ANY = pl.BlockSpec(memory_space=pl.ANY)
@@ -265,43 +265,29 @@
     full_sums(own_ref, sta, own, other, weight_ref[...])
 
 
-def times(spectra_ref, table_ref):
+def times(spectra_ref, table_ref, slot, lags):
     _, rows, stations, bins = spectra_ref.shape
     total = 0.0
     for c in range(2):
-        spectra = spectra_ref[c].reshape(rows * stations, bins).astype(jnp.bfloat16)
-        total = total + jnp.dot(spectra, table_ref[c], preferred_element_type=jnp.float32)
+        spectra = spectra_ref[c].reshape(rows * stations, bins)
+        table = table_ref[slot, c, :, lags]
+        total = total + jnp.dot(spectra, table, preferred_element_type=jnp.float32)
     return total
 
 
-def split_kernel(slot, end, table_ref, *refs):
-    outs = 2 if end else 1
-    spectra_ref, *before = refs[:-outs]
-    total = times(spectra_ref, table_ref.at[slot])
+def sums_kernel(slot, first_lag, table_ref, spectra_ref, *refs):
+    *before, out_ref = refs
+    lags = pl.ds(first_lag, out_ref.shape[-1])
+    total = times(spectra_ref, table_ref, slot, lags)
     for before_ref in before:
-        total = total + before_ref[...]
-    if end:
-        mine_ref, theirs_ref = refs[-2:]
-        half = mine_ref.shape[-1]
-        mine_ref[...], theirs_ref[...] = total[:, :half], total[:, half:].astype(theirs_ref.dtype)
-    else:
-        refs[-1][...] = total
-
-
-def whole_kernel(slot, table_ref, spectra_ref, before_ref, out_ref):
-    out_ref[...] = before_ref[...] + times(spectra_ref, table_ref.at[slot])
-
-
-def final_kernel(keep_ref, mine_ref, theirs_ref, out_hbm, out_ref, sems):
-    rows, stations, half = out_ref.shape
-    copies = []
-    for r in range(rows):
-        row = pl.ds(r * stations, stations)
-        out_ref[r] = (mine_ref[row] + theirs_ref[row].astype(jnp.float32)) * keep_ref[r]
-        copies.append(pltpu.make_async_copy(out_ref.at[r], out_hbm.at[r], sems.at[r]))
-        copies[-1].start()
-    for copy in copies:
-        copy.wait()
+        total = total + before_ref[:, lags]
+    out_ref[...] = total
+
+
+def mine_kernel(slot, split_ref, whole_ref, spectra_ref, own_ref, before_ref, out_ref):
+    lags = pl.ds(0, out_ref.shape[-1])
+    total = before_ref[:, lags] + times(spectra_ref, split_ref, slot, lags)
+    out_ref[...] = total + times(own_ref, whole_ref, 1, lags)
 
 
 def per_device(phases, window_valid, freq_taper, pair_mask):
@@ -380,40 +366,37 @@
     )(sent[-1])
     pairs, sums = rows * stations, []
     for slot in range(split):
-        end = slot == split - 1
+        before, end = sums, slot == split - 1
         sums = kernel(
-            functools.partial(split_kernel, slot, end),
+            functools.partial(sums_kernel, slot, half if end else 0),
             "split_lag_sums",
-            [((pairs, half), f32)] * 2 if end else [((pairs, LAGS), f32)],
+            [((pairs, half if end else LAGS), f32)],
             [VMEM] * (2 + len(sums)),
             flops=SMALL,
         )(split_table, arrived[slot], *sums)
-    mine, theirs = sums
-    theirs = lax.ppermute(theirs, "win", swap)
+    theirs = lax.ppermute(sums[0], "win", swap)
     own_spectra, whole_table = kernel(
         functools.partial(whole_table_kernel, blocks, rounds),
         "whole_lag_table",
         [full_shape, ((2, 2, bins, half), bf16)],
         [VMEM] * 10,
         scratch(2, half),
-    )(weight, *own, *other, mine)
-    for slot, spectra in ((1, own_spectra), (0, arrived[-1])):
-        (mine,) = kernel(
-            functools.partial(whole_kernel, slot),
-            "whole_lag_sums",
-            [((pairs, half), f32)],
-            [VMEM] * 3,
-            flops=SMALL,
-        )(whole_table, spectra, mine)
-    return pl.pallas_call(
-        final_kernel,
-        out_shape=jax.ShapeDtypeStruct(*half_shape),
-        in_specs=[VMEM] * 3,
-        out_specs=ANY,
-        scratch_shapes=[pltpu.VMEM(*half_shape), pltpu.SemaphoreType.DMA((rows,))],
-        compiler_params=PARAMS,
-        name="correlations",
-    )(keep, mine, theirs)
+    )(weight, *own, *other, sums[0])
+    (mine,) = kernel(
+        functools.partial(mine_kernel, split - 1),
+        "own_lag_sums",
+        [((pairs, half), f32)],
+        [VMEM] * 5,
+        flops=SMALL,
+    )(split_table, whole_table, arrived[split - 1], own_spectra, *before)
+    (mine,) = kernel(
+        functools.partial(sums_kernel, 0, 0),
+        "last_lag_sums",
+        [((pairs, half), f32)],
+        [VMEM] * 3,
+        flops=SMALL,
+    )(whole_table, arrived[-1], mine)
+    return (mine + theirs).reshape(rows, stations, half) * keep
 
 
 def solution(mesh):

time: 14 us -> 13.9 us (level)
  other arithmetic: 0 us -> 0.63 us
  Pallas kernels: 4.81 us -> 4.18 us
  starting transfers between devices: 8.41 us -> 8.03 us
  waiting for transfers between devices: 0.53 us -> 0.84 us
    pallas_call x6 -> x5, Pallas kernels: 1.48 us -> 0.86 us  [the longest x3 0.51 us: per_device(): kernel(functools.partial(sums_kernel, slot, half if end else 0), 'split_l...]
    mul x0 -> x1, other arithmetic: none -> 0.62 us  [per_device(): return (mine + theirs).reshape(rows, stations, half) * keep]
    ppermute x1, starting transfers between devices: 0.65 us -> 0.22 us  [per_device(): theirs = lax.ppermute(sums[0], 'win', swap)]
    ppermute x4, waiting for transfers between devices: 0.42 us -> 0.59 us  [per_device(): arrived.append(lax.ppermute(spectra, axes, moves))]
    ppermute x1, waiting for transfers between devices: 0.1 us -> 0.25 us  [per_device(): theirs = lax.ppermute(sums[0], 'win', swap)]
  transfers between devices with their start and end apart: 6 -> 6, of which waited for: 3 -> 2; matrix products, arithmetic and copies ran while one was open for 0% -> 0% of each run, Pallas kernels for 28% -> 28%
where the time goes in v6:
time: 13.9 us; the launch traced here: 13.8 us
  starting transfers between devices  8.03 us (58%)
  Pallas kernels  4.18 us (30%)
  waiting for transfers between devices  0.84 us (6%)
  other arithmetic  0.63 us (5%)
    ppermute x4, starting transfers between devices, per_device(): arrived.append(lax.ppermute(spectra, axes, moves))  7.36 us
    pallas_call x1, Pallas kernels, per_device(): kernel(functools.partial(prepare_kernel, blocks, begun), 'own_phasors', p...  1.4 us
    pallas_call x4, Pallas kernels, per_device(): kernel(functools.partial(cross_kernel, targets, not index, index < len(be...  0.83 us
    pallas_call x1, Pallas kernels, per_device(): kernel(functools.partial(split_table_kernel, blocks, rounds), 'split_lag_...  0.67 us
    mul x1, other arithmetic, per_device(): return (mine + theirs).reshape(rows, stations, half) * keep  0.62 us
    ppermute x4, waiting for transfers between devices, per_device(): arrived.append(lax.ppermute(spectra, axes, moves))  0.59 us
    pallas_call x3, Pallas kernels, per_device(): kernel(functools.partial(sums_kernel, slot, half if end else 0), 'split_l...  0.51 us
    ppermute x1, starting transfers between devices, per_device(): arriving = lax.ppermute(phases, 'win', swap)  0.45 us
  transfers between devices with their start and end apart: 6, of which 2 were waited for; matrix products, arithmetic and copies ran while one was open for 0% of the time, Pallas kernels for 28%

profile of v6, /device:TPU:0, one launch (start us, length us, event | category | flops | bytes accessed | tf_op | source)
XLA Modules:
  0.0 13.8 jit_solution(2680407756159417662)
XLA Ops:
  0.0 0.5 %collective-permute-start = (bf16[12,16,256]{2,1,0:T(8,128)(2,1)}, bf16[12,16,256]{2,1,0:T(8,128)(2,1)S(1)}, u32[]{:S(2)}, u32[]{:S(2)}) collective-permute-start(bf16[12,16,256]{2,1,0:T(8,128)(2,1)} %bitcast.4), channel_id=1, source_target_pairs={{0,1},{1,0},{2,3},{3,2},{4,5},{5,4},{6,7},{7,6},{8,9},{9,8},{10,11... | collective-permute-start | bytes 294920 | tf_op jit(solution)/shard_map/ppermute | solution.py:318
  0.5 1.4 %own_phasors.1 = (f32[12,16,256]{2,1,0:T(8,128)S(1)}, f32[12,16,256]{2,1,0:T(8,128)S(1)}, f32[12,16,256]{2,1,0:T(8,128)S(1)}, f32[12,16,256]{2,1,0:T(8,128)S(1)}...) custom-call(bf16[12,16,256]{2,1,0:T(8,128)(2,1)} %bitcast.5, ...), custom_call_target="tpu_custom_call" | custom-call | tf_op jit(solution)/shard_map/own_phasors/pallas_call | solution.py:323
  1.9 0.3 %cross_spectra.4 = (f32[12,16,256]{2,1,0:T(8,128)S(1)}, f32[12,16,256]{2,1,0:T(8,128)S(1)}, f32[12,16,256]{2,1,0:T(8,128)S(1)}, f32[12,16,256]{2,1,0:T(8,128)S(1)}, bf16[2,2,16,256]{3,2,1,0:T(8,128)(2,1)S(1)}) custom-call(f32[1,256]{1,0:T(1,128)S(1)} %get-tuple-element.21.weight_ref, f32[12,16,256]{2,1,0:T(8,128)S(1)} %get-tuple-element.22.refs_0_, ...), custom_call_target="tpu_custom_call" | custom-call | tf_op jit(solution)/shard_map/cross_spectra/pallas_call | solution.py:344
  2.2 2.7 %collective-permute-start.3 = (bf16[2,2,16,256]{3,2,1,0:T(8,128)(2,1)S(1)}, bf16[2,2,16,256]{3,2,1,0:T(8,128)(2,1)S(1)}, u32[]{:S(2)}, u32[]{:S(2)}) collective-permute-start(bf16[2,2,16,256]{3,2,1,0:T(8,128)(2,1)S(1)} %get-tuple-element.33.refs_9_), channel_id=1, source_target_pairs={{0,4},{1,9},{2,6},{3,13},{4,12},{5,11},{6,10},{7,1},{8,2},{9,15},{... | collective-permute-start | bytes 98312 | tf_op jit(solution)/shard_map/ppermute | solution.py:355
  4.9 0.1 cross_spectra.5.refs_8_
  5.0 2.5 %collective-permute-start.2 = (bf16[2,2,16,256]{3,2,1,0:T(8,128)(2,1)S(1)}, bf16[2,2,16,256]{3,2,1,0:T(8,128)(2,1)S(1)}, u32[]{:S(2)}, u32[]{:S(2)}) collective-permute-start(bf16[2,2,16,256]{3,2,1,0:T(8,128)(2,1)S(1)} %cross_spectra.5.refs_8_), channel_id=1, source_target_pairs={{0,12},{1,11},{2,8},{3,15},{4,14},{5,3},{6,2},{7,9},{8,4},{9,13},{... | collective-permute-start | bytes 98312 | tf_op jit(solution)/shard_map/ppermute | solution.py:355
  7.6 0.2 %cross_spectra.6.refs_8_ = bf16[2,2,16,256]{3,2,1,0:T(8,128)(2,1)S(1)} custom-call(f32[1,256]{1,0:T(1,128)S(1)} %get-tuple-element.21.weight_ref, f32[12,16,256]{2,1,0:T(8,128)S(1)} %get-tuple-element.22.refs_0_, f32[12,16,256]{2,1,0:T(8,128)S(1)} %get-tuple-element.23.refs_1_, f32[12,16,256]{2,1,0:T(8,128)S(1)} %get-tuple-element.24.refs_2_, ...), custom_call_target="tpu_custom_call" | custom-call | tf_op jit(solution)/shard_map/cross_spectra/pallas_call | solution.py:344
  7.8 0.6 %collective-permute-start.1 = (bf16[2,2,16,256]{3,2,1,0:T(8,128)(2,1)S(1)}, bf16[2,2,16,256]{3,2,1,0:T(8,128)(2,1)S(1)}, u32[]{:S(2)}, u32[]{:S(2)}) collective-permute-start(bf16[2,2,16,256]{3,2,1,0:T(8,128)(2,1)S(1)} %cross_spectra.6.refs_8_), channel_id=1, source_target_pairs={{0,6},{1,15},{2,0},{3,11},{4,8},{5,7},{6,4},{7,13},{8,10},{9,1},{1... | collective-permute-start | bytes 98312 | tf_op jit(solution)/shard_map/ppermute | solution.py:355
  8.3 0.2 %cross_spectra.7.after_ref = bf16[2,2,16,256]{3,2,1,0:T(8,128)(2,1)S(1)} custom-call(f32[1,256]{1,0:T(1,128)S(1)} %get-tuple-element.21.weight_ref, f32[12,16,256]{2,1,0:T(8,128)S(1)} %get-tuple-element.22.refs_0_, f32[12,16,256]{2,1,0:T(8,128)S(1)} %get-tuple-element.23.refs_1_, f32[12,16,256]{2,1,0:T(8,128)S(1)} %get-tuple-element.24.refs_2_, ...), custom_call_target="tpu_custom_call" | custom-call | tf_op jit(solution)/shard_map/cross_spectra/pallas_call | solution.py:344
  8.5 1.6 %collective-permute-start.4 = (bf16[2,2,16,256]{3,2,1,0:T(8,128)(2,1)S(1)}, bf16[2,2,16,256]{3,2,1,0:T(8,128)(2,1)S(1)}, u32[]{:S(2)}, u32[]{:S(2)}) collective-permute-start(bf16[2,2,16,256]{3,2,1,0:T(8,128)(2,1)S(1)} %cross_spectra.7.after_ref), channel_id=1, source_target_pairs={{0,2},{1,3},{2,4},{3,5},{4,0},{5,1},{6,14},{7,15},{8,6},{9,7},{10,... | collective-permute-start | bytes 98312 | tf_op jit(solution)/shard_map/ppermute | solution.py:355
  10.1 0.7 %split_lag_table.1.table_ref.split_ref = bf16[3,2,256,512]{3,2,1,0:T(8,128)(2,1)S(1)} custom-call(bf16[2,2,16,256]{3,2,1,0:T(8,128)(2,1)S(1)} %cross_spectra.7.after_ref), custom_call_target="tpu_custom_call" | custom-call | tf_op jit(solution)/shard_map/split_lag_table/pallas_call | solution.py:360
  10.8 0.0 collective-permute-done.3.spectra_ref
  10.8 0.2 %split_lag_sums.3.refs_0_ = f32[32,512]{1,0:T(8,128)S(1)} custom-call(bf16[3,2,256,512]{3,2,1,0:T(8,128)(2,1)S(1)} %split_lag_table.1.table_ref.split_ref, bf16[2,2,16,256]{3,2,1,0:T(8,128)(2,1)S(1)} %collective-permute-done.3.spectra_ref), custom_call_target="tpu_custom_call" | custom-call | flops 1000 | bytes 1000 | tf_op jit(solution)/shard_map/split_lag_sums/pallas_call | solution.py:370
  11.0 0.0 collective-permute-done.2.spectra_ref
  11.0 0.2 %split_lag_sums.4.refs_0_.before_ref = f32[32,512]{1,0:T(8,128)S(1)} custom-call(bf16[3,2,256,512]{3,2,1,0:T(8,128)(2,1)S(1)} %split_lag_table.1.table_ref.split_ref, bf16[2,2,16,256]{3,2,1,0:T(8,128)(2,1)S(1)} %collective-permute-done.2.spectra_ref, f32[32,512]{1,0:T(8,128)S(1)} %split_lag_sums.3.refs_0_), custom_call_target="tpu_custom_call" | custom-call | flops 1000 | bytes 1000 | tf_op jit(solution)/shard_map/split_lag_sums/pallas_call | solution.py:370
  11.2 0.5 %collective-permute-done.1.spectra_ref = bf16[2,2,16,256]{3,2,1,0:T(8,128)(2,1)S(1)} collective-permute-done((bf16[2,2,16,256]{3,2,1,0:T(8,128)(2,1)S(1)}, bf16[2,2,16,256]{3,2,1,0:T(8,128)(2,1)S(1)}, u32[]{:S(2)}, u32[]{:S(2)}) %collective-permute-start.1) | collective-permute-done | bytes 32800 | tf_op jit(solution)/shard_map/ppermute | solution.py:355
  11.7 0.1 %split_lag_sums.5.refs_8_ = f32[32,256]{1,0:T(8,128)S(1)} custom-call(bf16[3,2,256,512]{3,2,1,0:T(8,128)(2,1)S(1)} %split_lag_table.1.table_ref.split_ref, bf16[2,2,16,256]{3,2,1,0:T(8,128)(2,1)S(1)} %collective-permute-done.1.spectra_ref, f32[32,512]{1,0:T(8,128)S(1)} %split_lag_sums.4.refs_0_.before_ref), custom_call_target="tpu_custom_call" | custom-call | flops 1000 | bytes 1000 | tf_op jit(solution)/shard_map/split_lag_sums/pallas_call | solution.py:370
  11.9 0.2 %collective-permute-start.5 = (f32[32,256]{1,0:T(8,128)S(1)}, f32[32,256]{1,0:T(8,128)S(1)}, u32[]{:S(2)}, u32[]{:S(2)}) collective-permute-start(f32[32,256]{1,0:T(8,128)S(1)} %split_lag_sums.5.refs_8_), channel_id=1, source_target_pairs={{0,1},{1,0},{2,3},{3,2},{4,5},{5,4},{6,7},{7,6},{8,9},{9,8},{10,11... | collective-permute-start | bytes 98312 | tf_op jit(solution)/shard_map/ppermute | solution.py:377
  12.1 0.4 %whole_lag_table.1 = (bf16[2,2,16,256]{3,2,1,0:T(8,128)(2,1)S(1)}, bf16[2,2,256,256]{3,2,1,0:T(8,128)(2,1)S(1)}) custom-call(f32[1,256]{1,0:T(1,128)S(1)} %get-tuple-element.21.weight_ref, f32[12,16,256]{2,1,0:T(8,128)S(1)} %get-tuple-element.22.refs_0_, f32[12,16,256]{2,1,0:T(8,128)S(1)} %get-tuple-element.23.refs_1_, ...), custom_call_target="tpu_custom_call" | custom-call | tf_op jit(solution)/shard_map/whole_lag_table/pallas_call | solution.py:378
  12.5 0.2 %own_lag_sums.1.refs_0_ = f32[32,256]{1,0:T(8,128)S(1)} custom-call(bf16[3,2,256,512]{3,2,1,0:T(8,128)(2,1)S(1)} %split_lag_table.1.table_ref.split_ref, bf16[2,2,256,256]{3,2,1,0:T(8,128)(2,1)S(1)} %get-tuple-element.34.whole_ref.table_ref, bf16[2,2,16,256]{3,2,1,0:T(8,128)(2,1)S(1)} %collective-permute-done.1.spectra_ref, ...), custom_call_target="tpu_custom_call" | custom-call | flops 1000 | bytes 1000 | tf_op jit(solution)/shard_map/own_lag_sums/pallas_call | solution.py:385
  12.7 0.0 collective-permute-done.4.spectra_ref
  12.7 0.1 %last_lag_sums.1 = f32[32,256]{1,0:T(8,128)S(1)} custom-call(bf16[2,2,256,256]{3,2,1,0:T(8,128)(2,1)S(1)} %get-tuple-element.34.whole_ref.table_ref, bf16[2,2,16,256]{3,2,1,0:T(8,128)(2,1)S(1)} %collective-permute-done.4.spectra_ref, f32[32,256]{1,0:T(8,128)S(1)} %own_lag_sums.1.refs_0_), custom_call_target="tpu_custom_call" | custom-call | flops 1000 | bytes 1000 | tf_op jit(solution)/shard_map/last_lag_sums/pallas_call | solution.py:392
  12.9 0.2 %collective-permute-done.5 = f32[32,256]{1,0:T(8,128)S(1)} collective-permute-done((f32[32,256]{1,0:T(8,128)S(1)}, f32[32,256]{1,0:T(8,128)S(1)}, u32[]{:S(2)}, u32[]{:S(2)}) %collective-permute-start.5) | collective-permute-done | bytes 32800 | tf_op jit(solution)/shard_map/ppermute | solution.py:377
  13.2 0.6 %mul.3 = f32[2,16,256]{2,1,0:T(8,128)} multiply(f32[2,16,256]{2,1,0:T(8,128)S(1)} %bitcast.3, f32[2,16,256]{2,1,0:T(8,128)S(1)} %get-tuple-element.36) | non-fusion elementwise | flops 8192 | bytes 98304 | tf_op jit(solution)/shard_map/mul | solution.py:399
  (2 shorter events, 0.0 us)
Async XLA Ops:
  0.0 1.9 %collective-permute-start = (bf16[12,16,256]{2,1,0:T(8,128)(2,1)}, bf16[12,16,256]{2,1,0:T(8,128)(2,1)S(1)}, u32[]{:S(2)}, u32[]{:S(2)}) collective-permute-start(bf16[12,16,256]{2,1,0:T(8,128)(2,1)} %bitcast.4), channel_id=1, source_target_pairs={{0,1},{1,0},{2,3},{3,2},{4,5},{5,4},{6,7},{7,6},{8,9},{9,8},{10,11... | collective-permute-start | bytes 294920 | tf_op jit(solution)/shard_map/ppermute | solution.py:318
  2.2 8.6 %collective-permute-start.3 = (bf16[2,2,16,256]{3,2,1,0:T(8,128)(2,1)S(1)}, bf16[2,2,16,256]{3,2,1,0:T(8,128)(2,1)S(1)}, u32[]{:S(2)}, u32[]{:S(2)}) collective-permute-start(bf16[2,2,16,256]{3,2,1,0:T(8,128)(2,1)S(1)} %get-tuple-element.33.refs_9_), channel_id=1, source_target_pairs={{0,4},{1,9},{2,6},{3,13},{4,12},{5,11},{6,10},{7,1},{8,2},{9,15},{... | collective-permute-start | bytes 98312 | tf_op jit(solution)/shard_map/ppermute | solution.py:355
  5.0 5.9 %collective-permute-start.2 = (bf16[2,2,16,256]{3,2,1,0:T(8,128)(2,1)S(1)}, bf16[2,2,16,256]{3,2,1,0:T(8,128)(2,1)S(1)}, u32[]{:S(2)}, u32[]{:S(2)}) collective-permute-start(bf16[2,2,16,256]{3,2,1,0:T(8,128)(2,1)S(1)} %cross_spectra.5.refs_8_), channel_id=1, source_target_pairs={{0,12},{1,11},{2,8},{3,15},{4,14},{5,3},{6,2},{7,9},{8,4},{9,13},{... | collective-permute-start | bytes 98312 | tf_op jit(solution)/shard_map/ppermute | solution.py:355
  7.8 4.0 %collective-permute-start.1 = (bf16[2,2,16,256]{3,2,1,0:T(8,128)(2,1)S(1)}, bf16[2,2,16,256]{3,2,1,0:T(8,128)(2,1)S(1)}, u32[]{:S(2)}, u32[]{:S(2)}) collective-permute-start(bf16[2,2,16,256]{3,2,1,0:T(8,128)(2,1)S(1)} %cross_spectra.6.refs_8_), channel_id=1, source_target_pairs={{0,6},{1,15},{2,0},{3,11},{4,8},{5,7},{6,4},{7,13},{8,10},{9,1},{1... | collective-permute-start | bytes 98312 | tf_op jit(solution)/shard_map/ppermute | solution.py:355
  8.5 4.2 %collective-permute-start.4 = (bf16[2,2,16,256]{3,2,1,0:T(8,128)(2,1)S(1)}, bf16[2,2,16,256]{3,2,1,0:T(8,128)(2,1)S(1)}, u32[]{:S(2)}, u32[]{:S(2)}) collective-permute-start(bf16[2,2,16,256]{3,2,1,0:T(8,128)(2,1)S(1)} %cross_spectra.7.after_ref), channel_id=1, source_target_pairs={{0,2},{1,3},{2,4},{3,5},{4,0},{5,1},{6,14},{7,15},{8,6},{9,7},{10,... | collective-permute-start | bytes 98312 | tf_op jit(solution)/shard_map/ppermute | solution.py:355
  11.9 1.3 %collective-permute-start.5 = (f32[32,256]{1,0:T(8,128)S(1)}, f32[32,256]{1,0:T(8,128)S(1)}, u32[]{:S(2)}, u32[]{:S(2)}) collective-permute-start(f32[32,256]{1,0:T(8,128)S(1)} %split_lag_sums.5.refs_8_), channel_id=1, source_target_pairs={{0,1},{1,0},{2,3},{3,2},{4,5},{5,4},{6,7},{7,6},{8,9},{9,8},{10,11... | collective-permute-start | bytes 98312 | tf_op jit(solution)/shard_map/ppermute | solution.py:377

commit v7 on v6

--- a/solution.py
+++ b/solution.py
@@ -12,10 +12,10 @@
 BEGUN = 2
 SMALL = 1000
 ROUNDS = (
-    ((2, 3, 6, 5, 1, 7, 4, 0), (4, 6, 5, 0, 7, 3, 1, 2)),
-    ((6, 4, 7, 1, 2, 0, 3, 5), (5, 7, 1, 4, 6, 2, 0, 3)),
-    ((3, 0, 4, 2, 5, 1, 7, 6), (7, 5, 3, 6, 0, 4, 2, 1)),
-    ((1, 2, 0, 7, 3, 6, 5, 4), (1, 2, 0, 7, 3, 6, 5, 4)),
+    ((3, 2, 6, 7, 5, 1, 0, 4), (4, 7, 5, 2, 1, 6, 3, 0)),
+    ((6, 5, 7, 4, 0, 2, 1, 3), (7, 4, 1, 6, 3, 0, 5, 2)),
+    ((1, 0, 4, 5, 7, 3, 2, 6), (5, 6, 3, 0, 2, 4, 7, 1)),
+    ((2, 3, 0, 1, 6, 7, 4, 5), (2, 3, 0, 1, 6, 7, 4, 5)),
 )
 VMEM = pl.BlockSpec(memory_space=pltpu.VMEM)
 ANY = pl.BlockSpec(memory_space=pl.ANY)

time: 13.9 us -> 14 us (level)
  starting transfers between devices: 8.03 us -> 8.67 us
  waiting for transfers between devices: 0.84 us -> 0.25 us
    ppermute x1, starting transfers between devices: 0.22 us -> 0.88 us  [per_device(): theirs = lax.ppermute(sums[0], 'win', swap)]
    ppermute x4, waiting for transfers between devices: 0.59 us -> 0.19 us  [per_device(): arrived.append(lax.ppermute(spectra, axes, moves))]
    ppermute x1, waiting for transfers between devices: 0.25 us -> 0.06 us  [per_device(): theirs = lax.ppermute(sums[0], 'win', swap)]
where the time goes in v7:
time: 14 us; the launch traced here: 13.8 us
  starting transfers between devices  8.67 us (62%)
  Pallas kernels  4.2 us (30%)
  other arithmetic  0.63 us (4%)
  waiting for transfers between devices  0.25 us (2%)
    ppermute x4, starting transfers between devices, per_device(): arrived.append(lax.ppermute(spectra, axes, moves))  7.34 us
    pallas_call x1, Pallas kernels, per_device(): kernel(functools.partial(prepare_kernel, blocks, begun), 'own_phasors', p...  1.4 us
    ppermute x1, starting transfers between devices, per_device(): theirs = lax.ppermute(sums[0], 'win', swap)  0.88 us
    pallas_call x4, Pallas kernels, per_device(): kernel(functools.partial(cross_kernel, targets, not index, index < len(be...  0.83 us
    pallas_call x1, Pallas kernels, per_device(): kernel(functools.partial(split_table_kernel, blocks, rounds), 'split_lag_...  0.67 us
    mul x1, other arithmetic, per_device(): return (mine + theirs).reshape(rows, stations, half) * keep  0.62 us
    pallas_call x3, Pallas kernels, per_device(): kernel(functools.partial(sums_kernel, slot, half if end else 0), 'split_l...  0.53 us
    ppermute x1, starting transfers between devices, per_device(): arriving = lax.ppermute(phases, 'win', swap)  0.45 us
  transfers between devices with their start and end apart: 6, of which 2 were waited for; matrix products, arithmetic and copies ran while one was open for 0% of the time, Pallas kernels for 28%

profile of v7, /device:TPU:0, one launch (start us, length us, event | category | flops | bytes accessed | tf_op | source)
XLA Modules:
  0.0 13.8 jit_solution(1601748240195762020)
XLA Ops:
  0.0 0.5 %collective-permute-start = (bf16[12,16,256]{2,1,0:T(8,128)(2,1)}, bf16[12,16,256]{2,1,0:T(8,128)(2,1)S(1)}, u32[]{:S(2)}, u32[]{:S(2)}) collective-permute-start(bf16[12,16,256]{2,1,0:T(8,128)(2,1)} %bitcast.4), channel_id=1, source_target_pairs={{0,1},{1,0},{2,3},{3,2},{4,5},{5,4},{6,7},{7,6},{8,9},{9,8},{10,11... | collective-permute-start | bytes 294920 | tf_op jit(solution)/shard_map/ppermute | solution.py:318
  0.5 1.4 %own_phasors.1 = (f32[12,16,256]{2,1,0:T(8,128)S(1)}, f32[12,16,256]{2,1,0:T(8,128)S(1)}, f32[12,16,256]{2,1,0:T(8,128)S(1)}, f32[12,16,256]{2,1,0:T(8,128)S(1)}...) custom-call(bf16[12,16,256]{2,1,0:T(8,128)(2,1)} %bitcast.5, ...), custom_call_target="tpu_custom_call" | custom-call | tf_op jit(solution)/shard_map/own_phasors/pallas_call | solution.py:323
  1.9 0.0 collective-permute-done.refs_5_
  1.9 0.3 %cross_spectra.4 = (f32[12,16,256]{2,1,0:T(8,128)S(1)}, f32[12,16,256]{2,1,0:T(8,128)S(1)}, f32[12,16,256]{2,1,0:T(8,128)S(1)}, f32[12,16,256]{2,1,0:T(8,128)S(1)}, bf16[2,2,16,256]{3,2,1,0:T(8,128)(2,1)S(1)}) custom-call(f32[1,256]{1,0:T(1,128)S(1)} %get-tuple-element.21.weight_ref, f32[12,16,256]{2,1,0:T(8,128)S(1)} %get-tuple-element.22.refs_0_, ...), custom_call_target="tpu_custom_call" | custom-call | tf_op jit(solution)/shard_map/cross_spectra/pallas_call | solution.py:344
  2.2 3.7 %collective-permute-start.3 = (bf16[2,2,16,256]{3,2,1,0:T(8,128)(2,1)S(1)}, bf16[2,2,16,256]{3,2,1,0:T(8,128)(2,1)S(1)}, u32[]{:S(2)}, u32[]{:S(2)}) collective-permute-start(bf16[2,2,16,256]{3,2,1,0:T(8,128)(2,1)S(1)} %get-tuple-element.33.refs_9_), channel_id=1, source_target_pairs={{0,6},{1,9},{2,4},{3,15},{4,12},{5,11},{6,14},{7,5},{8,10},{9,3},{... | collective-permute-start | bytes 98312 | tf_op jit(solution)/shard_map/ppermute | solution.py:355
  5.9 0.1 cross_spectra.5.refs_8_
  6.0 1.2 %collective-permute-start.2 = (bf16[2,2,16,256]{3,2,1,0:T(8,128)(2,1)S(1)}, bf16[2,2,16,256]{3,2,1,0:T(8,128)(2,1)S(1)}, u32[]{:S(2)}, u32[]{:S(2)}) collective-permute-start(bf16[2,2,16,256]{3,2,1,0:T(8,128)(2,1)S(1)} %cross_spectra.5.refs_8_), channel_id=1, source_target_pairs={{0,12},{1,15},{2,10},{3,9},{4,14},{5,3},{6,8},{7,13},{8,0},{9,7},{... | collective-permute-start | bytes 98312 | tf_op jit(solution)/shard_map/ppermute | solution.py:355
  7.1 0.2 %cross_spectra.6.refs_8_ = bf16[2,2,16,256]{3,2,1,0:T(8,128)(2,1)S(1)} custom-call(f32[1,256]{1,0:T(1,128)S(1)} %get-tuple-element.21.weight_ref, f32[12,16,256]{2,1,0:T(8,128)S(1)} %get-tuple-element.22.refs_0_, f32[12,16,256]{2,1,0:T(8,128)S(1)} %get-tuple-element.23.refs_1_, f32[12,16,256]{2,1,0:T(8,128)S(1)} %get-tuple-element.24.refs_2_, ...), custom_call_target="tpu_custom_call" | custom-call | tf_op jit(solution)/shard_map/cross_spectra/pallas_call | solution.py:344
  7.3 0.8 %collective-permute-start.1 = (bf16[2,2,16,256]{3,2,1,0:T(8,128)(2,1)S(1)}, bf16[2,2,16,256]{3,2,1,0:T(8,128)(2,1)S(1)}, u32[]{:S(2)}, u32[]{:S(2)}) collective-permute-start(bf16[2,2,16,256]{3,2,1,0:T(8,128)(2,1)S(1)} %cross_spectra.6.refs_8_), channel_id=1, source_target_pairs={{0,2},{1,11},{2,0},{3,13},{4,8},{5,7},{6,10},{7,1},{8,14},{9,5},{1... | collective-permute-start | bytes 98312 | tf_op jit(solution)/shard_map/ppermute | solution.py:355
  8.2 0.2 %cross_spectra.7.after_ref = bf16[2,2,16,256]{3,2,1,0:T(8,128)(2,1)S(1)} custom-call(f32[1,256]{1,0:T(1,128)S(1)} %get-tuple-element.21.weight_ref, f32[12,16,256]{2,1,0:T(8,128)S(1)} %get-tuple-element.22.refs_0_, f32[12,16,256]{2,1,0:T(8,128)S(1)} %get-tuple-element.23.refs_1_, f32[12,16,256]{2,1,0:T(8,128)S(1)} %get-tuple-element.24.refs_2_, ...), custom_call_target="tpu_custom_call" | custom-call | tf_op jit(solution)/shard_map/cross_spectra/pallas_call | solution.py:344
  8.4 1.7 %collective-permute-start.4 = (bf16[2,2,16,256]{3,2,1,0:T(8,128)(2,1)S(1)}, bf16[2,2,16,256]{3,2,1,0:T(8,128)(2,1)S(1)}, u32[]{:S(2)}, u32[]{:S(2)}) collective-permute-start(bf16[2,2,16,256]{3,2,1,0:T(8,128)(2,1)S(1)} %cross_spectra.7.after_ref), channel_id=1, source_target_pairs={{0,4},{1,5},{2,6},{3,7},{4,0},{5,1},{6,2},{7,3},{8,12},{9,13},{10,... | collective-permute-start | bytes 98312 | tf_op jit(solution)/shard_map/ppermute | solution.py:355
  10.1 0.7 %split_lag_table.1.table_ref.split_ref = bf16[3,2,256,512]{3,2,1,0:T(8,128)(2,1)S(1)} custom-call(bf16[2,2,16,256]{3,2,1,0:T(8,128)(2,1)S(1)} %cross_spectra.7.after_ref), custom_call_target="tpu_custom_call" | custom-call | tf_op jit(solution)/shard_map/split_lag_table/pallas_call | solution.py:360
  10.7 0.0 collective-permute-done.3.spectra_ref
  10.8 0.2 %split_lag_sums.3.refs_0_ = f32[32,512]{1,0:T(8,128)S(1)} custom-call(bf16[3,2,256,512]{3,2,1,0:T(8,128)(2,1)S(1)} %split_lag_table.1.table_ref.split_ref, bf16[2,2,16,256]{3,2,1,0:T(8,128)(2,1)S(1)} %collective-permute-done.3.spectra_ref), custom_call_target="tpu_custom_call" | custom-call | flops 1000 | bytes 1000 | tf_op jit(solution)/shard_map/split_lag_sums/pallas_call | solution.py:370
  10.9 0.2 %split_lag_sums.4.refs_0_.before_ref = f32[32,512]{1,0:T(8,128)S(1)} custom-call(bf16[3,2,256,512]{3,2,1,0:T(8,128)(2,1)S(1)} %split_lag_table.1.table_ref.split_ref, bf16[2,2,16,256]{3,2,1,0:T(8,128)(2,1)S(1)} %collective-permute-done.2.spectra_ref, f32[32,512]{1,0:T(8,128)S(1)} %split_lag_sums.3.refs_0_), custom_call_target="tpu_custom_call" | custom-call | flops 1000 | bytes 1000 | tf_op jit(solution)/shard_map/split_lag_sums/pallas_call | solution.py:370
  11.1 0.2 %collective-permute-done.1.spectra_ref = bf16[2,2,16,256]{3,2,1,0:T(8,128)(2,1)S(1)} collective-permute-done((bf16[2,2,16,256]{3,2,1,0:T(8,128)(2,1)S(1)}, bf16[2,2,16,256]{3,2,1,0:T(8,128)(2,1)S(1)}, u32[]{:S(2)}, u32[]{:S(2)}) %collective-permute-start.1) | collective-permute-done | bytes 32800 | tf_op jit(solution)/shard_map/ppermute | solution.py:355
  11.3 0.1 %split_lag_sums.5.refs_8_ = f32[32,256]{1,0:T(8,128)S(1)} custom-call(bf16[3,2,256,512]{3,2,1,0:T(8,128)(2,1)S(1)} %split_lag_table.1.table_ref.split_ref, bf16[2,2,16,256]{3,2,1,0:T(8,128)(2,1)S(1)} %collective-permute-done.1.spectra_ref, f32[32,512]{1,0:T(8,128)S(1)} %split_lag_sums.4.refs_0_.before_ref), custom_call_target="tpu_custom_call" | custom-call | flops 1000 | bytes 1000 | tf_op jit(solution)/shard_map/split_lag_sums/pallas_call | solution.py:370
  11.5 0.9 %collective-permute-start.5 = (f32[32,256]{1,0:T(8,128)S(1)}, f32[32,256]{1,0:T(8,128)S(1)}, u32[]{:S(2)}, u32[]{:S(2)}) collective-permute-start(f32[32,256]{1,0:T(8,128)S(1)} %split_lag_sums.5.refs_8_), channel_id=1, source_target_pairs={{0,1},{1,0},{2,3},{3,2},{4,5},{5,4},{6,7},{7,6},{8,9},{9,8},{10,11... | collective-permute-start | bytes 98312 | tf_op jit(solution)/shard_map/ppermute | solution.py:377
  12.4 0.4 %whole_lag_table.1 = (bf16[2,2,16,256]{3,2,1,0:T(8,128)(2,1)S(1)}, bf16[2,2,256,256]{3,2,1,0:T(8,128)(2,1)S(1)}) custom-call(f32[1,256]{1,0:T(1,128)S(1)} %get-tuple-element.21.weight_ref, f32[12,16,256]{2,1,0:T(8,128)S(1)} %get-tuple-element.22.refs_0_, f32[12,16,256]{2,1,0:T(8,128)S(1)} %get-tuple-element.23.refs_1_, ...), custom_call_target="tpu_custom_call" | custom-call | tf_op jit(solution)/shard_map/whole_lag_table/pallas_call | solution.py:378
  12.8 0.2 %own_lag_sums.1.refs_0_ = f32[32,256]{1,0:T(8,128)S(1)} custom-call(bf16[3,2,256,512]{3,2,1,0:T(8,128)(2,1)S(1)} %split_lag_table.1.table_ref.split_ref, bf16[2,2,256,256]{3,2,1,0:T(8,128)(2,1)S(1)} %get-tuple-element.34.whole_ref.table_ref, bf16[2,2,16,256]{3,2,1,0:T(8,128)(2,1)S(1)} %collective-permute-done.1.spectra_ref, ...), custom_call_target="tpu_custom_call" | custom-call | flops 1000 | bytes 1000 | tf_op jit(solution)/shard_map/own_lag_sums/pallas_call | solution.py:385
  13.0 0.0 collective-permute-done.4.spectra_ref
  13.0 0.1 %last_lag_sums.1 = f32[32,256]{1,0:T(8,128)S(1)} custom-call(bf16[2,2,256,256]{3,2,1,0:T(8,128)(2,1)S(1)} %get-tuple-element.34.whole_ref.table_ref, bf16[2,2,16,256]{3,2,1,0:T(8,128)(2,1)S(1)} %collective-permute-done.4.spectra_ref, f32[32,256]{1,0:T(8,128)S(1)} %own_lag_sums.1.refs_0_), custom_call_target="tpu_custom_call" | custom-call | flops 1000 | bytes 1000 | tf_op jit(solution)/shard_map/last_lag_sums/pallas_call | solution.py:392
  13.2 0.1 collective-permute-done.5
  13.2 0.6 %mul.3 = f32[2,16,256]{2,1,0:T(8,128)} multiply(f32[2,16,256]{2,1,0:T(8,128)S(1)} %bitcast.3, f32[2,16,256]{2,1,0:T(8,128)S(1)} %get-tuple-element.36) | non-fusion elementwise | flops 8192 | bytes 98304 | tf_op jit(solution)/shard_map/mul | solution.py:399
  (2 shorter events, 0.0 us)
Async XLA Ops:
  0.0 1.9 %collective-permute-start = (bf16[12,16,256]{2,1,0:T(8,128)(2,1)}, bf16[12,16,256]{2,1,0:T(8,128)(2,1)S(1)}, u32[]{:S(2)}, u32[]{:S(2)}) collective-permute-start(bf16[12,16,256]{2,1,0:T(8,128)(2,1)} %bitcast.4), channel_id=1, source_target_pairs={{0,1},{1,0},{2,3},{3,2},{4,5},{5,4},{6,7},{7,6},{8,9},{9,8},{10,11... | collective-permute-start | bytes 294920 | tf_op jit(solution)/shard_map/ppermute | solution.py:318
  2.2 8.5 %collective-permute-start.3 = (bf16[2,2,16,256]{3,2,1,0:T(8,128)(2,1)S(1)}, bf16[2,2,16,256]{3,2,1,0:T(8,128)(2,1)S(1)}, u32[]{:S(2)}, u32[]{:S(2)}) collective-permute-start(bf16[2,2,16,256]{3,2,1,0:T(8,128)(2,1)S(1)} %get-tuple-element.33.refs_9_), channel_id=1, source_target_pairs={{0,6},{1,9},{2,4},{3,15},{4,12},{5,11},{6,14},{7,5},{8,10},{9,3},{... | collective-permute-start | bytes 98312 | tf_op jit(solution)/shard_map/ppermute | solution.py:355
  6.0 5.0 %collective-permute-start.2 = (bf16[2,2,16,256]{3,2,1,0:T(8,128)(2,1)S(1)}, bf16[2,2,16,256]{3,2,1,0:T(8,128)(2,1)S(1)}, u32[]{:S(2)}, u32[]{:S(2)}) collective-permute-start(bf16[2,2,16,256]{3,2,1,0:T(8,128)(2,1)S(1)} %cross_spectra.5.refs_8_), channel_id=1, source_target_pairs={{0,12},{1,15},{2,10},{3,9},{4,14},{5,3},{6,8},{7,13},{8,0},{9,7},{... | collective-permute-start | bytes 98312 | tf_op jit(solution)/shard_map/ppermute | solution.py:355
  7.3 4.0 %collective-permute-start.1 = (bf16[2,2,16,256]{3,2,1,0:T(8,128)(2,1)S(1)}, bf16[2,2,16,256]{3,2,1,0:T(8,128)(2,1)S(1)}, u32[]{:S(2)}, u32[]{:S(2)}) collective-permute-start(bf16[2,2,16,256]{3,2,1,0:T(8,128)(2,1)S(1)} %cross_spectra.6.refs_8_), channel_id=1, source_target_pairs={{0,2},{1,11},{2,0},{3,13},{4,8},{5,7},{6,10},{7,1},{8,14},{9,5},{1... | collective-permute-start | bytes 98312 | tf_op jit(solution)/shard_map/ppermute | solution.py:355
  8.4 4.6 %collective-permute-start.4 = (bf16[2,2,16,256]{3,2,1,0:T(8,128)(2,1)S(1)}, bf16[2,2,16,256]{3,2,1,0:T(8,128)(2,1)S(1)}, u32[]{:S(2)}, u32[]{:S(2)}) collective-permute-start(bf16[2,2,16,256]{3,2,1,0:T(8,128)(2,1)S(1)} %cross_spectra.7.after_ref), channel_id=1, source_target_pairs={{0,4},{1,5},{2,6},{3,7},{4,0},{5,1},{6,2},{7,3},{8,12},{9,13},{10,... | collective-permute-start | bytes 98312 | tf_op jit(solution)/shard_map/ppermute | solution.py:355
  11.5 1.7 %collective-permute-start.5 = (f32[32,256]{1,0:T(8,128)S(1)}, f32[32,256]{1,0:T(8,128)S(1)}, u32[]{:S(2)}, u32[]{:S(2)}) collective-permute-start(f32[32,256]{1,0:T(8,128)S(1)} %split_lag_sums.5.refs_8_), channel_id=1, source_target_pairs={{0,1},{1,0},{2,3},{3,2},{4,5},{5,4},{6,7},{7,6},{8,9},{9,8},{10,11... | collective-permute-start | bytes 98312 | tf_op jit(solution)/shard_map/ppermute | solution.py:377
